TPU v7x, 32 devices: a whole 2x2x4 slice. The times are simulated.
32 devices in a mesh: energy: 8 (over z, core), seg: 4 (over y, x).
Axes of the slice: x: 2, y: 2, z: 4, core: 2. Of those that a mesh axis runs over, the one named last changes fastest.
Arguments:
- energies: float32 [8], P('energy'), may hold values from -2 to 2
- h_blocks: float32 [4, 4, 64, 128], P('seg'), as said below
- couplings: float32 [4, 4, 64, 128], P('seg')
- shift_real: float32 [8, 4, 256], P('energy', 'seg'), may hold values from -0.625 to 0.625
- shift_rate: float32 [8, 4, 256], P('energy', 'seg'), may hold values from 0.005 to 0.05
- screened: float32 [8, 4, 4, 64, 128], P(None, 'seg'), may hold values from -3 to 3
- sources: int32 [8, 8], P('energy'), may hold values from 0 to 7, as said below
- counts: int32 [4], P('seg'), may hold values from 1 to 4, 8 in all
Outputs:
- sigma_new: float32 [8, 4, 4, 64, 128], P('energy', 'seg')
Inputs may be any that keep to these rules, and one draw needn't show every extreme that they name: `h_blocks`: each diagonal block is Hermitian: its real part symmetric, its imaginary part antisymmetric. The counts sum to 8; some segment holds exactly 4 blocks. For every group of 1 consecutive energies starting at a multiple of 1, its 8 sources lie at most 1 in any one such group, and exactly 1 in some group.
All inputs are finite; a program needn't handle non-finite values.
Results may differ from a plain program's by a relative error of at most 0.0029.
Values may be sent and summed in bfloat16 or wider, within the bound.
No kernel may reach another device: no remote copies, remote signals or barrier semaphores. Data moves between devices by JAX's collectives and lax.ppermute only.
A program may use at most 64 MiB of HBM per device.

v0:
```python
import jax
import jax.numpy as jnp
from jax import lax
from jax.sharding import PartitionSpec as P

broadening = 0.02


def carried_in(part, axis, combine, identity, reverse):
    count = lax.axis_size(axis)
    place = lax.axis_index(axis)
    ahead = count - 1 - place if reverse else place
    gathered = jax.tree.map(lambda a: lax.all_gather(a, axis), part)
    state = jax.tree.map(lambda a, e: jnp.zeros_like(a) + jnp.asarray(e, a.dtype), part, identity)

    def one(turn, state):
        source = count - 1 - turn if reverse else turn
        return combine(
            state, jax.tree.map(lambda a: lax.dynamic_index_in_dim(a, source, 0, False), gathered)
        )

    return lax.fori_loop(0, ahead, one, state)


def expand(matrix):
    order = matrix.shape[-2]
    real_part = matrix[..., :order]
    imag_part = matrix[..., order:]
    return jnp.concatenate(
        [jnp.concatenate([real_part, imag_part], -1), jnp.concatenate([-imag_part, real_part], -1)],
        -2,
    )


def complex_product(matrix, other):
    return jnp.matmul(matrix, expand(other), precision=lax.Precision.HIGHEST)


def adjoint(matrix):
    order = matrix.shape[-2]
    return jnp.concatenate(
        [jnp.swapaxes(matrix[..., :order], -1, -2), -jnp.swapaxes(matrix[..., order:], -1, -2)], -1
    )


def complex_inverse(matrix):
    order = matrix.shape[-2]
    real_part = matrix[..., :order]
    imag_part = matrix[..., order:]
    real_form = jnp.concatenate(
        [jnp.concatenate([real_part, -imag_part], -1), jnp.concatenate([imag_part, real_part], -1)],
        -2,
    )
    flipped = jnp.swapaxes(real_form, -1, -2)
    normal = jnp.matmul(flipped, real_form, precision=lax.Precision.HIGHEST)
    factor = jnp.linalg.cholesky(normal)
    middle = jax.scipy.linalg.solve_triangular(factor, flipped[..., :order], lower=True)
    solved = jax.scipy.linalg.solve_triangular(factor, middle, lower=True, trans=1)
    return jnp.concatenate([solved[..., :order, :], solved[..., order:, :]], -1)


def unit_block(order):
    return jnp.concatenate(
        [jnp.eye(order, dtype=jnp.float32), jnp.zeros((order, order), jnp.float32)], -1
    )


def entry_product(green, weight):
    order = green.shape[-2]
    green_re = green[..., :order]
    green_im = green[..., order:]
    weight_re = weight[..., :order]
    weight_im = weight[..., order:]
    return jnp.concatenate(
        [green_re * weight_re - green_im * weight_im, green_re * weight_im + green_im * weight_re],
        -1,
    )


def build_blocks(energies, hams, shift_real, shift_rate):
    slots, order = (hams.shape[0], hams.shape[1])
    batch = energies.shape[0]
    identity = jnp.eye(order, dtype=jnp.float32)
    shifts = shift_real.reshape(batch, slots, order)
    rates = shift_rate.reshape(batch, slots, order)
    real_part = (
        energies[:, None, None, None] * identity
        - hams[None, :, :, :order]
        - shifts[..., :, None] * identity
    )
    imag_part = broadening * identity - hams[None, :, :, order:] + rates[..., :, None] * identity
    return jnp.concatenate([real_part, imag_part], -1)


def summary_step(diag_block, link_block, state):
    head_block, upper_block, lower_block, last_block = state
    back_link = adjoint(link_block)
    fresh_block = complex_inverse(
        diag_block - complex_product(complex_product(back_link, last_block), link_block)
    )
    left_part = complex_product(upper_block, link_block)
    right_part = complex_product(back_link, lower_block)
    new_upper = complex_product(left_part, fresh_block)
    new_lower = complex_product(fresh_block, right_part)
    new_head = head_block + complex_product(new_upper, right_part)
    return (new_head, new_upper, new_lower, fresh_block)


def summary_counted(diag_a, links, used_blocks):
    last_block = complex_inverse(diag_a[:, 0])

    def advance(k, state):
        diag_block = lax.dynamic_index_in_dim(diag_a, k, 1, keepdims=False)
        link_block = lax.dynamic_index_in_dim(links, k, 0, keepdims=False)
        return summary_step(diag_block, link_block, state)

    return lax.fori_loop(1, used_blocks, advance, (last_block, last_block, last_block, last_block))


def pick_blocks(flag, first_item, second_item):
    return jnp.where(flag[..., None, None] > 0.5, first_item, second_item)


def join_segments(left_group, right_group):
    a, b, c, d, entry_a, flag_a = left_group
    p, q, r, s, link_v, flag_b = right_group
    back_v = adjoint(link_v)
    order = a.shape[-2]
    cross_term = complex_product(complex_product(back_v, d), link_v)
    resolvent = complex_inverse(unit_block(order) - complex_product(p, cross_term))
    res_first = complex_product(resolvent, p)
    res_upper = complex_product(resolvent, q)
    d_link = complex_product(d, link_v)
    back_c = complex_product(back_v, c)
    b_link = complex_product(b, link_v)
    head_block = a + complex_product(complex_product(b_link, res_first), back_c)
    upper_block = complex_product(b_link, res_upper)
    k_lower = c + complex_product(complex_product(d_link, res_first), back_c)
    lower_block = complex_product(r, complex_product(back_v, k_lower))
    last_block = s + complex_product(complex_product(r, cross_term), res_upper)
    joined = (head_block, upper_block, lower_block, last_block, entry_a)
    result = tuple(
        (
            pick_blocks(flag_a, rb, pick_blocks(flag_b, lb, jb))
            for lb, rb, jb in zip(left_group[:5], right_group[:5], joined)
        )
    )
    return result + (flag_a * flag_b,)


def join_reversed(earlier, later):
    return join_segments(later, earlier)


def greens_counted(diag_a, links, used_blocks, previous, sig_right):

    def forward(k, state):
        earlier, buffer = state
        link_block = lax.dynamic_index_in_dim(links, k, 0, keepdims=False)
        diag_block = lax.dynamic_index_in_dim(diag_a, k, 1, keepdims=False)
        inner_block = (
            diag_block
            - complex_product(complex_product(adjoint(link_block), earlier), link_block)
            - jnp.where(k == used_blocks - 1, sig_right, 0.0)
        )
        fresh_block = complex_inverse(inner_block)
        return (fresh_block, lax.dynamic_update_index_in_dim(buffer, fresh_block, k, 1))

    _, forward_blocks = lax.fori_loop(0, used_blocks, forward, (previous, jnp.zeros_like(diag_a)))

    def backward(step, greens):
        k = used_blocks - 2 - step
        link_block = lax.dynamic_index_in_dim(links, k + 1, 0, keepdims=False)
        own_block = lax.dynamic_index_in_dim(forward_blocks, k, 1, keepdims=False)
        later_block = lax.dynamic_index_in_dim(greens, k + 1, 1, keepdims=False)
        spread = complex_product(own_block, link_block)
        updated = own_block + complex_product(
            complex_product(spread, later_block), complex_product(adjoint(link_block), own_block)
        )
        return lax.dynamic_update_index_in_dim(greens, updated, k, 1)

    return lax.fori_loop(0, used_blocks - 1, backward, forward_blocks)


def body(energies, h_blocks, couplings, shift_real, shift_rate, screened, sources, counts):
    used_blocks = counts[0]
    hams = h_blocks[0]
    links = couplings[0]
    batch = energies.shape[0]
    diag_a = build_blocks(energies, hams, shift_real[:, 0], shift_rate[:, 0])
    summary = summary_counted(diag_a, links, used_blocks)
    entry_link = jnp.broadcast_to(links[0], (batch,) + links[0].shape)
    own_item = summary + (entry_link, jnp.zeros((batch,), jnp.float32))
    zero_block = jnp.zeros_like(entry_link)
    identity_item = (
        zero_block,
        zero_block,
        zero_block,
        zero_block,
        zero_block,
        jnp.ones((batch,), jnp.float32),
    )
    before = carried_in(own_item, "seg", join_segments, identity_item, False)
    after = carried_in(own_item, "seg", join_reversed, identity_item, True)
    right_link = after[4]
    sig_right = complex_product(complex_product(right_link, after[0]), adjoint(right_link))
    greens = greens_counted(diag_a, links, used_blocks, before[3], sig_right)
    packed = greens.astype(jnp.bfloat16)
    weights = screened[:, 0][:, None]
    portion = lax.all_gather(packed, "energy", axis=0, tiled=True)
    energy_index = jnp.arange(portion.shape[0], dtype=jnp.int32)
    selector = (jnp.transpose(sources)[:, :, None] == energy_index[None, None, :]).astype(
        jnp.bfloat16
    )
    picked = jnp.einsum("jtc,cmab->jtmab", selector, portion, preferred_element_type=jnp.float32)
    sigma_local = jnp.sum(entry_product(picked, weights), 0)
    return sigma_local[:, None]


def solution(mesh):
    in_specs = (
        P("energy"),
        P("seg", None, None, None),
        P("seg", None, None, None),
        P("energy", "seg", None),
        P("energy", "seg", None),
        P(None, "seg", None, None, None),
        P("energy", None),
        P("seg"),
    )
    out_specs = P("energy", "seg", None, None, None)
    return jax.shard_map(body, mesh=mesh, in_specs=in_specs, out_specs=out_specs, check_vma=False)
```

profile of v0, /device:TPU:0, one launch (start us, length us, event | category | flops | bytes accessed | tf_op | source)
XLA Modules:
  0.0 389.3 jit_solution(6915925293804573331)
XLA Ops:
  2.6 0.7 dynamic-update-slice
  3.3 11.3 %all-reduce.2 = f32[4]{0:T(128)S(1)} all-reduce(f32[4]{0:T(128)S(1)} %dynamic-update-slice), channel_id=1, replica_groups=mesh['energy'=8,'seg'=4] {'seg'}, use_global_device_ids=true, to_apply=%add.2 | all-reduce | flops 4 | bytes 32
  16.8 0.8 slice.506
  17.6 7.7 %all_gather.48 = f32[4,1,64,128]{3,2,1,0:T(8,128)S(1)} all-gather(f32[1,1,64,128]{3,2,1,0:T(8,128)S(1)} %slice.506), channel_id=1, replica_groups=mesh['energy'=8,'seg'=4] {'seg'}, dimensions={0}, use_global_device_ids=true | all-gather | bytes 163840 | tf_op jit(solution)/shard_map/all_gather | solution.py:13
  26.3 11.7 %custom-call.33 = f32[1,128,128]{2,1,0:T(8,128)S(1)} custom-call(f32[1,128,128]{2,1,0:T(8,128)S(1)} %fusion.221), custom_call_target="Cholesky" | custom-call | tf_op jit(solution)/shard_map/jit(cholesky)/cholesky/custom-call.1 | solution.py:56
  39.4 9.8 %custom-call.35 = f32[1,128,128]{1,2,0:T(8,128)S(1)} custom-call(f32[1,128,128]{2,1,0:T(8,128)S(1)} %fusion.227), custom_call_target="InvertDiagBlocksLowerTriangular" | custom-call | tf_op jit(solution)/shard_map/jit(_solve_triangular)/triangular_solve/custom-call.2 | solution.py:58
  50.0 0.8 copy-done.1
  50.8 82.9 %while.81 = (s32[]{:T(128)}, f32[1,64,128]{2,1,0:T(8,128)S(1)}, f32[1,64,128]{2,1,0:T(8,128)S(1)}, f32[1,64,128]{2,1,0:T(8,128)S(1)}, f32[1,64,128]{1,2,0:T(8,12...) while((s32[]{:T(128)}, f32[1,64,128]{2,1,0:T(8,128)S(1)}, ...), condition=%wide.region_3.7_spmd, body=%wide.region_2.6_spmd.sunk | while | flops 139034752 | bytes 2573473 | solution.py:117
  54.0 11.7 %custom-call.44 = f32[1,128,128]{2,1,0:T(8,128)S(1)} custom-call(f32[1,128,128]{2,1,0:T(8,128)S(1)} %fusion.371), custom_call_target="Cholesky" | custom-call | tf_op jit(solution)/shard_map/while/body/jit(cholesky)/cholesky/custom-call.1 | solution.py:56
  67.1 9.8 %custom-call.45 = f32[1,128,128]{1,2,0:T(8,128)S(1)} custom-call(f32[1,128,128]{2,1,0:T(8,128)S(1)} %fusion.372), custom_call_target="InvertDiagBlocksLowerTriangular" | custom-call | tf_op jit(solution)/shard_map/while/body/jit(_solve_triangular)/triangular_solve/custom-call.2 | solution.py:58
  81.3 11.7 %custom-call.44 = f32[1,128,128]{2,1,0:T(8,128)S(1)} custom-call(f32[1,128,128]{2,1,0:T(8,128)S(1)} %fusion.371), custom_call_target="Cholesky" | custom-call | tf_op jit(solution)/shard_map/while/body/jit(cholesky)/cholesky/custom-call.1 | solution.py:56
  94.3 9.8 %custom-call.45 = f32[1,128,128]{1,2,0:T(8,128)S(1)} custom-call(f32[1,128,128]{2,1,0:T(8,128)S(1)} %fusion.372), custom_call_target="InvertDiagBlocksLowerTriangular" | custom-call | tf_op jit(solution)/shard_map/while/body/jit(_solve_triangular)/triangular_solve/custom-call.2 | solution.py:58
  108.5 11.7 %custom-call.44 = f32[1,128,128]{2,1,0:T(8,128)S(1)} custom-call(f32[1,128,128]{2,1,0:T(8,128)S(1)} %fusion.371), custom_call_target="Cholesky" | custom-call | tf_op jit(solution)/shard_map/while/body/jit(cholesky)/cholesky/custom-call.1 | solution.py:56
  121.6 9.8 %custom-call.45 = f32[1,128,128]{1,2,0:T(8,128)S(1)} custom-call(f32[1,128,128]{2,1,0:T(8,128)S(1)} %fusion.372), custom_call_target="InvertDiagBlocksLowerTriangular" | custom-call | tf_op jit(solution)/shard_map/while/body/jit(_solve_triangular)/triangular_solve/custom-call.2 | solution.py:58
  133.7 7.0 %all-gather = f32[4,64,128]{2,1,0:T(8,128)S(1)} all-gather(f32[1,64,128]{2,1,0:T(8,128)S(1)} %copy.42), channel_id=2, replica_groups=mesh['energy'=8,'seg'=4] {'seg'}, dimensions={0}, use_global_device_ids=true | all-gather | bytes 163840 | tf_op jit(solution)/shard_map/all_gather | solution.py:13
  140.7 9.1 %all-gather.2 = f32[4,64,128]{2,1,0:T(8,128)S(1)} all-gather(f32[1,64,128]{2,1,0:T(8,128)S(1)} %get-tuple-element.552), channel_id=4, replica_groups=mesh['energy'=8,'seg'=4] {'seg'}, dimensions={0}, use_global_device_ids=true | all-gather | bytes 163840 | tf_op jit(solution)/shard_map/all_gather | solution.py:13
  149.8 6.9 %all-gather.3 = f32[4,64,128]{2,1,0:T(8,128)S(1)} all-gather(f32[1,64,128]{2,1,0:T(8,128)S(1)} %get-tuple-element.553), channel_id=5, replica_groups=mesh['energy'=8,'seg'=4] {'seg'}, dimensions={0}, use_global_device_ids=true | all-gather | bytes 163840 | tf_op jit(solution)/shard_map/all_gather | solution.py:13
  156.8 9.0 %all-gather.1 = f32[4,64,128]{2,1,0:T(8,128)S(1)} all-gather(f32[1,64,128]{2,1,0:T(8,128)S(1)} %get-tuple-element.551), channel_id=3, replica_groups=mesh['energy'=8,'seg'=4] {'seg'}, dimensions={0}, use_global_device_ids=true | all-gather | bytes 163840 | tf_op jit(solution)/shard_map/all_gather | solution.py:13
  165.8 88.8 %while.83 = (s32[]{:T(128)}, f32[1,64,128]{2,1,0:T(8,128)S(1)}, f32[1,64,128]{2,1,0:T(8,128)S(1)}, f32[1]{0:T(128)}, s32[]{:T(128)}, /*index=5*/f32[4,1]{0,1:T(1...) while((s32[]{:T(128)}, f32[1,64,128]{2,1,0:T(8,128)S(1)}, ...), condition=%wide.region_7.11_spmd, body=%wide.region_6.10_spmd.sunk | while | flops 151679104 | bytes 3040514 | solution.py:22
  170.3 11.7 %custom-call.48 = f32[1,128,128]{2,1,0:T(8,128)S(1)} custom-call(f32[1,128,128]{2,1,0:T(8,128)S(1)} %fusion.412), custom_call_target="Cholesky" | custom-call | tf_op jit(solution)/shard_map/while/body/jit(cholesky)/cholesky/custom-call.1 | solution.py:56
  182.0 0.7 compare_reduce_fusion.11
  183.4 9.8 %custom-call.49 = f32[1,128,128]{1,2,0:T(8,128)S(1)} custom-call(f32[1,128,128]{2,1,0:T(8,128)S(1)} %fusion.413), custom_call_target="InvertDiagBlocksLowerTriangular" | custom-call | tf_op jit(solution)/shard_map/while/body/jit(_solve_triangular)/triangular_solve/custom-call.2 | solution.py:58
  194.6 0.9 fusion.419
  199.8 11.7 %custom-call.48 = f32[1,128,128]{2,1,0:T(8,128)S(1)} custom-call(f32[1,128,128]{2,1,0:T(8,128)S(1)} %fusion.412), custom_call_target="Cholesky" | custom-call | tf_op jit(solution)/shard_map/while/body/jit(cholesky)/cholesky/custom-call.1 | solution.py:56
  211.6 0.7 compare_reduce_fusion.11
  212.9 9.8 %custom-call.49 = f32[1,128,128]{1,2,0:T(8,128)S(1)} custom-call(f32[1,128,128]{2,1,0:T(8,128)S(1)} %fusion.413), custom_call_target="InvertDiagBlocksLowerTriangular" | custom-call | tf_op jit(solution)/shard_map/while/body/jit(_solve_triangular)/triangular_solve/custom-call.2 | solution.py:58
  224.1 0.9 fusion.419
  229.3 11.7 %custom-call.48 = f32[1,128,128]{2,1,0:T(8,128)S(1)} custom-call(f32[1,128,128]{2,1,0:T(8,128)S(1)} %fusion.412), custom_call_target="Cholesky" | custom-call | tf_op jit(solution)/shard_map/while/body/jit(cholesky)/cholesky/custom-call.1 | solution.py:56
  241.1 0.7 compare_reduce_fusion.11
  242.4 9.8 %custom-call.49 = f32[1,128,128]{1,2,0:T(8,128)S(1)} custom-call(f32[1,128,128]{2,1,0:T(8,128)S(1)} %fusion.413), custom_call_target="InvertDiagBlocksLowerTriangular" | custom-call | tf_op jit(solution)/shard_map/while/body/jit(_solve_triangular)/triangular_solve/custom-call.2 | solution.py:58
  253.6 0.9 fusion.419
  255.7 109.8 %while.84 = (s32[]{:T(128)}, f32[1,64,128]{1,2,0:T(8,128)S(1)}, f32[1,4,64,128]{3,2,1,0:T(8,128)S(1)}, s32[]{:T(128)}, f32[1,4,64,128]{3,2,1,0:T(8,128)S(1)}, /*...) while((s32[]{:T(128)}, f32[1,64,128]{1,2,0:T(8,128)S(1)}, ...), condition=%wide.region_9.13_spmd, body=%wide.region_8.12_spmd.sunk | while | flops 75935872 | bytes 1983663 | solution.py:169
  264.1 11.7 %custom-call.50 = f32[1,128,128]{2,1,0:T(8,128)S(1)} custom-call(f32[1,128,128]{2,1,0:T(8,128)S(1)} %fusion.431), custom_call_target="Cholesky" | custom-call | tf_op jit(solution)/shard_map/while/body/jit(cholesky)/cholesky/custom-call.1 | solution.py:56
  275.8 0.7 compare_reduce_fusion.12
  277.2 9.8 %custom-call.51 = f32[1,128,128]{1,2,0:T(8,128)S(1)} custom-call(f32[1,128,128]{2,1,0:T(8,128)S(1)} %fusion.432), custom_call_target="InvertDiagBlocksLowerTriangular" | custom-call | tf_op jit(solution)/shard_map/while/body/jit(_solve_triangular)/triangular_solve/custom-call.2 | solution.py:58
  289.8 11.7 %custom-call.50 = f32[1,128,128]{2,1,0:T(8,128)S(1)} custom-call(f32[1,128,128]{2,1,0:T(8,128)S(1)} %fusion.431), custom_call_target="Cholesky" | custom-call | tf_op jit(solution)/shard_map/while/body/jit(cholesky)/cholesky/custom-call.1 | solution.py:56
  301.5 0.7 compare_reduce_fusion.12
  302.9 9.8 %custom-call.51 = f32[1,128,128]{1,2,0:T(8,128)S(1)} custom-call(f32[1,128,128]{2,1,0:T(8,128)S(1)} %fusion.432), custom_call_target="InvertDiagBlocksLowerTriangular" | custom-call | tf_op jit(solution)/shard_map/while/body/jit(_solve_triangular)/triangular_solve/custom-call.2 | solution.py:58
  315.5 11.7 %custom-call.50 = f32[1,128,128]{2,1,0:T(8,128)S(1)} custom-call(f32[1,128,128]{2,1,0:T(8,128)S(1)} %fusion.431), custom_call_target="Cholesky" | custom-call | tf_op jit(solution)/shard_map/while/body/jit(cholesky)/cholesky/custom-call.1 | solution.py:56
  327.2 0.7 compare_reduce_fusion.12
  328.6 9.8 %custom-call.51 = f32[1,128,128]{1,2,0:T(8,128)S(1)} custom-call(f32[1,128,128]{2,1,0:T(8,128)S(1)} %fusion.432), custom_call_target="InvertDiagBlocksLowerTriangular" | custom-call | tf_op jit(solution)/shard_map/while/body/jit(_solve_triangular)/triangular_solve/custom-call.2 | solution.py:58
  341.2 11.7 %custom-call.50 = f32[1,128,128]{2,1,0:T(8,128)S(1)} custom-call(f32[1,128,128]{2,1,0:T(8,128)S(1)} %fusion.431), custom_call_target="Cholesky" | custom-call | tf_op jit(solution)/shard_map/while/body/jit(cholesky)/cholesky/custom-call.1 | solution.py:56
  352.9 0.7 compare_reduce_fusion.12
  354.3 9.8 %custom-call.51 = f32[1,128,128]{1,2,0:T(8,128)S(1)} custom-call(f32[1,128,128]{2,1,0:T(8,128)S(1)} %fusion.432), custom_call_target="InvertDiagBlocksLowerTriangular" | custom-call | tf_op jit(solution)/shard_map/while/body/jit(_solve_triangular)/triangular_solve/custom-call.2 | solution.py:58
  365.5 4.4 %while.85 = (s32[]{:T(128)}, f32[1,4,64,128]{3,2,1,0:T(8,128)S(1)}, s32[]{:T(128)}, s32[]{:T(128)}, f32[1,4,64,128]{3,2,1,0:T(8,128)S(1)}, /*index=5*/f32[4,64,1...) while((s32[]{:T(128)}, f32[1,4,64,128]{3,2,1,0:T(8,128)S(1)}, s32[]{:T(128)}, s32[]{:T(128)}, ...), condition=%wide.region_11.15_spmd, body=%wide.region_10.14_spmd.sunk | while | flops 50495496 | bytes 1114333 | solution.py:182
  370.0 15.6 %all_gather.53 = bf16[8,4,64,128]{3,2,1,0:T(8,128)(2,1)S(1)} all-gather(bf16[1,4,64,128]{3,2,1,0:T(8,128)(2,1)S(1)} %convert_element_type.24), channel_id=1, replica_groups=mesh['energy'=8,'seg'=4] {'energy'}, dimensions={0}, use_global_device_ids=true | all-gather | bytes 589824 | tf_op jit(solution)/shard_map/all_gather | solution.py:210
  386.3 1.6 multiply_subtract_fusion
  387.9 1.1 maximum_reduce_fusion
  (315 shorter events, 55.1 us)
Async XLA Ops:
  1.3 0.7 copy-start.6
  14.7 0.7 copy-start.3
  15.3 0.7 copy-start.4
  17.6 7.7 %copy-start.2 = (f32[1,4,64,128]{3,2,1,0:T(8,128)S(1)}, f32[1,4,64,128]{3,2,1,0:T(8,128)}, u32[]{:S(2)}) copy-start(f32[1,4,64,128]{3,2,1,0:T(8,128)} %param.24) | copy-start | bytes 393220
  49.8 0.9 copy-start.1
  365.5 20.0 %copy-start.5 = (s32[1,8]{1,0:T(1,128)S(1)}, s32[1,8]{1,0:T(1,128)}, u32[]{:S(2)}) copy-start(s32[1,8]{1,0:T(1,128)} %param.29) | copy-start | bytes 100
  369.9 16.0 %copy-start = (f32[8,1,4,64,128]{4,3,2,1,0:T(8,128)S(1)}, f32[8,1,4,64,128]{4,3,2,1,0:T(8,128)}, u32[]{:S(2)}) copy-start(f32[8,1,4,64,128]{4,3,2,1,0:T(8,128)} %param.28) | copy-start | bytes 3145732
where the time goes:
time: 396 us; the launch traced here: 389 us
  other arithmetic  266 us (67%)
  blocking collectives  66.5 us (17%)
  matrix products  31.1 us (8%)
  loops' own time  16.8 us (4%)
  local copies, waits for them, and re-layouts  7.22 us (2%)
    another operation x33, other arithmetic, complex_inverse(): factor = jnp.linalg.cholesky(normal)  137 us
    another operation x22, other arithmetic, complex_inverse(): jax.scipy.linalg.solve_triangular(factor, middle, lower=True, trans=1)  115 us
    all_gather x5, blocking collectives, carried_in(): gathered = jax.tree.map(lambda a: lax.all_gather(a, axis), part)  39.7 us
    dot_general x67, matrix products, complex_product(): return jnp.matmul(matrix, expand(other), precision=lax.Precision.HIGHEST)  20.6 us
    all_gather x1, blocking collectives, body(): portion = lax.all_gather(packed, 'energy', axis=0, tiled=True)  15.6 us
    unnamed x1, blocking collectives  11.3 us
    another operation x1, loops' own time, greens_counted(): lax.fori_loop(0, used_blocks, forward, (previous, jnp.zeros_like(diag_a)))  10.2 us

commit v1 on v0

v1 whole, which is shorter than its diff:
```python
import jax
import jax.numpy as jnp
from jax import lax
from jax.experimental import pallas as pl
from jax.experimental.pallas import tpu as pltpu
from jax.sharding import PartitionSpec as P

broadening = 0.02
cores = 2
f32 = jnp.float32
bf16 = jnp.bfloat16
VMEM = pl.BlockSpec(memory_space=pltpu.VMEM)
SMEM = pl.BlockSpec(memory_space=pltpu.SMEM)


def column(slab, k, lane):
    return jnp.take_along_axis(slab, jnp.where(lane < 64, k, 64 + k), axis=1)


def row(slab, k):
    return jnp.broadcast_to(slab[k : k + 1, :], (8, 128))


def added(parts):
    while len(parts) > 1:
        parts = [a + b for a, b in zip(parts[::2], parts[1::2])]
    return parts[0]


def invert_small(xr, xi, sub):
    for k in range(8):
        pr, pi = row(xr[k], k), row(xi[k], k)
        q = 1.0 / (pr * pr + pi * pi)
        ipr, ipi = pr * q, -(pi * q)
        at = sub == k
        cr, ci = xr[k], xi[k]
        for j in [(k + 1 + d) % 8 for d in range(7)]:
            ar, ai = row(xr[j], k), row(xi[j], k)
            tr = ar * ipr - ai * ipi
            ti = ar * ipi + ai * ipr
            xr[j] = jnp.where(at, tr, xr[j] - (cr * tr - ci * ti))
            xi[j] = jnp.where(at, ti, xi[j] - (cr * ti + ci * tr))
        xr[k] = jnp.where(at, ipr, ci * ipi - cr * ipr)
        xi[k] = jnp.where(at, ipi, -(cr * ipi + ci * ipr))
    return xr, xi


def pair_inverse(mr, mi):
    lane = lax.broadcasted_iota(jnp.int32, (8, 128), 1)
    sub = lax.broadcasted_iota(jnp.int32, (8, 128), 0)
    col = lane & 63
    mr, mi = list(mr), list(mi)
    for t in range(8):
        xr = [column(mr[t], 8 * t + j, lane) for j in range(8)]
        xi = [column(mi[t], 8 * t + j, lane) for j in range(8)]
        xr, xi = invert_small(xr, xi, sub)
        inside = (col >= 8 * t) & (col < 8 * t + 8)
        rr = jnp.where(inside, jnp.where(col == sub + 8 * t, 1.0, 0.0), mr[t])
        ri = jnp.where(inside, 0.0, mi[t])
        sr, si = [], []
        for j in range(8):
            br, bi = row(rr, j), row(ri, j)
            sr.append(xr[j] * br - xi[j] * bi)
            si.append(xr[j] * bi + xi[j] * br)
        pr, pi = added(sr), added(si)
        rows = [(row(pr, j), row(pi, j)) for j in range(8)]
        for s in [(t + d) % 8 for d in range(1, 8)]:
            ar, ai = [], []
            for j in range(8):
                cr, ci = column(mr[s], 8 * t + j, lane), column(mi[s], 8 * t + j, lane)
                ar.append(cr * rows[j][0] - ci * rows[j][1])
                ai.append(cr * rows[j][1] + ci * rows[j][0])
            mr[s] = jnp.where(inside, 0.0, mr[s]) - added(ar)
            mi[s] = jnp.where(inside, 0.0, mi[s]) - added(ai)
        mr[t], mi[t] = pr, pi
    return mr, mi


def slabs(x):
    return [x[8 * s : 8 * s + 8] for s in range(8)]


def invert_pair(zr, zi):
    mr, mi = pair_inverse(slabs(zr), slabs(zi))
    return jnp.concatenate(mr, 0), jnp.concatenate(mi, 0)


def low_lanes(x):
    return lax.broadcasted_iota(jnp.int32, x.shape, 1) < 64


def split(x):
    high = x.astype(bf16)
    return high, (x - high.astype(f32)).astype(bf16)


def diagonal(x):
    keep = low_lanes(x)
    zero = jnp.zeros_like(x)
    return jnp.concatenate([jnp.where(keep, x, zero), jnp.where(keep, zero, x)], 0)


def dot(a, b):
    return jnp.dot(a, b, preferred_element_type=f32)


def left_factor(qr, qi):
    rh, rl = split(qr)
    ih, il = split(qi)

    def whole(r, i):
        return jnp.concatenate(
            [jnp.concatenate([r, -i], 1), jnp.concatenate([i, r], 1)], 0
        )

    return jnp.concatenate([whole(rh, ih), whole(rl, il)], 0)


def right_factor(yr, yi):
    def whole(r, i):
        dr, di = diagonal(r), diagonal(i)
        return jnp.concatenate(
            [jnp.concatenate([dr, di], 1), jnp.concatenate([-di, dr], 1)], 0
        )

    rh, rl = split(yr)
    ih, il = split(yi)
    return whole(rh, ih), whole(rl, il)


def times_right(xr, xi, high, low):
    xh, xl = split(jnp.concatenate([xr, xi], 1))
    both = dot(jnp.concatenate([xh, xl], 0), high)
    out = both[:64] + (both[64:] + dot(xh, low))
    return out[:, :128], out[:, 128:]


def times_left(left, xr, xi):
    rh, rl = split(xr)
    ih, il = split(xi)
    right = jnp.concatenate(
        [
            jnp.concatenate([diagonal(rh), diagonal(rl)], 1),
            jnp.concatenate([diagonal(ih), diagonal(il)], 1),
        ],
        0,
    )
    out = dot(left, right)
    out = out[:128, :128] + (out[:128, 128:] + out[128:, :128])
    return out[:64], out[64:]


def swapped(x):
    return pltpu.roll(x, 64, 1)


def pack_kernel(core_ref, counts_ref, hams_ref, links_ref, shifts_ref, rates_ref, out_ref):
    first = 2 * core_ref[0]
    out_ref[0:64] = links_ref[first]
    out_ref[64:128] = links_ref[first + 1]
    one, two = hams_ref[first], hams_ref[first + 1]
    lower = lax.broadcasted_iota(jnp.int32, (64, 128), 0) >= (
        lax.broadcasted_iota(jnp.int32, (64, 128), 1) & 63
    )
    keep = low_lanes(one)
    left = jnp.where(lower, one, swapped(one))
    right = jnp.where(lower, swapped(two), two)
    out_ref[128:192] = jnp.where(keep, left, right)
    out_ref[192:194] = shifts_ref[...]
    out_ref[194:196] = rates_ref[...]
    out_ref[196:200] = jnp.full((4, 128), counts_ref[0].astype(f32))


def pack(core, counts, hams, links, shifts, rates):
    return pl.pallas_call(
        pack_kernel,
        out_shape=jax.ShapeDtypeStruct((200, 128), f32),
        in_specs=[SMEM, SMEM, VMEM, VMEM, VMEM, VMEM],
        out_specs=VMEM,
        name="pack",
    )(core, counts, hams, links, shifts, rates)


def wire_kernel(segs, place_ref, energy_ref, *refs):
    own = refs[:segs]
    other = refs[segs : 2 * segs]
    out_ref = refs[2 * segs]
    (u_ref, h_ref, m_ref, at_ref, ar_ref, ai_ref, yright_ref, yleft_ref, g_ref, s_ref, k_ref, t_ref) = (
        refs[2 * segs + 1 :]
    )
    blocks = 2 * segs
    half = segs
    place, core = place_ref[0], place_ref[1]
    energy = energy_ref[0]

    for k in range(segs):
        seg = jnp.bitwise_xor(place, k)
        for c, ref in ((core, own[k]), (1 - core, other[k])):
            u_ref[4 * seg + 2 * c] = ref[0:64]
            u_ref[4 * seg + 2 * c + 1] = ref[64:128]
            h_ref[2 * seg + c] = ref[128:192]
        m_ref[seg] = own[k][192:200]

    start = jnp.int32(0)
    first, used = jnp.int32(0), jnp.int32(0)
    for seg in range(segs):
        count = jnp.max(m_ref[seg, 4:5, :]).astype(jnp.int32)
        for k in range(4):
            at_ref[start + k] = 4 * seg + k
        first = jnp.where(seg == place, start, first)
        used = jnp.where(seg == place, count, used)
        start = start + count

    keep = low_lanes(jnp.zeros((64, 128), f32))
    rows = lax.broadcasted_iota(jnp.int32, (64, 128), 0)
    cols = lax.broadcasted_iota(jnp.int32, (64, 128), 1) & 63

    def prepare_block(i, carry):
        one, two = at_ref[i], at_ref[blocks - 1 - i]
        odd_one, odd_two = one & 1, two & 1
        raw_one, raw_two = h_ref[one >> 1], h_ref[two >> 1]
        one_low = pltpu.roll(raw_one, 64 * odd_one, 1)
        two_low = pltpu.roll(raw_two, 64 * odd_two, 1)
        two_high = pltpu.roll(raw_two, 64 * (1 - odd_two), 1)
        packed = jnp.where(keep, one_low, two_high)
        flipped = jnp.concatenate([one_low, two_low], 0).T[:64]
        real = jnp.where(rows >= cols, packed, flipped)
        imag = jnp.where(rows < cols, packed, jnp.where(rows > cols, -flipped, 0.0))
        extra = []
        for base in (0, 2):
            line_one = m_ref[one >> 2, pl.ds(base + ((one >> 1) & 1), 1), :]
            line_two = m_ref[two >> 2, pl.ds(base + ((two >> 1) & 1), 1), :]
            line_one = pltpu.roll(jnp.broadcast_to(line_one, (8, 128)), 64 * odd_one, 1)
            line_two = pltpu.roll(jnp.broadcast_to(line_two, (8, 128)), 64 * (1 - odd_two), 1)
            line = jnp.where(keep[:8], line_one, line_two)
            extra.append(jnp.broadcast_to(line[:1], (64, 128)))
        on = rows == cols
        ar_ref[i] = jnp.where(on, energy - extra[0], 0.0) - real
        ai_ref[i] = jnp.where(on, broadening + extra[1], 0.0) - imag
        return carry

    def prepare_link(i, carry):
        one, two = u_ref[at_ref[i]], u_ref[at_ref[blocks - i]]
        flat_re = jnp.where(keep, one, swapped(two))
        flat_im = jnp.where(keep, swapped(one), two)
        turned = jnp.concatenate([one, two], 0).T
        turned_re, turned_im = turned[:64], -turned[64:]
        high, low = right_factor(
            jnp.where(keep, flat_re, turned_re), jnp.where(keep, flat_im, turned_im)
        )
        yright_ref[i - 1, 0] = high
        yright_ref[i - 1, 1] = low
        yleft_ref[i - 1] = left_factor(
            jnp.where(keep, turned_re, flat_re), jnp.where(keep, turned_im, flat_im)
        )
        return carry

    lax.fori_loop(0, half, prepare_block, 0)
    lax.fori_loop(1, half + 1, prepare_link, 0)

    s_ref[...] = jnp.zeros_like(s_ref)

    def inward(i, carry):
        fr = ar_ref[i] - s_ref[0]
        fi = ai_ref[i] - s_ref[1]
        gr, gi = invert_pair(fr, fi)
        g_ref[i, 0] = gr
        g_ref[i, 1] = gi

        @pl.when(i < half)
        def _():
            tr, ti = times_right(gr, gi, yright_ref[i, 0], yright_ref[i, 1])
            t_ref[i] = left_factor(tr, ti)
            sr, si = times_left(yleft_ref[i], tr, ti)
            kr, ki = times_left(yleft_ref[i], gr, gi)
            high, low = right_factor(kr, ki)
            k_ref[i, 0] = high
            k_ref[i, 1] = low
            s_ref[0] = sr
            s_ref[1] = si

        @pl.when(i == half - 1)
        def _():
            s_ref[0] = swapped(s_ref[0])
            s_ref[1] = swapped(s_ref[1])
            ar_ref[half] = fr
            ai_ref[half] = fi

        return carry

    lax.fori_loop(0, half + 1, inward, 0)

    g_ref[half - 1] = g_ref[half]

    def outward(step, carry):
        i = half - 2 - step
        zr, zi = times_right(g_ref[i + 1, 0], g_ref[i + 1, 1], k_ref[i, 0], k_ref[i, 1])
        wr, wi = times_left(t_ref[i], zr, zi)
        g_ref[i, 0] = g_ref[i, 0] + wr
        g_ref[i, 1] = g_ref[i, 1] + wi
        return carry

    lax.fori_loop(0, half - 1, outward, 0)

    for k in range(4):
        block = jnp.minimum(first + k, blocks - 1)
        right = (block >= half).astype(jnp.int32)
        i = jnp.where(block >= half, blocks - 1 - block, block)
        re = pltpu.roll(g_ref[i, 0], 64 * right, 1)
        im = pltpu.roll(g_ref[i, 1], 64 * (1 - right), 1)
        live = (k < used).astype(f32)
        out_ref[k] = (jnp.where(keep, re, im) * live).astype(bf16)


def wire(place, energy, own, other):
    segs = len(own)
    half = segs

    def kernel(*refs):
        wire_kernel(segs, *refs)

    return pl.pallas_call(
        kernel,
        out_shape=jax.ShapeDtypeStruct((4, 64, 128), bf16),
        in_specs=[SMEM, SMEM] + [VMEM] * (2 * segs),
        out_specs=VMEM,
        scratch_shapes=[
            pltpu.VMEM((4 * segs, 64, 128), f32),
            pltpu.VMEM((2 * segs, 64, 128), f32),
            pltpu.VMEM((segs, 8, 128), f32),
            pltpu.SMEM((2 * segs + 4,), jnp.int32),
            pltpu.VMEM((half + 1, 64, 128), f32),
            pltpu.VMEM((half + 1, 64, 128), f32),
            pltpu.VMEM((half, 2, 256, 256), bf16),
            pltpu.VMEM((half, 256, 256), bf16),
            pltpu.VMEM((half + 1, 2, 64, 128), f32),
            pltpu.VMEM((2, 64, 128), f32),
            pltpu.VMEM((half, 2, 256, 256), bf16),
            pltpu.VMEM((half, 256, 256), bf16),
        ],
        compiler_params=pltpu.CompilerParams(vmem_limit_bytes=48 * 2**20),
        name="wire",
    )(place, energy, *own, *other)


def sum_kernel(chips, place_ref, sources_ref, *refs):
    own = refs[:chips]
    other = refs[chips : 2 * chips]
    screened_ref, out_ref, all_ref = refs[2 * chips :]
    chip, core = place_ref[0], place_ref[1]
    for k in range(chips):
        place = jnp.bitwise_xor(chip, k) * cores
        all_ref[place + core] = own[k][...]
        all_ref[place + 1 - core] = other[k][...]
    shifts = screened_ref.shape[0]
    keep = low_lanes(jnp.zeros((64, 128), f32))
    for slot in range(4):
        direct = jnp.zeros((64, 128), f32)
        crossed = jnp.zeros((64, 128), f32)
        for j in range(shifts):
            green = all_ref[sources_ref[0, j], slot].astype(f32)
            weight = screened_ref[j, slot]
            direct = direct + green * weight
            crossed = crossed + green * swapped(weight)
        out_ref[slot] = jnp.where(keep, direct - swapped(direct), crossed + swapped(crossed))


def sum_shifts(place, sources, own, other, screened):
    chips = len(own)

    def kernel(*refs):
        sum_kernel(chips, *refs)

    return pl.pallas_call(
        kernel,
        out_shape=jax.ShapeDtypeStruct(screened.shape[1:], f32),
        in_specs=[SMEM, SMEM] + [VMEM] * (2 * chips + 1),
        out_specs=VMEM,
        scratch_shapes=[pltpu.VMEM((cores * chips,) + screened.shape[1:], bf16)],
        compiler_params=pltpu.CompilerParams(vmem_limit_bytes=48 * 2**20),
        name="sum_shifts",
    )(place, sources, *own, *other, screened)


def flipped_to(x, axis, mask):
    count = lax.axis_size(axis)
    return lax.ppermute(x, axis, [(i, i ^ mask) for i in range(count)])


def body(energies, h_blocks, couplings, shift_real, shift_rate, screened, sources, counts):
    segs = lax.axis_size("seg")
    chips = lax.axis_size("energy") // cores
    seg = lax.axis_index("seg")
    energy = lax.axis_index("energy")
    core, chip = energy % cores, energy // cores
    piece = pack(
        core[None],
        counts,
        h_blocks[0],
        couplings[0],
        shift_real.reshape(2, 128),
        shift_rate.reshape(2, 128),
    )
    own = [piece] + [flipped_to(piece, "seg", k) for k in range(1, segs)]
    other = [flipped_to(x, "energy", 1) for x in own]
    greens = wire(jnp.stack([seg, core]), energies, own, other)
    near = [greens] + [flipped_to(greens, "energy", cores * k) for k in range(1, chips)]
    far = [flipped_to(x, "energy", 1) for x in near]
    out = sum_shifts(jnp.stack([chip, core]), sources, near, far, screened[:, 0])
    return out[None, None]


def solution(mesh):
    in_specs = (
        P("energy"),
        P("seg", None, None, None),
        P("seg", None, None, None),
        P("energy", "seg", None),
        P("energy", "seg", None),
        P(None, "seg", None, None, None),
        P("energy", None),
        P("seg"),
    )
    out_specs = P("energy", "seg", None, None, None)
    return jax.shard_map(body, mesh=mesh, in_specs=in_specs, out_specs=out_specs, check_vma=False)
```

time: 396 us -> 46.1 us (0.12); the launches traced: 389 us -> 45.9 us
  other arithmetic: 266 us -> 0.15 us
  blocking collectives: 66.5 us -> 0 us
  matrix products: 31.1 us -> 0 us
  Pallas kernels: 0 us -> 22.3 us
  loops' own time: 16.8 us -> 0 us
  waiting for transfers between devices: 0 us -> 11.5 us
  starting transfers between devices: 0 us -> 9.66 us
  local copies, waits for them, and re-layouts: 7.22 us -> 0.9 us
    another operation x55 -> x2, other arithmetic: 252 us -> 0.15 us  [the longest x1 0.07 us: body(): greens = wire(jnp.stack([seg, core]), energies, own, other)]
    all_gather x6 -> x0, blocking collectives: 55.2 us -> none  [the longest x5 39.7 us: carried_in(): gathered = jax.tree.map(lambda a: lax.all_gather(a, axis), part)]
    dot_general x79 -> x0, matrix products: 25 us -> none  [the longest x67 20.6 us: complex_product(): return jnp.matmul(matrix, expand(other), precision=lax.Precision.HIGHEST)]
    pallas_call x0 -> x3, Pallas kernels: none -> 22.3 us  [the longest x1 18.7 us: wire(): pl.pallas_call(kernel, out_shape=jax.ShapeDtypeStruct((4, 64, 128), bf16)...]
    another operation x5 -> x0, loops' own time: 16.8 us -> none  [the longest x1 10.2 us: greens_counted(): lax.fori_loop(0, used_blocks, forward, (previous, jnp.zeros_like(diag_a)))]
    ppermute x0 -> x14, waiting for transfers between devices: none -> 11.5 us  [flipped_to(): return lax.ppermute(x, axis, [(i, i ^ mask) for i in range(count)])]
    unnamed x1 -> x0, blocking collectives: 11.3 us -> none
    ppermute x0 -> x14, starting transfers between devices: none -> 9.66 us  [flipped_to(): return lax.ppermute(x, axis, [(i, i ^ mask) for i in range(count)])]
  transfers between devices with their start and end apart: 0 -> 14, of which waited for: 0 -> 9; matrix products, arithmetic and copies ran while one was open for 0% -> 0% of each run, Pallas kernels for 0% -> 0%
where the time goes in v1:
time: 46.1 us; the launch traced here: 45.9 us
  Pallas kernels  22.3 us (48%)
  waiting for transfers between devices  11.5 us (25%)
  starting transfers between devices  9.66 us (21%)
  between operations  1.43 us (3%)
  local copies, waits for them, and re-layouts  0.9 us (2%)
    pallas_call x1, Pallas kernels, wire(): pl.pallas_call(kernel, out_shape=jax.ShapeDtypeStruct((4, 64, 128), bf16)...  18.7 us
    ppermute x14, waiting for transfers between devices, flipped_to(): return lax.ppermute(x, axis, [(i, i ^ mask) for i in range(count)])  11.5 us
    ppermute x14, starting transfers between devices, flipped_to(): return lax.ppermute(x, axis, [(i, i ^ mask) for i in range(count)])  9.66 us
    pallas_call x1, Pallas kernels, sum_shifts(): pl.pallas_call(kernel, out_shape=jax.ShapeDtypeStruct(screened.shape[1:],...  1.85 us
    pallas_call x1, Pallas kernels, pack(): pl.pallas_call(pack_kernel, out_shape=jax.ShapeDtypeStruct((200, 128), f3...  1.7 us
  transfers between devices with their start and end apart: 14, of which 9 were waited for; matrix products, arithmetic and copies ran while one was open for 0% of the time, Pallas kernels for 0%

profile of v1, /device:TPU:0, one launch (start us, length us, event | category | flops | bytes accessed | tf_op | source)
XLA Modules:
  0.0 45.9 jit_solution(15773049322687171880)
XLA Ops:
  0.0 0.0 copy-start
  0.7 1.7 %pack.1.refs_2_ = f32[200,128]{1,0:T(8,128)} custom-call(s32[1]{0:T(128)} %bitcast.1.core_ref, s32[1]{0:T(128)S(6)} %copy.10.counts_ref, f32[4,64,128]{2,1,0:T(8,128)} %bitcast.10, f32[4,64,128]{2,1,0:T(8,128)} %bitcast.11, f32[2,128]{1,0:T(2,128)} %bitcast.12, f32[2,128]{1,0:T(2,128)} %bitcast.13), custom_call_target="tpu_custom_call" | custom-call | tf_op jit(solution)/shard_map/pack/pallas_call | solution.py:175
  2.5 3.9 %collective-permute-start.2 = (f32[200,128]{1,0:T(8,128)}, f32[200,128]{1,0:T(8,128)S(1)}, u32[]{:S(2)}, u32[]{:S(2)}) collective-permute-start(f32[200,128]{1,0:T(8,128)} %pack.1.refs_2_), channel_id=1, source_target_pairs={{0,3},{1,2},{2,1},{3,0},{4,7},{5,6},{6,5},{7,4},{8,11},{9,10},{10,... | collective-permute-start | bytes 307208 | tf_op jit(solution)/shard_map/ppermute | solution.py:387
  6.3 0.5 %collective-permute-start.1 = (f32[200,128]{1,0:T(8,128)}, f32[200,128]{1,0:T(8,128)S(1)}, u32[]{:S(2)}, u32[]{:S(2)}) collective-permute-start(f32[200,128]{1,0:T(8,128)} %pack.1.refs_2_), channel_id=1, source_target_pairs={{0,2},{1,3},{2,0},{3,1},{4,6},{5,7},{6,4},{7,5},{8,10},{9,11},{10,... | collective-permute-start | bytes 307208 | tf_op jit(solution)/shard_map/ppermute | solution.py:387
  6.9 0.1 collective-permute-start
  6.9 0.0 collective-permute-start.3
  7.6 2.4 %collective-permute-done.2.refs_5_ = f32[200,128]{1,0:T(8,128)S(1)} collective-permute-done((f32[200,128]{1,0:T(8,128)}, f32[200,128]{1,0:T(8,128)S(1)}, u32[]{:S(2)}, u32[]{:S(2)}) %collective-permute-start.2) | collective-permute-done | bytes 102432 | tf_op jit(solution)/shard_map/ppermute | solution.py:387
  9.9 0.0 collective-permute-start.6
  9.9 1.7 %collective-permute-done.1.refs_4_ = f32[200,128]{1,0:T(8,128)S(1)} collective-permute-done((f32[200,128]{1,0:T(8,128)}, f32[200,128]{1,0:T(8,128)S(1)}, u32[]{:S(2)}, u32[]{:S(2)}) %collective-permute-start.1) | collective-permute-done | bytes 102432 | tf_op jit(solution)/shard_map/ppermute | solution.py:387
  11.6 0.0 collective-permute-start.5
  11.6 0.3 collective-permute-done.refs_3_
  11.9 0.2 collective-permute-start.4
  12.1 0.1 pad_add_fusion.1.refs_0_
  12.2 0.0 collective-permute-done.3.refs_6_
  12.2 0.0 collective-permute-done.6.refs_9_
  12.2 0.7 %collective-permute-done.5.refs_8_ = f32[200,128]{1,0:T(8,128)S(1)} collective-permute-done((f32[200,128]{1,0:T(8,128)S(1)}, f32[200,128]{1,0:T(8,128)S(1)}, u32[]{:S(2)}, u32[]{:S(2)}) %collective-permute-start.5) | collective-permute-done | bytes 102432 | tf_op jit(solution)/shard_map/ppermute | solution.py:387
  12.9 0.3 collective-permute-done.4.refs_7_
  13.2 0.0 copy-start.1
  13.2 0.9 %copy-done.1 = f32[200,128]{1,0:T(8,128)S(1)} copy-done((f32[200,128]{1,0:T(8,128)S(1)}, f32[200,128]{1,0:T(8,128)}, u32[]{:S(2)}) %copy-start.1) | copy-done | bytes 102424
  14.1 18.7 %wire.1.refs_2_ = bf16[4,64,128]{2,1,0:T(8,128)(2,1)S(1)} custom-call(s32[2]{0:T(128)S(1)} %pad_add_fusion.1.refs_0_, f32[1]{0:T(128)S(6)} %copy.9.refs_1_, f32[200,128]{1,0:T(8,128)S(1)} %copy-done.1, f32[200,128]{1,0:T(8,128)S(1)} %collective-permute-done.refs_3_, f32[200,128]{1,0:T(8,128)S(1)} %collective-permute-done.1.refs_4_, ...), custom_call_target="tpu_custom_call" | custom-call | tf_op jit(solution)/shard_map/wire/pallas_call | solution.py:322
  32.9 3.8 %collective-permute-start.9 = (bf16[4,64,128]{2,1,0:T(8,128)(2,1)S(1)}, bf16[4,64,128]{2,1,0:T(8,128)(2,1)S(1)}, u32[]{:S(2)}, u32[]{:S(2)}) collective-permute-start(bf16[4,64,128]{2,1,0:T(8,128)(2,1)S(1)} %wire.1.refs_2_), channel_id=1, source_target_pairs={{0,24},{4,28},{8,16},{12,20},{16,8},{20,12},{24,0},{28,4},{1,25},{... | collective-permute-start | bytes 196616 | tf_op jit(solution)/shard_map/ppermute | solution.py:387
  36.7 0.0 collective-permute-start.8
  36.7 0.7 %collective-permute-start.7 = (bf16[4,64,128]{2,1,0:T(8,128)(2,1)S(1)}, bf16[4,64,128]{2,1,0:T(8,128)(2,1)S(1)}, u32[]{:S(2)}, u32[]{:S(2)}) collective-permute-start(bf16[4,64,128]{2,1,0:T(8,128)(2,1)S(1)} %wire.1.refs_2_), channel_id=1, source_target_pairs={{0,8},{4,12},{8,0},{12,4},{16,24},{20,28},{24,16},{28,20},{1,9},{5... | collective-permute-start | bytes 196616 | tf_op jit(solution)/shard_map/ppermute | solution.py:387
  37.3 0.0 collective-permute-start.10
  37.3 2.1 %collective-permute-done.9.refs_5_ = bf16[4,64,128]{2,1,0:T(8,128)(2,1)S(1)} collective-permute-done((bf16[4,64,128]{2,1,0:T(8,128)(2,1)S(1)}, bf16[4,64,128]{2,1,0:T(8,128)(2,1)S(1)}, u32[]{:S(2)}, u32[]{:S(2)}) %collective-permute-start.9) | collective-permute-done | bytes 65568 | tf_op jit(solution)/shard_map/ppermute | solution.py:387
  39.5 0.0 collective-permute-start.13
  39.5 3.1 %collective-permute-done.8.refs_4_ = bf16[4,64,128]{2,1,0:T(8,128)(2,1)S(1)} collective-permute-done((bf16[4,64,128]{2,1,0:T(8,128)(2,1)S(1)}, bf16[4,64,128]{2,1,0:T(8,128)(2,1)S(1)}, u32[]{:S(2)}, u32[]{:S(2)}) %collective-permute-start.8) | collective-permute-done | bytes 65568 | tf_op jit(solution)/shard_map/ppermute | solution.py:387
  42.6 0.0 collective-permute-start.12
  42.6 0.0 collective-permute-done.7.refs_3_
  42.6 0.5 %collective-permute-start.11 = (bf16[4,64,128]{2,1,0:T(8,128)(2,1)S(1)}, bf16[4,64,128]{2,1,0:T(8,128)(2,1)S(1)}, u32[]{:S(2)}, u32[]{:S(2)}) collective-permute-start(bf16[4,64,128]{2,1,0:T(8,128)(2,1)S(1)} %collective-permute-done.7.refs_3_), channel_id=1, source_target_pairs={{0,4},{4,0},{8,12},{12,8},{16,20},{20,16},{24,28},{28,24},{1,5},{5... | collective-permute-start | bytes 196616 | tf_op jit(solution)/shard_map/ppermute | solution.py:387
  43.1 0.1 pad_add_fusion.refs_0_
  43.2 0.0 copy-start.2
  43.2 0.0 collective-permute-done.10.refs_6_
  43.2 0.0 collective-permute-done.13.refs_9_
  43.2 0.7 %collective-permute-done.12.refs_8_ = bf16[4,64,128]{2,1,0:T(8,128)(2,1)S(1)} collective-permute-done((bf16[4,64,128]{2,1,0:T(8,128)(2,1)S(1)}, bf16[4,64,128]{2,1,0:T(8,128)(2,1)S(1)}, u32[]{:S(2)}, u32[]{:S(2)}) %collective-permute-start.12) | collective-permute-done | bytes 65568 | tf_op jit(solution)/shard_map/ppermute | solution.py:387
  43.9 0.2 collective-permute-done.11.refs_7_
  44.0 0.0 copy-done
  44.0 0.0 copy-done.2
  44.0 1.9 %sum_shifts.1 = f32[4,64,128]{2,1,0:T(8,128)} custom-call(s32[2]{0:T(128)S(1)} %pad_add_fusion.refs_0_, s32[1,8]{1,0:T(1,128)S(1)} %copy-done.2, bf16[4,64,128]{2,1,0:T(8,128)(2,1)S(1)} %wire.1.refs_2_, bf16[4,64,128]{2,1,0:T(8,128)(2,1)S(1)} %collective-permute-done.7.refs_3_, bf16[4,64,128]{2,1,0:T(8,128)(2,1)S(1)} %collective-permute-done.8.refs_4_, ...), custom_call_target="tpu_custom_call" | custom-call | tf_op jit(solution)/shard_map/sum_shifts/pallas_call | solution.py:374
Async XLA Ops:
  0.0 44.0 %copy-start = (f32[8,1,4,64,128]{4,3,2,1,0:T(8,128)S(1)}, f32[8,1,4,64,128]{4,3,2,1,0:T(8,128)}, u32[]{:S(2)}) copy-start(f32[8,1,4,64,128]{4,3,2,1,0:T(8,128)} %param.13) | copy-start | bytes 3145732
  2.5 7.5 %collective-permute-start.2 = (f32[200,128]{1,0:T(8,128)}, f32[200,128]{1,0:T(8,128)S(1)}, u32[]{:S(2)}, u32[]{:S(2)}) collective-permute-start(f32[200,128]{1,0:T(8,128)} %pack.1.refs_2_), channel_id=1, source_target_pairs={{0,3},{1,2},{2,1},{3,0},{4,7},{5,6},{6,5},{7,4},{8,11},{9,10},{10,... | collective-permute-start | bytes 307208 | tf_op jit(solution)/shard_map/ppermute | solution.py:387
  6.3 5.3 %collective-permute-start.1 = (f32[200,128]{1,0:T(8,128)}, f32[200,128]{1,0:T(8,128)S(1)}, u32[]{:S(2)}, u32[]{:S(2)}) collective-permute-start(f32[200,128]{1,0:T(8,128)} %pack.1.refs_2_), channel_id=1, source_target_pairs={{0,2},{1,3},{2,0},{3,1},{4,6},{5,7},{6,4},{7,5},{8,10},{9,11},{10,... | collective-permute-start | bytes 307208 | tf_op jit(solution)/shard_map/ppermute | solution.py:387
  6.9 5.1 %collective-permute-start = (f32[200,128]{1,0:T(8,128)}, f32[200,128]{1,0:T(8,128)S(1)}, u32[]{:S(2)}, u32[]{:S(2)}) collective-permute-start(f32[200,128]{1,0:T(8,128)} %pack.1.refs_2_), channel_id=1, source_target_pairs={{0,1},{1,0},{2,3},{3,2},{4,5},{5,4},{6,7},{7,6},{8,9},{9,8},{10,11... | collective-permute-start | bytes 307208 | tf_op jit(solution)/shard_map/ppermute | solution.py:387
  6.9 5.3 %collective-permute-start.3 = (f32[200,128]{1,0:T(8,128)}, f32[200,128]{1,0:T(8,128)S(1)}, u32[]{:S(2)}, u32[]{:S(2)}) collective-permute-start(f32[200,128]{1,0:T(8,128)} %pack.1.refs_2_), channel_id=1, source_target_pairs={{0,4},{4,0},{8,12},{12,8},{16,20},{20,16},{24,28},{28,24},{1,5},{5... | collective-permute-start | bytes 307208 | tf_op jit(solution)/shard_map/ppermute | solution.py:387
  9.9 2.3 %collective-permute-start.6 = (f32[200,128]{1,0:T(8,128)S(1)}, f32[200,128]{1,0:T(8,128)S(1)}, u32[]{:S(2)}, u32[]{:S(2)}) collective-permute-start(f32[200,128]{1,0:T(8,128)S(1)} %collective-permute-done.2.refs_5_), channel_id=1, source_target_pairs={{0,4},{4,0},{8,12},{12,8},{16,20},{20,16},{24,28},{28,24},{1,5},{5... | collective-permute-start | bytes 307208 | tf_op jit(solution)/shard_map/ppermute | solution.py:387
  11.6 1.3 %collective-permute-start.5 = (f32[200,128]{1,0:T(8,128)S(1)}, f32[200,128]{1,0:T(8,128)S(1)}, u32[]{:S(2)}, u32[]{:S(2)}) collective-permute-start(f32[200,128]{1,0:T(8,128)S(1)} %collective-permute-done.1.refs_4_), channel_id=1, source_target_pairs={{0,4},{4,0},{8,12},{12,8},{16,20},{20,16},{24,28},{28,24},{1,5},{5... | collective-permute-start | bytes 307208 | tf_op jit(solution)/shard_map/ppermute | solution.py:387
  11.9 1.3 %collective-permute-start.4 = (f32[200,128]{1,0:T(8,128)S(1)}, f32[200,128]{1,0:T(8,128)S(1)}, u32[]{:S(2)}, u32[]{:S(2)}) collective-permute-start(f32[200,128]{1,0:T(8,128)S(1)} %collective-permute-done.refs_3_), channel_id=1, source_target_pairs={{0,4},{4,0},{8,12},{12,8},{16,20},{20,16},{24,28},{28,24},{1,5},{5... | collective-permute-start | bytes 307208 | tf_op jit(solution)/shard_map/ppermute | solution.py:387
  13.2 0.9 %copy-start.1 = (f32[200,128]{1,0:T(8,128)S(1)}, f32[200,128]{1,0:T(8,128)}, u32[]{:S(2)}) copy-start(f32[200,128]{1,0:T(8,128)} %pack.1.refs_2_) | copy-start | bytes 307204
  32.9 6.6 %collective-permute-start.9 = (bf16[4,64,128]{2,1,0:T(8,128)(2,1)S(1)}, bf16[4,64,128]{2,1,0:T(8,128)(2,1)S(1)}, u32[]{:S(2)}, u32[]{:S(2)}) collective-permute-start(bf16[4,64,128]{2,1,0:T(8,128)(2,1)S(1)} %wire.1.refs_2_), channel_id=1, source_target_pairs={{0,24},{4,28},{8,16},{12,20},{16,8},{20,12},{24,0},{28,4},{1,25},{... | collective-permute-start | bytes 196616 | tf_op jit(solution)/shard_map/ppermute | solution.py:387
  36.7 6.0 %collective-permute-start.8 = (bf16[4,64,128]{2,1,0:T(8,128)(2,1)S(1)}, bf16[4,64,128]{2,1,0:T(8,128)(2,1)S(1)}, u32[]{:S(2)}, u32[]{:S(2)}) collective-permute-start(bf16[4,64,128]{2,1,0:T(8,128)(2,1)S(1)} %wire.1.refs_2_), channel_id=1, source_target_pairs={{0,16},{4,20},{8,24},{12,28},{16,0},{20,4},{24,8},{28,12},{1,17},{... | collective-permute-start | bytes 196616 | tf_op jit(solution)/shard_map/ppermute | solution.py:387
  36.7 6.0 %collective-permute-start.7 = (bf16[4,64,128]{2,1,0:T(8,128)(2,1)S(1)}, bf16[4,64,128]{2,1,0:T(8,128)(2,1)S(1)}, u32[]{:S(2)}, u32[]{:S(2)}) collective-permute-start(bf16[4,64,128]{2,1,0:T(8,128)(2,1)S(1)} %wire.1.refs_2_), channel_id=1, source_target_pairs={{0,8},{4,12},{8,0},{12,4},{16,24},{20,28},{24,16},{28,20},{1,9},{5... | collective-permute-start | bytes 196616 | tf_op jit(solution)/shard_map/ppermute | solution.py:387
  37.3 5.9 %collective-permute-start.10 = (bf16[4,64,128]{2,1,0:T(8,128)(2,1)S(1)}, bf16[4,64,128]{2,1,0:T(8,128)(2,1)S(1)}, u32[]{:S(2)}, u32[]{:S(2)}) collective-permute-start(bf16[4,64,128]{2,1,0:T(8,128)(2,1)S(1)} %wire.1.refs_2_), channel_id=1, source_target_pairs={{0,4},{4,0},{8,12},{12,8},{16,20},{20,16},{24,28},{28,24},{1,5},{5... | collective-permute-start | bytes 196616 | tf_op jit(solution)/shard_map/ppermute | solution.py:387
  39.5 3.7 %collective-permute-start.13 = (bf16[4,64,128]{2,1,0:T(8,128)(2,1)S(1)}, bf16[4,64,128]{2,1,0:T(8,128)(2,1)S(1)}, u32[]{:S(2)}, u32[]{:S(2)}) collective-permute-start(bf16[4,64,128]{2,1,0:T(8,128)(2,1)S(1)} %collective-permute-done.9.refs_5_), channel_id=1, source_target_pairs={{0,4},{4,0},{8,12},{12,8},{16,20},{20,16},{24,28},{28,24},{1,5},{5... | collective-permute-start | bytes 196616 | tf_op jit(solution)/shard_map/ppermute | solution.py:387
  42.6 1.3 %collective-permute-start.12 = (bf16[4,64,128]{2,1,0:T(8,128)(2,1)S(1)}, bf16[4,64,128]{2,1,0:T(8,128)(2,1)S(1)}, u32[]{:S(2)}, u32[]{:S(2)}) collective-permute-start(bf16[4,64,128]{2,1,0:T(8,128)(2,1)S(1)} %collective-permute-done.8.refs_4_), channel_id=1, source_target_pairs={{0,4},{4,0},{8,12},{12,8},{16,20},{20,16},{24,28},{28,24},{1,5},{5... | collective-permute-start | bytes 196616 | tf_op jit(solution)/shard_map/ppermute | solution.py:387
  42.6 1.4 %collective-permute-start.11 = (bf16[4,64,128]{2,1,0:T(8,128)(2,1)S(1)}, bf16[4,64,128]{2,1,0:T(8,128)(2,1)S(1)}, u32[]{:S(2)}, u32[]{:S(2)}) collective-permute-start(bf16[4,64,128]{2,1,0:T(8,128)(2,1)S(1)} %collective-permute-done.7.refs_3_), channel_id=1, source_target_pairs={{0,4},{4,0},{8,12},{12,8},{16,20},{20,16},{24,28},{28,24},{1,5},{5... | collective-permute-start | bytes 196616 | tf_op jit(solution)/shard_map/ppermute | solution.py:387
  43.2 0.8 %copy-start.2 = (s32[1,8]{1,0:T(1,128)S(1)}, s32[1,8]{1,0:T(1,128)}, u32[]{:S(2)}) copy-start(s32[1,8]{1,0:T(1,128)} %refs_1_.2) | copy-start | bytes 100

commit v2 on v1

--- a/solution.py
+++ b/solution.py
@@ -27,52 +27,74 @@
     return parts[0]
 
 
-def invert_small(xr, xi, sub):
-    for k in range(8):
-        pr, pi = row(xr[k], k), row(xi[k], k)
-        q = 1.0 / (pr * pr + pi * pi)
-        ipr, ipi = pr * q, -(pi * q)
-        at = sub == k
-        cr, ci = xr[k], xi[k]
-        for j in [(k + 1 + d) % 8 for d in range(7)]:
-            ar, ai = row(xr[j], k), row(xi[j], k)
-            tr = ar * ipr - ai * ipi
-            ti = ar * ipi + ai * ipr
-            xr[j] = jnp.where(at, tr, xr[j] - (cr * tr - ci * ti))
-            xi[j] = jnp.where(at, ti, xi[j] - (cr * ti + ci * tr))
-        xr[k] = jnp.where(at, ipr, ci * ipi - cr * ipr)
-        xi[k] = jnp.where(at, ipi, -(cr * ipi + ci * ipr))
-    return xr, xi
-
-
-def pair_inverse(mr, mi):
+def far_product(whole_r, whole_i, pr, pi, t):
+    lane = lax.broadcasted_iota(jnp.int32, (8, 128), 1)
+    keep = lane < 64
+    source = (lane & 64) + 8 * t + (lane & 7)
+    re = jnp.concatenate([jnp.take_along_axis(x, source, axis=1) for x in whole_r], 0)
+    im = jnp.concatenate([jnp.take_along_axis(x, source, axis=1) for x in whole_i], 0)
+    wide = lax.broadcasted_iota(jnp.int32, re.shape, 1)
+    both = jnp.where((wide & 8) > 0, im, re)
+    high = both.astype(bf16).astype(f32)
+    left = jnp.where(((wide & 63) >> 4) == 1, both - high, high).astype(bf16)
+    zero = jnp.zeros((8, 128), f32)
+    empty = jnp.zeros((16, 256), bf16)
+    right = []
+    for kept in (keep, ~keep):
+        r, i = jnp.where(kept, pr, zero), jnp.where(kept, pi, zero)
+        high, low = split(
+            jnp.concatenate([jnp.concatenate([r, i], 1), jnp.concatenate([-i, r], 1)], 0)
+        )
+        right += [high, high, low, empty]
+    out = dot(left, jnp.concatenate(right, 0))
+    return out[:, :128], out[:, 128:]
+
+
+def pair_inverse(mr, mi, beside):
     lane = lax.broadcasted_iota(jnp.int32, (8, 128), 1)
     sub = lax.broadcasted_iota(jnp.int32, (8, 128), 0)
     col = lane & 63
     mr, mi = list(mr), list(mi)
     for t in range(8):
+        near = (t + 1) % 8
+        far = [(t + d) % 8 for d in range(2, 8)]
+        inside = (col >= 8 * t) & (col < 8 * t + 8)
         xr = [column(mr[t], 8 * t + j, lane) for j in range(8)]
         xi = [column(mi[t], 8 * t + j, lane) for j in range(8)]
-        xr, xi = invert_small(xr, xi, sub)
-        inside = (col >= 8 * t) & (col < 8 * t + 8)
+        cr = [column(mr[near], 8 * t + j, lane) for j in range(8)]
+        ci = [column(mi[near], 8 * t + j, lane) for j in range(8)]
         rr = jnp.where(inside, jnp.where(col == sub + 8 * t, 1.0, 0.0), mr[t])
         ri = jnp.where(inside, 0.0, mi[t])
-        sr, si = [], []
-        for j in range(8):
-            br, bi = row(rr, j), row(ri, j)
-            sr.append(xr[j] * br - xi[j] * bi)
-            si.append(xr[j] * bi + xi[j] * br)
-        pr, pi = added(sr), added(si)
-        rows = [(row(pr, j), row(pi, j)) for j in range(8)]
-        for s in [(t + d) % 8 for d in range(1, 8)]:
-            ar, ai = [], []
-            for j in range(8):
-                cr, ci = column(mr[s], 8 * t + j, lane), column(mi[s], 8 * t + j, lane)
-                ar.append(cr * rows[j][0] - ci * rows[j][1])
-                ai.append(cr * rows[j][1] + ci * rows[j][0])
-            mr[s] = jnp.where(inside, 0.0, mr[s]) - added(ar)
-            mi[s] = jnp.where(inside, 0.0, mi[s]) - added(ai)
-        mr[t], mi[t] = pr, pi
+        for k in range(8):
+            at = sub == k
+            pr, pi = row(xr[k], k), row(xi[k], k)
+            q = 1.0 / (pr * pr + pi * pi)
+            er, ei = jnp.where(at, -1.0, xr[k]), jnp.where(at, 0.0, xi[k])
+
+            def step(yr, yi):
+                ar, ai = row(yr, k), row(yi, k)
+                ur, ui = ar * pr + ai * pi, ai * pr - ar * pi
+                wr, wi = er * ur - ei * ui, er * ui + ei * ur
+                return jnp.where(at, 0.0, yr) - wr * q, jnp.where(at, 0.0, yi) - wi * q
+
+            for j in range(k + 1, 8):
+                xr[j], xi[j] = step(xr[j], xi[j])
+            rr, ri = step(rr, ri)
+        lines = [(row(rr, j), row(ri, j)) for j in range(8)]
+        more_r = added([cr[j] * lines[j][0] - ci[j] * lines[j][1] for j in range(8)])
+        more_i = added([cr[j] * lines[j][1] + ci[j] * lines[j][0] for j in range(8)])
+        mr[near] = jnp.where(inside, 0.0, mr[near]) - more_r
+        mi[near] = jnp.where(inside, 0.0, mi[near]) - more_i
+        out_r, out_i = far_product([mr[s] for s in far], [mi[s] for s in far], rr, ri, t)
+        for n, s in enumerate(far):
+            mr[s] = jnp.where(inside, 0.0, mr[s]) - out_r[8 * n : 8 * n + 8]
+            mi[s] = jnp.where(inside, 0.0, mi[s]) - out_i[8 * n : 8 * n + 8]
+        mr[t], mi[t] = rr, ri
+        work = next(beside, None)
+        if work is not None:
+            work()
+    for work in beside:
+        work()
     return mr, mi
 
 
@@ -80,8 +102,8 @@
     return [x[8 * s : 8 * s + 8] for s in range(8)]
 
 
-def invert_pair(zr, zi):
-    mr, mi = pair_inverse(slabs(zr), slabs(zi))
+def invert_pair(zr, zi, beside=()):
+    mr, mi = pair_inverse(slabs(zr), slabs(zi), iter(beside))
     return jnp.concatenate(mr, 0), jnp.concatenate(mi, 0)
 
 
@@ -154,34 +176,55 @@
     return pltpu.roll(x, 64, 1)
 
 
-def pack_kernel(core_ref, counts_ref, hams_ref, links_ref, shifts_ref, rates_ref, out_ref):
-    first = 2 * core_ref[0]
-    out_ref[0:64] = links_ref[first]
-    out_ref[64:128] = links_ref[first + 1]
-    one, two = hams_ref[first], hams_ref[first + 1]
+def packed_pair(one, two):
     lower = lax.broadcasted_iota(jnp.int32, (64, 128), 0) >= (
         lax.broadcasted_iota(jnp.int32, (64, 128), 1) & 63
     )
-    keep = low_lanes(one)
     left = jnp.where(lower, one, swapped(one))
     right = jnp.where(lower, swapped(two), two)
-    out_ref[128:192] = jnp.where(keep, left, right)
+    return jnp.where(low_lanes(one), left, right)
+
+
+def pack_kernel(
+    counts_ref, shifts_ref, rates_ref, hams_ref, links_ref, out_ref
+):
+    first = 2 * (lax.axis_index("energy") & 1)
+    out_ref[0:64] = links_ref[first]
+    out_ref[64:128] = links_ref[first + 1]
+    out_ref[128:192] = packed_pair(hams_ref[first], hams_ref[first + 1])
     out_ref[192:194] = shifts_ref[...]
     out_ref[194:196] = rates_ref[...]
-    out_ref[196:200] = jnp.full((4, 128), counts_ref[0].astype(f32))
-
-
-def pack(core, counts, hams, links, shifts, rates):
+    out_ref[196:200] = jnp.broadcast_to(counts_ref[...].astype(f32), (4, 128))
+
+
+def pack(*arrays):
     return pl.pallas_call(
         pack_kernel,
         out_shape=jax.ShapeDtypeStruct((200, 128), f32),
-        in_specs=[SMEM, SMEM, VMEM, VMEM, VMEM, VMEM],
+        in_specs=[VMEM] * len(arrays),
         out_specs=VMEM,
         name="pack",
-    )(core, counts, hams, links, shifts, rates)
-
-
-def wire_kernel(segs, place_ref, energy_ref, *refs):
+    )(*arrays)
+
+
+def settle_kernel(energies_ref, in_ref, out_ref):
+    out_ref[0:192] = in_ref[0:192]
+    last = lax.broadcasted_iota(jnp.int32, (8, 128), 0) >= 6
+    out_ref[192:200] = jnp.where(last, energies_ref[0], in_ref[192:200])
+
+
+def settle(energies, piece):
+    return pl.pallas_call(
+        settle_kernel,
+        out_shape=jax.ShapeDtypeStruct(piece.shape, f32),
+        in_specs=[SMEM, VMEM],
+        out_specs=VMEM,
+        compiler_params=pltpu.CompilerParams(vmem_limit_bytes=4 * 2**20),
+        name="settle",
+    )(energies, piece)
+
+
+def wire_kernel(segs, *refs):
     own = refs[:segs]
     other = refs[segs : 2 * segs]
     out_ref = refs[2 * segs]
@@ -190,8 +233,7 @@
     )
     blocks = 2 * segs
     half = segs
-    place, core = place_ref[0], place_ref[1]
-    energy = energy_ref[0]
+    place, core = lax.axis_index("seg"), lax.axis_index("energy") & 1
 
     for k in range(segs):
         seg = jnp.bitwise_xor(place, k)
@@ -200,6 +242,7 @@
             u_ref[4 * seg + 2 * c + 1] = ref[64:128]
             h_ref[2 * seg + c] = ref[128:192]
         m_ref[seg] = own[k][192:200]
+    energy = own[0][198:199]
 
     start = jnp.int32(0)
     first, used = jnp.int32(0), jnp.int32(0)
@@ -255,52 +298,134 @@
         )
         return carry
 
-    lax.fori_loop(0, half, prepare_block, 0)
-    lax.fori_loop(1, half + 1, prepare_link, 0)
-
-    s_ref[...] = jnp.zeros_like(s_ref)
-
-    def inward(i, carry):
-        fr = ar_ref[i] - s_ref[0]
-        fi = ai_ref[i] - s_ref[1]
-        gr, gi = invert_pair(fr, fi)
-        g_ref[i, 0] = gr
-        g_ref[i, 1] = gi
-
-        @pl.when(i < half)
-        def _():
-            tr, ti = times_right(gr, gi, yright_ref[i, 0], yright_ref[i, 1])
-            t_ref[i] = left_factor(tr, ti)
-            sr, si = times_left(yleft_ref[i], tr, ti)
-            kr, ki = times_left(yleft_ref[i], gr, gi)
-            high, low = right_factor(kr, ki)
-            k_ref[i, 0] = high
-            k_ref[i, 1] = low
-            s_ref[0] = sr
-            s_ref[1] = si
-
-        @pl.when(i == half - 1)
-        def _():
-            s_ref[0] = swapped(s_ref[0])
-            s_ref[1] = swapped(s_ref[1])
-            ar_ref[half] = fr
-            ai_ref[half] = fi
-
-        return carry
-
-    lax.fori_loop(0, half + 1, inward, 0)
-
-    g_ref[half - 1] = g_ref[half]
-
-    def outward(step, carry):
-        i = half - 2 - step
-        zr, zi = times_right(g_ref[i + 1, 0], g_ref[i + 1, 1], k_ref[i, 0], k_ref[i, 1])
-        wr, wi = times_left(t_ref[i], zr, zi)
-        g_ref[i, 0] = g_ref[i, 0] + wr
-        g_ref[i, 1] = g_ref[i, 1] + wi
-        return carry
-
-    lax.fori_loop(0, half - 1, outward, 0)
+    def long_wire():
+        lax.fori_loop(0, half, prepare_block, 0)
+        lax.fori_loop(1, half + 1, prepare_link, 0)
+
+        s_ref[...] = jnp.zeros_like(s_ref)
+
+        def inward(i, carry):
+            fr = ar_ref[i] - s_ref[0]
+            fi = ai_ref[i] - s_ref[1]
+            gr, gi = invert_pair(fr, fi)
+            g_ref[i, 0] = gr
+            g_ref[i, 1] = gi
+
+            @pl.when(i < half)
+            def _():
+                tr, ti = times_right(gr, gi, yright_ref[i, 0], yright_ref[i, 1])
+                t_ref[i] = left_factor(tr, ti)
+                sr, si = times_left(yleft_ref[i], tr, ti)
+                kr, ki = times_left(yleft_ref[i], gr, gi)
+                high, low = right_factor(kr, ki)
+                k_ref[i, 0] = high
+                k_ref[i, 1] = low
+                s_ref[0] = sr
+                s_ref[1] = si
+
+            @pl.when(i == half - 1)
+            def _():
+                s_ref[0] = swapped(s_ref[0])
+                s_ref[1] = swapped(s_ref[1])
+                ar_ref[half] = fr
+                ai_ref[half] = fi
+
+            return carry
+
+        lax.fori_loop(0, half + 1, inward, 0)
+
+        g_ref[half - 1] = g_ref[half]
+
+        def outward(step, carry):
+            i = half - 2 - step
+            zr, zi = times_right(g_ref[i + 1, 0], g_ref[i + 1, 1], k_ref[i, 0], k_ref[i, 1])
+            wr, wi = times_left(t_ref[i], zr, zi)
+            g_ref[i, 0] = g_ref[i, 0] + wr
+            g_ref[i, 1] = g_ref[i, 1] + wi
+            return carry
+
+        lax.fori_loop(0, half - 1, outward, 0)
+
+    def short_wire():
+        last = half - 2
+        g, t, k = [None] * half, [None] * half, [None] * half
+        base, left, right = [None] * half, [None] * half, [None] * half
+
+        def do_block(i):
+            return lambda: prepare_block(i, 0)
+
+        def do_link(i):
+            return lambda: prepare_link(i, 0)
+
+        def do_k(i):
+            def run():
+                k[i] = times_left(yleft_ref[i], *g[i])
+                high, low = right_factor(*k[i])
+                k_ref[i, 0] = high
+                k_ref[i, 1] = low
+                if i == last:
+                    base[i], left[i], right[i] = g[i], t[i], k[i]
+
+            return run
+
+        def do_outer(i):
+            def one():
+                base[i] = times_left(t_ref[i], *base[i + 1])
+
+            def two():
+                more = times_right(*base[i], k_ref[i, 0], k_ref[i, 1])
+                base[i] = (g[i][0] + more[0], g[i][1] + more[1])
+
+            def three():
+                left[i] = times_left(t_ref[i], *left[i + 1])
+                t_ref[i] = left_factor(*left[i])
+
+            def four():
+                right[i] = times_right(*right[i + 1], k_ref[i, 0], k_ref[i, 1])
+                high, low = right_factor(*right[i])
+                k_ref[i, 0] = high
+                k_ref[i, 1] = low
+
+            return [one, two, three, four]
+
+        beside = [[] for _ in range(half + 1)]
+        beside[0] = [do_link(1), do_block(1)]
+        for i in range(2, half):
+            beside[0] += [do_block(i), do_link(i)]
+        beside[0] += [do_link(half)]
+        for i in range(half - 1):
+            beside[i + 1] += [do_k(i)]
+        for n, i in enumerate(range(last - 1, -1, -1)):
+            beside[min(half - 1 + n, half)] += do_outer(i)
+
+        prepare_block(0, 0)
+        sr = si = None
+        for i in range(half + 1):
+            if i == 0:
+                fr, fi = ar_ref[0], ai_ref[0]
+            elif i < half:
+                fr, fi = ar_ref[i] - sr, ai_ref[i] - si
+            else:
+                fr, fi = fr - swapped(sr), fi - swapped(si)
+            zr, zi = invert_pair(fr, fi, beside[i])
+            if i < half:
+                g[i] = (zr, zi)
+                t[i] = times_right(zr, zi, yright_ref[i, 0], yright_ref[i, 1])
+                sr, si = times_left(yleft_ref[i], *t[i])
+                if i < half - 1:
+                    t_ref[i] = left_factor(*t[i])
+        g_ref[half - 1, 0] = zr
+        g_ref[half - 1, 1] = zi
+        for i in range(half - 1):
+            more = times_right(zr, zi, k_ref[i, 0], k_ref[i, 1])
+            more = times_left(t_ref[i], *more)
+            g_ref[i, 0] = base[i][0] + more[0]
+            g_ref[i, 1] = base[i][1] + more[1]
+
+    if half in (3, 4, 5):
+        short_wire()
+    else:
+        long_wire()
 
     for k in range(4):
         block = jnp.minimum(first + k, blocks - 1)
@@ -312,7 +437,7 @@
         out_ref[k] = (jnp.where(keep, re, im) * live).astype(bf16)
 
 
-def wire(place, energy, own, other):
+def wire(own, other):
     segs = len(own)
     half = segs
 
@@ -322,7 +447,7 @@
     return pl.pallas_call(
         kernel,
         out_shape=jax.ShapeDtypeStruct((4, 64, 128), bf16),
-        in_specs=[SMEM, SMEM] + [VMEM] * (2 * segs),
+        in_specs=[VMEM] * (2 * segs),
         out_specs=VMEM,
         scratch_shapes=[
             pltpu.VMEM((4 * segs, 64, 128), f32),
@@ -338,16 +463,16 @@
             pltpu.VMEM((half, 2, 256, 256), bf16),
             pltpu.VMEM((half, 256, 256), bf16),
         ],
-        compiler_params=pltpu.CompilerParams(vmem_limit_bytes=48 * 2**20),
+        compiler_params=pltpu.CompilerParams(vmem_limit_bytes=(8 + 2 * segs) * 2**20),
         name="wire",
-    )(place, energy, *own, *other)
-
-
-def sum_kernel(chips, place_ref, sources_ref, *refs):
+    )(*own, *other)
+
+
+def sum_kernel(chips, sources_ref, *refs):
     own = refs[:chips]
     other = refs[chips : 2 * chips]
     screened_ref, out_ref, all_ref = refs[2 * chips :]
-    chip, core = place_ref[0], place_ref[1]
+    chip, core = lax.axis_index("energy") >> 1, lax.axis_index("energy") & 1
     for k in range(chips):
         place = jnp.bitwise_xor(chip, k) * cores
         all_ref[place + core] = own[k][...]
@@ -365,7 +490,7 @@
         out_ref[slot] = jnp.where(keep, direct - swapped(direct), crossed + swapped(crossed))
 
 
-def sum_shifts(place, sources, own, other, screened):
+def sum_shifts(sources, own, other, screened):
     chips = len(own)
 
     def kernel(*refs):
@@ -374,12 +499,12 @@
     return pl.pallas_call(
         kernel,
         out_shape=jax.ShapeDtypeStruct(screened.shape[1:], f32),
-        in_specs=[SMEM, SMEM] + [VMEM] * (2 * chips + 1),
+        in_specs=[SMEM] + [VMEM] * (2 * chips + 1),
         out_specs=VMEM,
         scratch_shapes=[pltpu.VMEM((cores * chips,) + screened.shape[1:], bf16)],
-        compiler_params=pltpu.CompilerParams(vmem_limit_bytes=48 * 2**20),
+        compiler_params=pltpu.CompilerParams(vmem_limit_bytes=(4 + 2 * chips) * 2**20),
         name="sum_shifts",
-    )(place, sources, *own, *other, screened)
+    )(sources, *own, *other, screened)
 
 
 def flipped_to(x, axis, mask):
@@ -390,24 +515,32 @@
 def body(energies, h_blocks, couplings, shift_real, shift_rate, screened, sources, counts):
     segs = lax.axis_size("seg")
     chips = lax.axis_size("energy") // cores
-    seg = lax.axis_index("seg")
-    energy = lax.axis_index("energy")
-    core, chip = energy % cores, energy // cores
-    piece = pack(
-        core[None],
-        counts,
-        h_blocks[0],
-        couplings[0],
-        shift_real.reshape(2, 128),
-        shift_rate.reshape(2, 128),
+    first = lax.axis_index("energy") % cores == 0
+    hams, links = h_blocks[0], couplings[0]
+    one = jnp.where(first, hams[0], hams[2])
+    two = jnp.where(first, hams[1], hams[3])
+    lower = jnp.arange(64)[:, None] >= jnp.arange(64)[None, :]
+    packed = jnp.concatenate(
+        [jnp.where(lower, one[:, :64], one[:, 64:]), jnp.where(lower, two[:, :64], two[:, 64:])], 1
     )
-    own = [piece] + [flipped_to(piece, "seg", k) for k in range(1, segs)]
-    other = [flipped_to(x, "energy", 1) for x in own]
-    greens = wire(jnp.stack([seg, core]), energies, own, other)
+    piece = jnp.concatenate(
+        [
+            jnp.where(first, links[0], links[2]),
+            jnp.where(first, links[1], links[3]),
+            packed,
+            shift_real.reshape(2, 128),
+            shift_rate.reshape(2, 128),
+            jnp.broadcast_to(counts.astype(f32)[:, None], (4, 128)),
+        ],
+        0,
+    )
+    sent = [flipped_to(piece, "seg", k) for k in range(1, segs)]
+    own = [settle(energies, piece)] + sent
+    other = [flipped_to(x, "energy", 1) for x in [piece] + sent]
+    greens = wire(own, other)
     near = [greens] + [flipped_to(greens, "energy", cores * k) for k in range(1, chips)]
     far = [flipped_to(x, "energy", 1) for x in near]
-    out = sum_shifts(jnp.stack([chip, core]), sources, near, far, screened[:, 0])
-    return out[None, None]
+    return sum_shifts(sources, near, far, screened[:, 0])[None, None]
 
 
 def solution(mesh):

time: 46.1 us -> 39.3 us (0.85)
  Pallas kernels: 22.3 us -> 14.7 us
  other arithmetic: 0.15 us -> 1.12 us
    pallas_call x1, Pallas kernels: 18.7 us -> 12.9 us  [wire(): pl.pallas_call(kernel, out_shape=jax.ShapeDtypeStruct((4, 64, 128), bf16)...]
    pallas_call x1, Pallas kernels: 1.7 us -> 0.01 us  [settle(): pl.pallas_call(settle_kernel, out_shape=jax.ShapeDtypeStruct(piece.shape,...]
    select_n x0 -> x3, other arithmetic: none -> 1.04 us  [the longest x1 0.89 us: body(): one = jnp.where(first, hams[0], hams[2])]
    unnamed x6 -> x4, local copies, waits for them, and re-layouts: 0.9 us -> 0.01 us
    concatenate x0 -> x1, local copies, waits for them, and re-layouts: none -> 0.73 us  [body(): jnp.concatenate([jnp.where(first, links[0], links[2]), jnp.where(first, l...]
where the time goes in v2:
time: 39.3 us; the launch traced here: 39.1 us
  Pallas kernels  14.7 us (37%)
  waiting for transfers between devices  11.3 us (29%)
  starting transfers between devices  9.72 us (25%)
  between operations  1.45 us (4%)
  other arithmetic  1.12 us (3%)
  local copies, waits for them, and re-layouts  0.74 us (2%)
    pallas_call x1, Pallas kernels, wire(): pl.pallas_call(kernel, out_shape=jax.ShapeDtypeStruct((4, 64, 128), bf16)...  12.9 us
    ppermute x14, waiting for transfers between devices, flipped_to(): return lax.ppermute(x, axis, [(i, i ^ mask) for i in range(count)])  11.3 us
    ppermute x14, starting transfers between devices, flipped_to(): return lax.ppermute(x, axis, [(i, i ^ mask) for i in range(count)])  9.72 us
    pallas_call x1, Pallas kernels, sum_shifts(): pl.pallas_call(kernel, out_shape=jax.ShapeDtypeStruct(screened.shape[1:],...  1.85 us
    select_n x1, other arithmetic, body(): one = jnp.where(first, hams[0], hams[2])  0.89 us
  transfers between devices with their start and end apart: 14, of which 9 were waited for; matrix products, arithmetic and copies ran while one was open for 0% of the time, Pallas kernels for 0%

profile of v2, /device:TPU:0, one launch (start us, length us, event | category | flops | bytes accessed | tf_op | source)
XLA Modules:
  0.0 39.1 jit_solution(15450087264919771954)
XLA Ops:
  0.0 0.0 copy-start
  0.7 0.9 %select_bitcast_fusion.1 = (f32[64,128]{1,0:T(8,128)S(1)}, f32[64,128]{1,0:T(8,128)S(1)}, f32[64,128]{1,0:T(8,128)S(1)}, f32[64,128]{1,0:T(8,128)S(1)}) fusion(f32[1,4,64,128]{3,2,1,0:T(8,128)} %param.9, pred[]{:T(512)S(6)} %eq.5, f32[1,4,64,128]{3,2,1,0:T(8,128)} %param.10), kind=kLoop, calls=%fused_computation.4 | loop fusion | flops 32768 | bytes 393217 | tf_op jit(solution)/shard_map/jit(_where)/select_n | solution.py:520
  1.6 0.1 slice_select_fusion.1
  1.7 0.1 slice_select_fusion
  1.8 0.1 pad_maximum_fusion
  1.9 0.7 %concatenate.7.in_ref = f32[200,128]{1,0:T(8,128)S(1)} concatenate(f32[64,128]{1,0:T(8,128)S(1)} %get-tuple-element.9, f32[64,128]{1,0:T(8,128)S(1)} %get-tuple-element.10, f32[64,128]{1,0:T(8,128)S(1)} %pad_maximum_fusion, f32[2,128]{1,0:T(2,128)} %bitcast.14, f32[2,128]{1,0:T(2,128)} %bitcast.15, f32[4,128]{1,0:T(4,128)S(1)} %broadcast_in_dim.14), dimensions={0} | concatenate | bytes 204800 | tf_op jit(solution)/shard_map/concatenate | solution.py:526
  2.6 3.9 %collective-permute-start.2 = (f32[200,128]{1,0:T(8,128)S(1)}, f32[200,128]{1,0:T(8,128)S(1)}, u32[]{:S(2)}, u32[]{:S(2)}) collective-permute-start(f32[200,128]{1,0:T(8,128)S(1)} %concatenate.7.in_ref), channel_id=1, source_target_pairs={{0,3},{1,2},{2,1},{3,0},{4,7},{5,6},{6,5},{7,4},{8,11},{9,10},{10,... | collective-permute-start | bytes 307208 | tf_op jit(solution)/shard_map/ppermute | solution.py:512
  6.5 0.5 %collective-permute-start.1 = (f32[200,128]{1,0:T(8,128)S(1)}, f32[200,128]{1,0:T(8,128)S(1)}, u32[]{:S(2)}, u32[]{:S(2)}) collective-permute-start(f32[200,128]{1,0:T(8,128)S(1)} %concatenate.7.in_ref), channel_id=1, source_target_pairs={{0,2},{1,3},{2,0},{3,1},{4,6},{5,7},{6,4},{7,5},{8,10},{9,11},{10,... | collective-permute-start | bytes 307208 | tf_op jit(solution)/shard_map/ppermute | solution.py:512
  7.0 0.1 collective-permute-start
  7.1 0.0 collective-permute-start.3
  7.1 2.7 %collective-permute-done.2.refs_3_ = f32[200,128]{1,0:T(8,128)S(1)} collective-permute-done((f32[200,128]{1,0:T(8,128)S(1)}, f32[200,128]{1,0:T(8,128)S(1)}, u32[]{:S(2)}, u32[]{:S(2)}) %collective-permute-start.2) | collective-permute-done | bytes 102432 | tf_op jit(solution)/shard_map/ppermute | solution.py:512
  9.8 0.0 collective-permute-start.6
  9.8 1.8 %collective-permute-done.1.refs_2_ = f32[200,128]{1,0:T(8,128)S(1)} collective-permute-done((f32[200,128]{1,0:T(8,128)S(1)}, f32[200,128]{1,0:T(8,128)S(1)}, u32[]{:S(2)}, u32[]{:S(2)}) %collective-permute-start.1) | collective-permute-done | bytes 102432 | tf_op jit(solution)/shard_map/ppermute | solution.py:512
  11.6 0.0 collective-permute-start.5
  11.6 0.3 collective-permute-done.refs_1_
  11.9 0.2 collective-permute-start.4
  12.8 0.0 collective-permute-done.3.refs_4_
  12.8 0.0 collective-permute-done.6.refs_7_
  12.8 0.1 collective-permute-done.5.refs_6_
  12.9 0.3 collective-permute-done.4.refs_5_
  13.2 12.9 %wire.1.refs_1_ = bf16[4,64,128]{2,1,0:T(8,128)(2,1)S(1)} custom-call(f32[200,128]{1,0:T(8,128)S(1)} %settle.1.refs_0_, f32[200,128]{1,0:T(8,128)S(1)} %collective-permute-done.refs_1_, f32[200,128]{1,0:T(8,128)S(1)} %collective-permute-done.1.refs_2_, f32[200,128]{1,0:T(8,128)S(1)} %collective-permute-done.2.refs_3_, ...), custom_call_target="tpu_custom_call" | custom-call | tf_op jit(solution)/shard_map/wire/pallas_call | solution.py:447
  26.0 0.0 copy-start.1
  26.1 3.8 %collective-permute-start.9 = (bf16[4,64,128]{2,1,0:T(8,128)(2,1)S(1)}, bf16[4,64,128]{2,1,0:T(8,128)(2,1)S(1)}, u32[]{:S(2)}, u32[]{:S(2)}) collective-permute-start(bf16[4,64,128]{2,1,0:T(8,128)(2,1)S(1)} %wire.1.refs_1_), channel_id=1, source_target_pairs={{0,24},{4,28},{8,16},{12,20},{16,8},{20,12},{24,0},{28,4},{1,25},{... | collective-permute-start | bytes 196616 | tf_op jit(solution)/shard_map/ppermute | solution.py:512
  29.8 0.0 collective-permute-start.8
  29.8 0.7 %collective-permute-start.7 = (bf16[4,64,128]{2,1,0:T(8,128)(2,1)S(1)}, bf16[4,64,128]{2,1,0:T(8,128)(2,1)S(1)}, u32[]{:S(2)}, u32[]{:S(2)}) collective-permute-start(bf16[4,64,128]{2,1,0:T(8,128)(2,1)S(1)} %wire.1.refs_1_), channel_id=1, source_target_pairs={{0,8},{4,12},{8,0},{12,4},{16,24},{20,28},{24,16},{28,20},{1,9},{5... | collective-permute-start | bytes 196616 | tf_op jit(solution)/shard_map/ppermute | solution.py:512
  30.5 0.0 collective-permute-start.10
  30.5 2.1 %collective-permute-done.9.refs_4_ = bf16[4,64,128]{2,1,0:T(8,128)(2,1)S(1)} collective-permute-done((bf16[4,64,128]{2,1,0:T(8,128)(2,1)S(1)}, bf16[4,64,128]{2,1,0:T(8,128)(2,1)S(1)}, u32[]{:S(2)}, u32[]{:S(2)}) %collective-permute-start.9) | collective-permute-done | bytes 65568 | tf_op jit(solution)/shard_map/ppermute | solution.py:512
  32.7 0.0 collective-permute-start.13
  32.7 3.1 %collective-permute-done.8.refs_3_ = bf16[4,64,128]{2,1,0:T(8,128)(2,1)S(1)} collective-permute-done((bf16[4,64,128]{2,1,0:T(8,128)(2,1)S(1)}, bf16[4,64,128]{2,1,0:T(8,128)(2,1)S(1)}, u32[]{:S(2)}, u32[]{:S(2)}) %collective-permute-start.8) | collective-permute-done | bytes 65568 | tf_op jit(solution)/shard_map/ppermute | solution.py:512
  35.8 0.0 collective-permute-start.12
  35.8 0.0 collective-permute-done.7.refs_2_
  35.8 0.5 %collective-permute-start.11 = (bf16[4,64,128]{2,1,0:T(8,128)(2,1)S(1)}, bf16[4,64,128]{2,1,0:T(8,128)(2,1)S(1)}, u32[]{:S(2)}, u32[]{:S(2)}) collective-permute-start(bf16[4,64,128]{2,1,0:T(8,128)(2,1)S(1)} %collective-permute-done.7.refs_2_), channel_id=1, source_target_pairs={{0,4},{4,0},{8,12},{12,8},{16,20},{20,16},{24,28},{28,24},{1,5},{5... | collective-permute-start | bytes 196616 | tf_op jit(solution)/shard_map/ppermute | solution.py:512
  36.3 0.0 collective-permute-done.10.refs_5_
  36.3 0.0 collective-permute-done.13.refs_8_
  36.3 0.7 %collective-permute-done.12.refs_7_ = bf16[4,64,128]{2,1,0:T(8,128)(2,1)S(1)} collective-permute-done((bf16[4,64,128]{2,1,0:T(8,128)(2,1)S(1)}, bf16[4,64,128]{2,1,0:T(8,128)(2,1)S(1)}, u32[]{:S(2)}, u32[]{:S(2)}) %collective-permute-start.12) | collective-permute-done | bytes 65568 | tf_op jit(solution)/shard_map/ppermute | solution.py:512
  37.1 0.2 collective-permute-done.11.refs_6_
  37.2 0.0 copy-done
  37.2 0.0 copy-done.1
  37.2 1.9 %sum_shifts.1 = f32[4,64,128]{2,1,0:T(8,128)} custom-call(s32[1,8]{1,0:T(1,128)S(1)} %copy-done.1, bf16[4,64,128]{2,1,0:T(8,128)(2,1)S(1)} %wire.1.refs_1_, bf16[4,64,128]{2,1,0:T(8,128)(2,1)S(1)} %collective-permute-done.7.refs_2_, bf16[4,64,128]{2,1,0:T(8,128)(2,1)S(1)} %collective-permute-done.8.refs_3_, ...), custom_call_target="tpu_custom_call" | custom-call | tf_op jit(solution)/shard_map/sum_shifts/pallas_call | solution.py:499
  (2 shorter events, 0.0 us)
Async XLA Ops:
  0.0 37.2 %copy-start = (f32[8,1,4,64,128]{4,3,2,1,0:T(8,128)S(1)}, f32[8,1,4,64,128]{4,3,2,1,0:T(8,128)}, u32[]{:S(2)}) copy-start(f32[8,1,4,64,128]{4,3,2,1,0:T(8,128)} %param.13) | copy-start | bytes 3145732
  2.6 7.2 %collective-permute-start.2 = (f32[200,128]{1,0:T(8,128)S(1)}, f32[200,128]{1,0:T(8,128)S(1)}, u32[]{:S(2)}, u32[]{:S(2)}) collective-permute-start(f32[200,128]{1,0:T(8,128)S(1)} %concatenate.7.in_ref), channel_id=1, source_target_pairs={{0,3},{1,2},{2,1},{3,0},{4,7},{5,6},{6,5},{7,4},{8,11},{9,10},{10,... | collective-permute-start | bytes 307208 | tf_op jit(solution)/shard_map/ppermute | solution.py:512
  6.5 5.1 %collective-permute-start.1 = (f32[200,128]{1,0:T(8,128)S(1)}, f32[200,128]{1,0:T(8,128)S(1)}, u32[]{:S(2)}, u32[]{:S(2)}) collective-permute-start(f32[200,128]{1,0:T(8,128)S(1)} %concatenate.7.in_ref), channel_id=1, source_target_pairs={{0,2},{1,3},{2,0},{3,1},{4,6},{5,7},{6,4},{7,5},{8,10},{9,11},{10,... | collective-permute-start | bytes 307208 | tf_op jit(solution)/shard_map/ppermute | solution.py:512
  7.0 4.9 %collective-permute-start = (f32[200,128]{1,0:T(8,128)S(1)}, f32[200,128]{1,0:T(8,128)S(1)}, u32[]{:S(2)}, u32[]{:S(2)}) collective-permute-start(f32[200,128]{1,0:T(8,128)S(1)} %concatenate.7.in_ref), channel_id=1, source_target_pairs={{0,1},{1,0},{2,3},{3,2},{4,5},{5,4},{6,7},{7,6},{8,9},{9,8},{10,11... | collective-permute-start | bytes 307208 | tf_op jit(solution)/shard_map/ppermute | solution.py:512
  7.1 5.6 %collective-permute-start.3 = (f32[200,128]{1,0:T(8,128)S(1)}, f32[200,128]{1,0:T(8,128)S(1)}, u32[]{:S(2)}, u32[]{:S(2)}) collective-permute-start(f32[200,128]{1,0:T(8,128)S(1)} %concatenate.7.in_ref), channel_id=1, source_target_pairs={{0,4},{4,0},{8,12},{12,8},{16,20},{20,16},{24,28},{28,24},{1,5},{5... | collective-permute-start | bytes 307208 | tf_op jit(solution)/shard_map/ppermute | solution.py:512
  9.8 3.0 %collective-permute-start.6 = (f32[200,128]{1,0:T(8,128)S(1)}, f32[200,128]{1,0:T(8,128)S(1)}, u32[]{:S(2)}, u32[]{:S(2)}) collective-permute-start(f32[200,128]{1,0:T(8,128)S(1)} %collective-permute-done.2.refs_3_), channel_id=1, source_target_pairs={{0,4},{4,0},{8,12},{12,8},{16,20},{20,16},{24,28},{28,24},{1,5},{5... | collective-permute-start | bytes 307208 | tf_op jit(solution)/shard_map/ppermute | solution.py:512
  11.6 1.3 %collective-permute-start.5 = (f32[200,128]{1,0:T(8,128)S(1)}, f32[200,128]{1,0:T(8,128)S(1)}, u32[]{:S(2)}, u32[]{:S(2)}) collective-permute-start(f32[200,128]{1,0:T(8,128)S(1)} %collective-permute-done.1.refs_2_), channel_id=1, source_target_pairs={{0,4},{4,0},{8,12},{12,8},{16,20},{20,16},{24,28},{28,24},{1,5},{5... | collective-permute-start | bytes 307208 | tf_op jit(solution)/shard_map/ppermute | solution.py:512
  11.9 1.3 %collective-permute-start.4 = (f32[200,128]{1,0:T(8,128)S(1)}, f32[200,128]{1,0:T(8,128)S(1)}, u32[]{:S(2)}, u32[]{:S(2)}) collective-permute-start(f32[200,128]{1,0:T(8,128)S(1)} %collective-permute-done.refs_1_), channel_id=1, source_target_pairs={{0,4},{4,0},{8,12},{12,8},{16,20},{20,16},{24,28},{28,24},{1,5},{5... | collective-permute-start | bytes 307208 | tf_op jit(solution)/shard_map/ppermute | solution.py:512
  26.0 11.2 %copy-start.1 = (s32[1,8]{1,0:T(1,128)S(1)}, s32[1,8]{1,0:T(1,128)}, u32[]{:S(2)}) copy-start(s32[1,8]{1,0:T(1,128)} %refs_0_.1) | copy-start | bytes 100
  26.1 6.6 %collective-permute-start.9 = (bf16[4,64,128]{2,1,0:T(8,128)(2,1)S(1)}, bf16[4,64,128]{2,1,0:T(8,128)(2,1)S(1)}, u32[]{:S(2)}, u32[]{:S(2)}) collective-permute-start(bf16[4,64,128]{2,1,0:T(8,128)(2,1)S(1)} %wire.1.refs_1_), channel_id=1, source_target_pairs={{0,24},{4,28},{8,16},{12,20},{16,8},{20,12},{24,0},{28,4},{1,25},{... | collective-permute-start | bytes 196616 | tf_op jit(solution)/shard_map/ppermute | solution.py:512
  29.8 6.0 %collective-permute-start.8 = (bf16[4,64,128]{2,1,0:T(8,128)(2,1)S(1)}, bf16[4,64,128]{2,1,0:T(8,128)(2,1)S(1)}, u32[]{:S(2)}, u32[]{:S(2)}) collective-permute-start(bf16[4,64,128]{2,1,0:T(8,128)(2,1)S(1)} %wire.1.refs_1_), channel_id=1, source_target_pairs={{0,16},{4,20},{8,24},{12,28},{16,0},{20,4},{24,8},{28,12},{1,17},{... | collective-permute-start | bytes 196616 | tf_op jit(solution)/shard_map/ppermute | solution.py:512
  29.8 6.0 %collective-permute-start.7 = (bf16[4,64,128]{2,1,0:T(8,128)(2,1)S(1)}, bf16[4,64,128]{2,1,0:T(8,128)(2,1)S(1)}, u32[]{:S(2)}, u32[]{:S(2)}) collective-permute-start(bf16[4,64,128]{2,1,0:T(8,128)(2,1)S(1)} %wire.1.refs_1_), channel_id=1, source_target_pairs={{0,8},{4,12},{8,0},{12,4},{16,24},{20,28},{24,16},{28,20},{1,9},{5... | collective-permute-start | bytes 196616 | tf_op jit(solution)/shard_map/ppermute | solution.py:512
  30.5 5.8 %collective-permute-start.10 = (bf16[4,64,128]{2,1,0:T(8,128)(2,1)S(1)}, bf16[4,64,128]{2,1,0:T(8,128)(2,1)S(1)}, u32[]{:S(2)}, u32[]{:S(2)}) collective-permute-start(bf16[4,64,128]{2,1,0:T(8,128)(2,1)S(1)} %wire.1.refs_1_), channel_id=1, source_target_pairs={{0,4},{4,0},{8,12},{12,8},{16,20},{20,16},{24,28},{28,24},{1,5},{5... | collective-permute-start | bytes 196616 | tf_op jit(solution)/shard_map/ppermute | solution.py:512
  32.7 3.7 %collective-permute-start.13 = (bf16[4,64,128]{2,1,0:T(8,128)(2,1)S(1)}, bf16[4,64,128]{2,1,0:T(8,128)(2,1)S(1)}, u32[]{:S(2)}, u32[]{:S(2)}) collective-permute-start(bf16[4,64,128]{2,1,0:T(8,128)(2,1)S(1)} %collective-permute-done.9.refs_4_), channel_id=1, source_target_pairs={{0,4},{4,0},{8,12},{12,8},{16,20},{20,16},{24,28},{28,24},{1,5},{5... | collective-permute-start | bytes 196616 | tf_op jit(solution)/shard_map/ppermute | solution.py:512
  35.8 1.3 %collective-permute-start.12 = (bf16[4,64,128]{2,1,0:T(8,128)(2,1)S(1)}, bf16[4,64,128]{2,1,0:T(8,128)(2,1)S(1)}, u32[]{:S(2)}, u32[]{:S(2)}) collective-permute-start(bf16[4,64,128]{2,1,0:T(8,128)(2,1)S(1)} %collective-permute-done.8.refs_3_), channel_id=1, source_target_pairs={{0,4},{4,0},{8,12},{12,8},{16,20},{20,16},{24,28},{28,24},{1,5},{5... | collective-permute-start | bytes 196616 | tf_op jit(solution)/shard_map/ppermute | solution.py:512
  35.8 1.4 %collective-permute-start.11 = (bf16[4,64,128]{2,1,0:T(8,128)(2,1)S(1)}, bf16[4,64,128]{2,1,0:T(8,128)(2,1)S(1)}, u32[]{:S(2)}, u32[]{:S(2)}) collective-permute-start(bf16[4,64,128]{2,1,0:T(8,128)(2,1)S(1)} %collective-permute-done.7.refs_2_), channel_id=1, source_target_pairs={{0,4},{4,0},{8,12},{12,8},{16,20},{20,16},{24,28},{28,24},{1,5},{5... | collective-permute-start | bytes 196616 | tf_op jit(solution)/shard_map/ppermute | solution.py:512

commit v3 on v2

--- a/solution.py
+++ b/solution.py
@@ -50,11 +50,10 @@
     return out[:, :128], out[:, 128:]
 
 
-def pair_inverse(mr, mi, beside):
+def panels(mr, mi):
     lane = lax.broadcasted_iota(jnp.int32, (8, 128), 1)
     sub = lax.broadcasted_iota(jnp.int32, (8, 128), 0)
     col = lane & 63
-    mr, mi = list(mr), list(mi)
     for t in range(8):
         near = (t + 1) % 8
         far = [(t + d) % 8 for d in range(2, 8)]
@@ -65,21 +64,24 @@
         ci = [column(mi[near], 8 * t + j, lane) for j in range(8)]
         rr = jnp.where(inside, jnp.where(col == sub + 8 * t, 1.0, 0.0), mr[t])
         ri = jnp.where(inside, 0.0, mi[t])
+        vr, vi = jnp.ones((8, 128), f32), jnp.zeros((8, 128), f32)
         for k in range(8):
             at = sub == k
             pr, pi = row(xr[k], k), row(xi[k], k)
             q = 1.0 / (pr * pr + pi * pi)
-            er, ei = jnp.where(at, -1.0, xr[k]), jnp.where(at, 0.0, xi[k])
+            er, ei = jnp.where(at, 0.0, xr[k]), jnp.where(at, 0.0, xi[k])
+            fr, fi = er * pr + ei * pi, ei * pr - er * pi
+            vr, vi = jnp.where(at, pr * q, vr), jnp.where(at, -(pi * q), vi)
 
             def step(yr, yi):
                 ar, ai = row(yr, k), row(yi, k)
-                ur, ui = ar * pr + ai * pi, ai * pr - ar * pi
-                wr, wi = er * ur - ei * ui, er * ui + ei * ur
-                return jnp.where(at, 0.0, yr) - wr * q, jnp.where(at, 0.0, yi) - wi * q
+                wr, wi = fr * ar - fi * ai, fr * ai + fi * ar
+                return yr - wr * q, yi - wi * q
 
             for j in range(k + 1, 8):
                 xr[j], xi[j] = step(xr[j], xi[j])
             rr, ri = step(rr, ri)
+        rr, ri = rr * vr - ri * vi, rr * vi + ri * vr
         lines = [(row(rr, j), row(ri, j)) for j in range(8)]
         more_r = added([cr[j] * lines[j][0] - ci[j] * lines[j][1] for j in range(8)])
         more_i = added([cr[j] * lines[j][1] + ci[j] * lines[j][0] for j in range(8)])
@@ -90,21 +92,23 @@
             mr[s] = jnp.where(inside, 0.0, mr[s]) - out_r[8 * n : 8 * n + 8]
             mi[s] = jnp.where(inside, 0.0, mi[s]) - out_i[8 * n : 8 * n + 8]
         mr[t], mi[t] = rr, ri
+        yield
+
+
+def slabs(x):
+    return [x[8 * s : 8 * s + 8] for s in range(8)]
+
+
+def invert_pairs(pairs, beside=()):
+    beside = iter(beside)
+    held = [(slabs(zr), slabs(zi)) for zr, zi in pairs]
+    for _ in zip(*[panels(mr, mi) for mr, mi in held]):
         work = next(beside, None)
         if work is not None:
             work()
     for work in beside:
         work()
-    return mr, mi
-
-
-def slabs(x):
-    return [x[8 * s : 8 * s + 8] for s in range(8)]
-
-
-def invert_pair(zr, zi, beside=()):
-    mr, mi = pair_inverse(slabs(zr), slabs(zi), iter(beside))
-    return jnp.concatenate(mr, 0), jnp.concatenate(mi, 0)
+    return [(jnp.concatenate(mr, 0), jnp.concatenate(mi, 0)) for mr, mi in held]
 
 
 def low_lanes(x):
@@ -288,26 +292,24 @@
         flat_im = jnp.where(keep, swapped(one), two)
         turned = jnp.concatenate([one, two], 0).T
         turned_re, turned_im = turned[:64], -turned[64:]
-        high, low = right_factor(
-            jnp.where(keep, flat_re, turned_re), jnp.where(keep, flat_im, turned_im)
-        )
+        y = jnp.where(keep, flat_re, turned_re), jnp.where(keep, flat_im, turned_im)
+        y_adjoint = jnp.where(keep, turned_re, flat_re), jnp.where(keep, turned_im, flat_im)
+        high, low = right_factor(*y)
         yright_ref[i - 1, 0] = high
         yright_ref[i - 1, 1] = low
-        yleft_ref[i - 1] = left_factor(
-            jnp.where(keep, turned_re, flat_re), jnp.where(keep, turned_im, flat_im)
-        )
-        return carry
+        yleft_ref[i - 1] = left_factor(*y_adjoint)
+        return y, y_adjoint
 
     def long_wire():
         lax.fori_loop(0, half, prepare_block, 0)
-        lax.fori_loop(1, half + 1, prepare_link, 0)
+        lax.fori_loop(1, half + 1, lambda i, carry: prepare_link(i, carry) and carry, 0)
 
         s_ref[...] = jnp.zeros_like(s_ref)
 
         def inward(i, carry):
             fr = ar_ref[i] - s_ref[0]
             fi = ai_ref[i] - s_ref[1]
-            gr, gi = invert_pair(fr, fi)
+            ((gr, gi),) = invert_pairs([(fr, fi)])
             g_ref[i, 0] = gr
             g_ref[i, 1] = gi
 
@@ -346,84 +348,142 @@
 
         lax.fori_loop(0, half - 1, outward, 0)
 
-    def short_wire():
-        last = half - 2
-        g, t, k = [None] * half, [None] * half, [None] * half
-        base, left, right = [None] * half, [None] * half, [None] * half
-
-        def do_block(i):
-            return lambda: prepare_block(i, 0)
-
-        def do_link(i):
-            return lambda: prepare_link(i, 0)
-
-        def do_k(i):
+    def wire_of_eight():
+        v = {}
+
+        def plus(x, y):
+            return x[0] + y[0], x[1] + y[1]
+
+        def minus(x, y):
+            return x[0] - y[0], x[1] - y[1]
+
+        def block(i):
+            return ar_ref[i], ai_ref[i]
+
+        def by_y(x, i):
+            return times_right(*x, yright_ref[i - 1, 0], yright_ref[i - 1, 1])
+
+        def adjoint_y_by(i, x):
+            return times_left(yleft_ref[i - 1], *x)
+
+        def do(step, *args):
+            return lambda: step(*args)
+
+        def link_two():
+            y, y_adjoint = prepare_link(2, 0)
+            v["y2_left"] = left_factor(*y)
+            v["y2_adjoint_right"] = right_factor(*y_adjoint)
+
+        def hold(name, product, *names):
             def run():
-                k[i] = times_left(yleft_ref[i], *g[i])
-                high, low = right_factor(*k[i])
-                k_ref[i, 0] = high
-                k_ref[i, 1] = low
-                if i == last:
-                    base[i], left[i], right[i] = g[i], t[i], k[i]
+                v[name] = product(*[v[x] for x in names])
 
             return run
 
-        def do_outer(i):
-            def one():
-                base[i] = times_left(t_ref[i], *base[i + 1])
-
-            def two():
-                more = times_right(*base[i], k_ref[i, 0], k_ref[i, 1])
-                base[i] = (g[i][0] + more[0], g[i][1] + more[1])
-
-            def three():
-                left[i] = times_left(t_ref[i], *left[i + 1])
-                t_ref[i] = left_factor(*left[i])
-
-            def four():
-                right[i] = times_right(*right[i + 1], k_ref[i, 0], k_ref[i, 1])
-                high, low = right_factor(*right[i])
-                k_ref[i, 0] = high
-                k_ref[i, 1] = low
-
-            return [one, two, three, four]
-
-        beside = [[] for _ in range(half + 1)]
-        beside[0] = [do_link(1), do_block(1)]
-        for i in range(2, half):
-            beside[0] += [do_block(i), do_link(i)]
-        beside[0] += [do_link(half)]
-        for i in range(half - 1):
-            beside[i + 1] += [do_k(i)]
-        for n, i in enumerate(range(last - 1, -1, -1)):
-            beside[min(half - 1 + n, half)] += do_outer(i)
+        def left_form(x):
+            return left_factor(*x)
+
+        def right_form(x):
+            return right_factor(*x)
+
+        def left_times(left, x):
+            return times_left(left, *x)
+
+        def times_right_form(x, right):
+            return times_right(*x, *right)
 
         prepare_block(0, 0)
-        sr = si = None
-        for i in range(half + 1):
-            if i == 0:
-                fr, fi = ar_ref[0], ai_ref[0]
-            elif i < half:
-                fr, fi = ar_ref[i] - sr, ai_ref[i] - si
-            else:
-                fr, fi = fr - swapped(sr), fi - swapped(si)
-            zr, zi = invert_pair(fr, fi, beside[i])
-            if i < half:
-                g[i] = (zr, zi)
-                t[i] = times_right(zr, zi, yright_ref[i, 0], yright_ref[i, 1])
-                sr, si = times_left(yleft_ref[i], *t[i])
-                if i < half - 1:
-                    t_ref[i] = left_factor(*t[i])
-        g_ref[half - 1, 0] = zr
-        g_ref[half - 1, 1] = zi
-        for i in range(half - 1):
-            more = times_right(zr, zi, k_ref[i, 0], k_ref[i, 1])
-            more = times_left(t_ref[i], *more)
-            g_ref[i, 0] = base[i][0] + more[0]
-            g_ref[i, 1] = base[i][1] + more[1]
-
-    if half in (3, 4, 5):
-        short_wire()
+        prepare_block(2, 0)
+        v["g0"], v["g2"] = invert_pairs(
+            [block(0), block(2)],
+            [
+                do(prepare_link, 1, 0),
+                link_two,
+                do(prepare_block, 1, 0),
+                do(prepare_link, 3, 0),
+                do(prepare_block, 3, 0),
+                do(prepare_link, 4, 0),
+            ],
+        )
+        v["t0"] = by_y(v["g0"], 1)
+        v["p_"] = left_times(v["y2_left"], v["g2"])
+        first_one = minus(block(1), adjoint_y_by(1, v["t0"]))
+        first_one = minus(first_one, times_right_form(v["p_"], v["y2_adjoint_right"]))
+
+        def third():
+            v["q_"] = adjoint_y_by(3, v["g2"])
+
+        def fourth():
+            v["f3"] = minus(block(3), by_y(v["q_"], 3))
+
+        def w13():
+            v["w13"] = right_form(by_y(v["p_"], 3))
+
+        def w31():
+            v["w31"] = left_form(times_right_form(v["q_"], v["y2_adjoint_right"]))
+
+        def k0():
+            v["k0"] = right_form(adjoint_y_by(1, v["g0"]))
+
+        def q():
+            v["q"] = by_y(v["g2"], 3)
+
+        def p():
+            v["p"] = left_form(times_right_form(v["g2"], v["y2_adjoint_right"]))
+
+        def forms():
+            v["t0_left"] = left_form(v["t0"])
+            v["p_right"] = right_form(v["p_"])
+
+        (v["g1"],) = invert_pairs([first_one], [third, w13, w31, fourth, k0, q, p, forms])
+        v["m"] = times_right_form(v["g1"], v["w13"])
+        f3 = minus(v["f3"], left_times(v["w31"], v["m"]))
+
+        def base_zero():
+            v["base0"] = plus(v["g0"], times_right_form(v["t0_g1"], v["k0"]))
+
+        def base_two():
+            v["base2"] = plus(v["g2"], times_right_form(v["p_g1"], v["p_right"]))
+
+        def left_two():
+            v["left2"] = left_form(plus(left_times(v["p"], v["m"]), v["q"]))
+
+        def right_two():
+            v["right2"] = right_form(plus(times_right_form(v["n"], v["p_right"]), v["q_"]))
+
+        def left_zero():
+            v["left0"] = left_form(left_times(v["t0_left"], v["m"]))
+
+        def right_zero():
+            v["right0"] = right_form(times_right_form(v["n"], v["k0"]))
+
+        def ends():
+            v["left1"] = left_form(v["m"])
+            v["right1"] = right_form(v["n"])
+
+        (g3,) = invert_pairs(
+            [f3],
+            [
+                hold("n", left_times, "w31", "g1"),
+                hold("t0_g1", left_times, "t0_left", "g1"),
+                hold("p_g1", left_times, "p", "g1"),
+                base_zero,
+                base_two,
+                left_two,
+                right_two,
+                ends,
+            ],
+        )
+        across = adjoint_y_by(4, by_y(g3, 4))
+        middle = minus(f3, (swapped(across[0]), swapped(across[1])))
+        (g_middle,) = invert_pairs([middle], [left_zero, right_zero])
+        g_ref[3, 0], g_ref[3, 1] = g_middle
+        for i, base in ((0, "base0"), (1, "g1"), (2, "base2")):
+            more = times_right_form(g_middle, v["right" + str(i)])
+            g_ref[i, 0], g_ref[i, 1] = plus(v[base], left_times(v["left" + str(i)], more))
+
+    if half == 4:
+        wire_of_eight()
     else:
         long_wire()
 

time: 39.3 us -> 37.1 us (0.944)
  Pallas kernels: 14.7 us -> 12.6 us
    pallas_call x1, Pallas kernels: 12.9 us -> 10.7 us  [wire(): pl.pallas_call(kernel, out_shape=jax.ShapeDtypeStruct((4, 64, 128), bf16)...]
where the time goes in v3:
time: 37.1 us; the launch traced here: 36.9 us
  Pallas kernels  12.6 us (34%)
  waiting for transfers between devices  11.3 us (30%)
  starting transfers between devices  9.72 us (26%)
  between operations  1.45 us (4%)
  other arithmetic  1.12 us (3%)
  local copies, waits for them, and re-layouts  0.74 us (2%)
    ppermute x14, waiting for transfers between devices, flipped_to(): return lax.ppermute(x, axis, [(i, i ^ mask) for i in range(count)])  11.3 us
    pallas_call x1, Pallas kernels, wire(): pl.pallas_call(kernel, out_shape=jax.ShapeDtypeStruct((4, 64, 128), bf16)...  10.7 us
    ppermute x14, starting transfers between devices, flipped_to(): return lax.ppermute(x, axis, [(i, i ^ mask) for i in range(count)])  9.72 us
    pallas_call x1, Pallas kernels, sum_shifts(): pl.pallas_call(kernel, out_shape=jax.ShapeDtypeStruct(screened.shape[1:],...  1.85 us
    select_n x1, other arithmetic, body(): one = jnp.where(first, hams[0], hams[2])  0.89 us
  transfers between devices with their start and end apart: 14, of which 9 were waited for; matrix products, arithmetic and copies ran while one was open for 0% of the time, Pallas kernels for 0%

profile of v3, /device:TPU:0, one launch (start us, length us, event | category | flops | bytes accessed | tf_op | source)
XLA Modules:
  0.0 36.9 jit_solution(979701396461494501)
XLA Ops:
  0.0 0.0 copy-start
  0.7 0.9 %select_bitcast_fusion.1 = (f32[64,128]{1,0:T(8,128)S(1)}, f32[64,128]{1,0:T(8,128)S(1)}, f32[64,128]{1,0:T(8,128)S(1)}, f32[64,128]{1,0:T(8,128)S(1)}) fusion(f32[1,4,64,128]{3,2,1,0:T(8,128)} %param.9, pred[]{:T(512)S(6)} %eq.5, f32[1,4,64,128]{3,2,1,0:T(8,128)} %param.10), kind=kLoop, calls=%fused_computation.4 | loop fusion | flops 32768 | bytes 393217 | tf_op jit(solution)/shard_map/jit(_where)/select_n | solution.py:580
  1.6 0.1 slice_select_fusion.1
  1.7 0.1 slice_select_fusion
  1.8 0.1 pad_maximum_fusion
  1.9 0.7 %concatenate.7.in_ref = f32[200,128]{1,0:T(8,128)S(1)} concatenate(f32[64,128]{1,0:T(8,128)S(1)} %get-tuple-element.9, f32[64,128]{1,0:T(8,128)S(1)} %get-tuple-element.10, f32[64,128]{1,0:T(8,128)S(1)} %pad_maximum_fusion, f32[2,128]{1,0:T(2,128)} %bitcast.14, f32[2,128]{1,0:T(2,128)} %bitcast.15, f32[4,128]{1,0:T(4,128)S(1)} %broadcast_in_dim.14), dimensions={0} | concatenate | bytes 204800 | tf_op jit(solution)/shard_map/concatenate | solution.py:586
  2.6 3.9 %collective-permute-start.2 = (f32[200,128]{1,0:T(8,128)S(1)}, f32[200,128]{1,0:T(8,128)S(1)}, u32[]{:S(2)}, u32[]{:S(2)}) collective-permute-start(f32[200,128]{1,0:T(8,128)S(1)} %concatenate.7.in_ref), channel_id=1, source_target_pairs={{0,3},{1,2},{2,1},{3,0},{4,7},{5,6},{6,5},{7,4},{8,11},{9,10},{10,... | collective-permute-start | bytes 307208 | tf_op jit(solution)/shard_map/ppermute | solution.py:572
  6.5 0.5 %collective-permute-start.1 = (f32[200,128]{1,0:T(8,128)S(1)}, f32[200,128]{1,0:T(8,128)S(1)}, u32[]{:S(2)}, u32[]{:S(2)}) collective-permute-start(f32[200,128]{1,0:T(8,128)S(1)} %concatenate.7.in_ref), channel_id=1, source_target_pairs={{0,2},{1,3},{2,0},{3,1},{4,6},{5,7},{6,4},{7,5},{8,10},{9,11},{10,... | collective-permute-start | bytes 307208 | tf_op jit(solution)/shard_map/ppermute | solution.py:572
  7.0 0.1 collective-permute-start
  7.1 0.0 collective-permute-start.3
  7.1 2.7 %collective-permute-done.2.refs_3_ = f32[200,128]{1,0:T(8,128)S(1)} collective-permute-done((f32[200,128]{1,0:T(8,128)S(1)}, f32[200,128]{1,0:T(8,128)S(1)}, u32[]{:S(2)}, u32[]{:S(2)}) %collective-permute-start.2) | collective-permute-done | bytes 102432 | tf_op jit(solution)/shard_map/ppermute | solution.py:572
  9.8 0.0 collective-permute-start.6
  9.8 1.8 %collective-permute-done.1.refs_2_ = f32[200,128]{1,0:T(8,128)S(1)} collective-permute-done((f32[200,128]{1,0:T(8,128)S(1)}, f32[200,128]{1,0:T(8,128)S(1)}, u32[]{:S(2)}, u32[]{:S(2)}) %collective-permute-start.1) | collective-permute-done | bytes 102432 | tf_op jit(solution)/shard_map/ppermute | solution.py:572
  11.6 0.0 collective-permute-start.5
  11.6 0.3 collective-permute-done.refs_1_
  11.9 0.2 collective-permute-start.4
  12.8 0.0 collective-permute-done.3.refs_4_
  12.8 0.0 collective-permute-done.6.refs_7_
  12.8 0.1 collective-permute-done.5.refs_6_
  12.9 0.3 collective-permute-done.4.refs_5_
  13.2 10.7 %wire.1.refs_1_ = bf16[4,64,128]{2,1,0:T(8,128)(2,1)S(1)} custom-call(f32[200,128]{1,0:T(8,128)S(1)} %settle.1.refs_0_, f32[200,128]{1,0:T(8,128)S(1)} %collective-permute-done.refs_1_, f32[200,128]{1,0:T(8,128)S(1)} %collective-permute-done.1.refs_2_, f32[200,128]{1,0:T(8,128)S(1)} %collective-permute-done.2.refs_3_, ...), custom_call_target="tpu_custom_call" | custom-call | tf_op jit(solution)/shard_map/wire/pallas_call | solution.py:507
  23.9 0.0 copy-start.1
  23.9 3.8 %collective-permute-start.9 = (bf16[4,64,128]{2,1,0:T(8,128)(2,1)S(1)}, bf16[4,64,128]{2,1,0:T(8,128)(2,1)S(1)}, u32[]{:S(2)}, u32[]{:S(2)}) collective-permute-start(bf16[4,64,128]{2,1,0:T(8,128)(2,1)S(1)} %wire.1.refs_1_), channel_id=1, source_target_pairs={{0,24},{4,28},{8,16},{12,20},{16,8},{20,12},{24,0},{28,4},{1,25},{... | collective-permute-start | bytes 196616 | tf_op jit(solution)/shard_map/ppermute | solution.py:572
  27.7 0.0 collective-permute-start.8
  27.7 0.7 %collective-permute-start.7 = (bf16[4,64,128]{2,1,0:T(8,128)(2,1)S(1)}, bf16[4,64,128]{2,1,0:T(8,128)(2,1)S(1)}, u32[]{:S(2)}, u32[]{:S(2)}) collective-permute-start(bf16[4,64,128]{2,1,0:T(8,128)(2,1)S(1)} %wire.1.refs_1_), channel_id=1, source_target_pairs={{0,8},{4,12},{8,0},{12,4},{16,24},{20,28},{24,16},{28,20},{1,9},{5... | collective-permute-start | bytes 196616 | tf_op jit(solution)/shard_map/ppermute | solution.py:572
  28.4 0.0 collective-permute-start.10
  28.4 2.1 %collective-permute-done.9.refs_4_ = bf16[4,64,128]{2,1,0:T(8,128)(2,1)S(1)} collective-permute-done((bf16[4,64,128]{2,1,0:T(8,128)(2,1)S(1)}, bf16[4,64,128]{2,1,0:T(8,128)(2,1)S(1)}, u32[]{:S(2)}, u32[]{:S(2)}) %collective-permute-start.9) | collective-permute-done | bytes 65568 | tf_op jit(solution)/shard_map/ppermute | solution.py:572
  30.5 0.0 collective-permute-start.13
  30.5 3.1 %collective-permute-done.8.refs_3_ = bf16[4,64,128]{2,1,0:T(8,128)(2,1)S(1)} collective-permute-done((bf16[4,64,128]{2,1,0:T(8,128)(2,1)S(1)}, bf16[4,64,128]{2,1,0:T(8,128)(2,1)S(1)}, u32[]{:S(2)}, u32[]{:S(2)}) %collective-permute-start.8) | collective-permute-done | bytes 65568 | tf_op jit(solution)/shard_map/ppermute | solution.py:572
  33.7 0.0 collective-permute-start.12
  33.7 0.0 collective-permute-done.7.refs_2_
  33.7 0.5 %collective-permute-start.11 = (bf16[4,64,128]{2,1,0:T(8,128)(2,1)S(1)}, bf16[4,64,128]{2,1,0:T(8,128)(2,1)S(1)}, u32[]{:S(2)}, u32[]{:S(2)}) collective-permute-start(bf16[4,64,128]{2,1,0:T(8,128)(2,1)S(1)} %collective-permute-done.7.refs_2_), channel_id=1, source_target_pairs={{0,4},{4,0},{8,12},{12,8},{16,20},{20,16},{24,28},{28,24},{1,5},{5... | collective-permute-start | bytes 196616 | tf_op jit(solution)/shard_map/ppermute | solution.py:572
  34.2 0.0 collective-permute-done.10.refs_5_
  34.2 0.0 collective-permute-done.13.refs_8_
  34.2 0.7 %collective-permute-done.12.refs_7_ = bf16[4,64,128]{2,1,0:T(8,128)(2,1)S(1)} collective-permute-done((bf16[4,64,128]{2,1,0:T(8,128)(2,1)S(1)}, bf16[4,64,128]{2,1,0:T(8,128)(2,1)S(1)}, u32[]{:S(2)}, u32[]{:S(2)}) %collective-permute-start.12) | collective-permute-done | bytes 65568 | tf_op jit(solution)/shard_map/ppermute | solution.py:572
  34.9 0.2 collective-permute-done.11.refs_6_
  35.1 0.0 copy-done
  35.1 0.0 copy-done.1
  35.1 1.9 %sum_shifts.1 = f32[4,64,128]{2,1,0:T(8,128)} custom-call(s32[1,8]{1,0:T(1,128)S(1)} %copy-done.1, bf16[4,64,128]{2,1,0:T(8,128)(2,1)S(1)} %wire.1.refs_1_, bf16[4,64,128]{2,1,0:T(8,128)(2,1)S(1)} %collective-permute-done.7.refs_2_, bf16[4,64,128]{2,1,0:T(8,128)(2,1)S(1)} %collective-permute-done.8.refs_3_, ...), custom_call_target="tpu_custom_call" | custom-call | tf_op jit(solution)/shard_map/sum_shifts/pallas_call | solution.py:559
  (2 shorter events, 0.0 us)
Async XLA Ops:
  0.0 35.1 %copy-start = (f32[8,1,4,64,128]{4,3,2,1,0:T(8,128)S(1)}, f32[8,1,4,64,128]{4,3,2,1,0:T(8,128)}, u32[]{:S(2)}) copy-start(f32[8,1,4,64,128]{4,3,2,1,0:T(8,128)} %param.13) | copy-start | bytes 3145732
  2.6 7.2 %collective-permute-start.2 = (f32[200,128]{1,0:T(8,128)S(1)}, f32[200,128]{1,0:T(8,128)S(1)}, u32[]{:S(2)}, u32[]{:S(2)}) collective-permute-start(f32[200,128]{1,0:T(8,128)S(1)} %concatenate.7.in_ref), channel_id=1, source_target_pairs={{0,3},{1,2},{2,1},{3,0},{4,7},{5,6},{6,5},{7,4},{8,11},{9,10},{10,... | collective-permute-start | bytes 307208 | tf_op jit(solution)/shard_map/ppermute | solution.py:572
  6.5 5.1 %collective-permute-start.1 = (f32[200,128]{1,0:T(8,128)S(1)}, f32[200,128]{1,0:T(8,128)S(1)}, u32[]{:S(2)}, u32[]{:S(2)}) collective-permute-start(f32[200,128]{1,0:T(8,128)S(1)} %concatenate.7.in_ref), channel_id=1, source_target_pairs={{0,2},{1,3},{2,0},{3,1},{4,6},{5,7},{6,4},{7,5},{8,10},{9,11},{10,... | collective-permute-start | bytes 307208 | tf_op jit(solution)/shard_map/ppermute | solution.py:572
  7.0 4.9 %collective-permute-start = (f32[200,128]{1,0:T(8,128)S(1)}, f32[200,128]{1,0:T(8,128)S(1)}, u32[]{:S(2)}, u32[]{:S(2)}) collective-permute-start(f32[200,128]{1,0:T(8,128)S(1)} %concatenate.7.in_ref), channel_id=1, source_target_pairs={{0,1},{1,0},{2,3},{3,2},{4,5},{5,4},{6,7},{7,6},{8,9},{9,8},{10,11... | collective-permute-start | bytes 307208 | tf_op jit(solution)/shard_map/ppermute | solution.py:572
  7.1 5.6 %collective-permute-start.3 = (f32[200,128]{1,0:T(8,128)S(1)}, f32[200,128]{1,0:T(8,128)S(1)}, u32[]{:S(2)}, u32[]{:S(2)}) collective-permute-start(f32[200,128]{1,0:T(8,128)S(1)} %concatenate.7.in_ref), channel_id=1, source_target_pairs={{0,4},{4,0},{8,12},{12,8},{16,20},{20,16},{24,28},{28,24},{1,5},{5... | collective-permute-start | bytes 307208 | tf_op jit(solution)/shard_map/ppermute | solution.py:572
  9.8 3.0 %collective-permute-start.6 = (f32[200,128]{1,0:T(8,128)S(1)}, f32[200,128]{1,0:T(8,128)S(1)}, u32[]{:S(2)}, u32[]{:S(2)}) collective-permute-start(f32[200,128]{1,0:T(8,128)S(1)} %collective-permute-done.2.refs_3_), channel_id=1, source_target_pairs={{0,4},{4,0},{8,12},{12,8},{16,20},{20,16},{24,28},{28,24},{1,5},{5... | collective-permute-start | bytes 307208 | tf_op jit(solution)/shard_map/ppermute | solution.py:572
  11.6 1.3 %collective-permute-start.5 = (f32[200,128]{1,0:T(8,128)S(1)}, f32[200,128]{1,0:T(8,128)S(1)}, u32[]{:S(2)}, u32[]{:S(2)}) collective-permute-start(f32[200,128]{1,0:T(8,128)S(1)} %collective-permute-done.1.refs_2_), channel_id=1, source_target_pairs={{0,4},{4,0},{8,12},{12,8},{16,20},{20,16},{24,28},{28,24},{1,5},{5... | collective-permute-start | bytes 307208 | tf_op jit(solution)/shard_map/ppermute | solution.py:572
  11.9 1.3 %collective-permute-start.4 = (f32[200,128]{1,0:T(8,128)S(1)}, f32[200,128]{1,0:T(8,128)S(1)}, u32[]{:S(2)}, u32[]{:S(2)}) collective-permute-start(f32[200,128]{1,0:T(8,128)S(1)} %collective-permute-done.refs_1_), channel_id=1, source_target_pairs={{0,4},{4,0},{8,12},{12,8},{16,20},{20,16},{24,28},{28,24},{1,5},{5... | collective-permute-start | bytes 307208 | tf_op jit(solution)/shard_map/ppermute | solution.py:572
  23.9 11.2 %copy-start.1 = (s32[1,8]{1,0:T(1,128)S(1)}, s32[1,8]{1,0:T(1,128)}, u32[]{:S(2)}) copy-start(s32[1,8]{1,0:T(1,128)} %refs_0_.1) | copy-start | bytes 100
  23.9 6.6 %collective-permute-start.9 = (bf16[4,64,128]{2,1,0:T(8,128)(2,1)S(1)}, bf16[4,64,128]{2,1,0:T(8,128)(2,1)S(1)}, u32[]{:S(2)}, u32[]{:S(2)}) collective-permute-start(bf16[4,64,128]{2,1,0:T(8,128)(2,1)S(1)} %wire.1.refs_1_), channel_id=1, source_target_pairs={{0,24},{4,28},{8,16},{12,20},{16,8},{20,12},{24,0},{28,4},{1,25},{... | collective-permute-start | bytes 196616 | tf_op jit(solution)/shard_map/ppermute | solution.py:572
  27.7 6.0 %collective-permute-start.8 = (bf16[4,64,128]{2,1,0:T(8,128)(2,1)S(1)}, bf16[4,64,128]{2,1,0:T(8,128)(2,1)S(1)}, u32[]{:S(2)}, u32[]{:S(2)}) collective-permute-start(bf16[4,64,128]{2,1,0:T(8,128)(2,1)S(1)} %wire.1.refs_1_), channel_id=1, source_target_pairs={{0,16},{4,20},{8,24},{12,28},{16,0},{20,4},{24,8},{28,12},{1,17},{... | collective-permute-start | bytes 196616 | tf_op jit(solution)/shard_map/ppermute | solution.py:572
  27.7 6.0 %collective-permute-start.7 = (bf16[4,64,128]{2,1,0:T(8,128)(2,1)S(1)}, bf16[4,64,128]{2,1,0:T(8,128)(2,1)S(1)}, u32[]{:S(2)}, u32[]{:S(2)}) collective-permute-start(bf16[4,64,128]{2,1,0:T(8,128)(2,1)S(1)} %wire.1.refs_1_), channel_id=1, source_target_pairs={{0,8},{4,12},{8,0},{12,4},{16,24},{20,28},{24,16},{28,20},{1,9},{5... | collective-permute-start | bytes 196616 | tf_op jit(solution)/shard_map/ppermute | solution.py:572
  28.4 5.8 %collective-permute-start.10 = (bf16[4,64,128]{2,1,0:T(8,128)(2,1)S(1)}, bf16[4,64,128]{2,1,0:T(8,128)(2,1)S(1)}, u32[]{:S(2)}, u32[]{:S(2)}) collective-permute-start(bf16[4,64,128]{2,1,0:T(8,128)(2,1)S(1)} %wire.1.refs_1_), channel_id=1, source_target_pairs={{0,4},{4,0},{8,12},{12,8},{16,20},{20,16},{24,28},{28,24},{1,5},{5... | collective-permute-start | bytes 196616 | tf_op jit(solution)/shard_map/ppermute | solution.py:572
  30.5 3.7 %collective-permute-start.13 = (bf16[4,64,128]{2,1,0:T(8,128)(2,1)S(1)}, bf16[4,64,128]{2,1,0:T(8,128)(2,1)S(1)}, u32[]{:S(2)}, u32[]{:S(2)}) collective-permute-start(bf16[4,64,128]{2,1,0:T(8,128)(2,1)S(1)} %collective-permute-done.9.refs_4_), channel_id=1, source_target_pairs={{0,4},{4,0},{8,12},{12,8},{16,20},{20,16},{24,28},{28,24},{1,5},{5... | collective-permute-start | bytes 196616 | tf_op jit(solution)/shard_map/ppermute | solution.py:572
  33.7 1.3 %collective-permute-start.12 = (bf16[4,64,128]{2,1,0:T(8,128)(2,1)S(1)}, bf16[4,64,128]{2,1,0:T(8,128)(2,1)S(1)}, u32[]{:S(2)}, u32[]{:S(2)}) collective-permute-start(bf16[4,64,128]{2,1,0:T(8,128)(2,1)S(1)} %collective-permute-done.8.refs_3_), channel_id=1, source_target_pairs={{0,4},{4,0},{8,12},{12,8},{16,20},{20,16},{24,28},{28,24},{1,5},{5... | collective-permute-start | bytes 196616 | tf_op jit(solution)/shard_map/ppermute | solution.py:572
  33.7 1.4 %collective-permute-start.11 = (bf16[4,64,128]{2,1,0:T(8,128)(2,1)S(1)}, bf16[4,64,128]{2,1,0:T(8,128)(2,1)S(1)}, u32[]{:S(2)}, u32[]{:S(2)}) collective-permute-start(bf16[4,64,128]{2,1,0:T(8,128)(2,1)S(1)} %collective-permute-done.7.refs_2_), channel_id=1, source_target_pairs={{0,4},{4,0},{8,12},{12,8},{16,20},{20,16},{24,28},{28,24},{1,5},{5... | collective-permute-start | bytes 196616 | tf_op jit(solution)/shard_map/ppermute | solution.py:572

commit v4 on v3

--- a/solution.py
+++ b/solution.py
@@ -180,41 +180,10 @@
     return pltpu.roll(x, 64, 1)
 
 
-def packed_pair(one, two):
-    lower = lax.broadcasted_iota(jnp.int32, (64, 128), 0) >= (
-        lax.broadcasted_iota(jnp.int32, (64, 128), 1) & 63
-    )
-    left = jnp.where(lower, one, swapped(one))
-    right = jnp.where(lower, swapped(two), two)
-    return jnp.where(low_lanes(one), left, right)
-
-
-def pack_kernel(
-    counts_ref, shifts_ref, rates_ref, hams_ref, links_ref, out_ref
-):
-    first = 2 * (lax.axis_index("energy") & 1)
-    out_ref[0:64] = links_ref[first]
-    out_ref[64:128] = links_ref[first + 1]
-    out_ref[128:192] = packed_pair(hams_ref[first], hams_ref[first + 1])
-    out_ref[192:194] = shifts_ref[...]
-    out_ref[194:196] = rates_ref[...]
-    out_ref[196:200] = jnp.broadcast_to(counts_ref[...].astype(f32), (4, 128))
-
-
-def pack(*arrays):
-    return pl.pallas_call(
-        pack_kernel,
-        out_shape=jax.ShapeDtypeStruct((200, 128), f32),
-        in_specs=[VMEM] * len(arrays),
-        out_specs=VMEM,
-        name="pack",
-    )(*arrays)
-
-
 def settle_kernel(energies_ref, in_ref, out_ref):
-    out_ref[0:192] = in_ref[0:192]
+    out_ref[0:200] = in_ref[0:200]
     last = lax.broadcasted_iota(jnp.int32, (8, 128), 0) >= 6
-    out_ref[192:200] = jnp.where(last, energies_ref[0], in_ref[192:200])
+    out_ref[200:208] = jnp.where(last, energies_ref[0], in_ref[200:208])
 
 
 def settle(energies, piece):
@@ -232,7 +201,7 @@
     own = refs[:segs]
     other = refs[segs : 2 * segs]
     out_ref = refs[2 * segs]
-    (u_ref, h_ref, m_ref, at_ref, ar_ref, ai_ref, yright_ref, yleft_ref, g_ref, s_ref, k_ref, t_ref) = (
+    (u_ref, h_ref, d_ref, m_ref, at_ref, ar_ref, ai_ref, yright_ref, yleft_ref, g_ref, s_ref, k_ref, t_ref) = (
         refs[2 * segs + 1 :]
     )
     blocks = 2 * segs
@@ -245,8 +214,9 @@
             u_ref[4 * seg + 2 * c] = ref[0:64]
             u_ref[4 * seg + 2 * c + 1] = ref[64:128]
             h_ref[2 * seg + c] = ref[128:192]
-        m_ref[seg] = own[k][192:200]
-    energy = own[0][198:199]
+            d_ref[2 * seg + c] = ref[192:200]
+        m_ref[seg] = own[k][200:208]
+    energy = own[0][206:207]
 
     start = jnp.int32(0)
     first, used = jnp.int32(0), jnp.int32(0)
@@ -266,13 +236,16 @@
         one, two = at_ref[i], at_ref[blocks - 1 - i]
         odd_one, odd_two = one & 1, two & 1
         raw_one, raw_two = h_ref[one >> 1], h_ref[two >> 1]
-        one_low = pltpu.roll(raw_one, 64 * odd_one, 1)
-        two_low = pltpu.roll(raw_two, 64 * odd_two, 1)
-        two_high = pltpu.roll(raw_two, 64 * (1 - odd_two), 1)
-        packed = jnp.where(keep, one_low, two_high)
-        flipped = jnp.concatenate([one_low, two_low], 0).T[:64]
-        real = jnp.where(rows >= cols, packed, flipped)
-        imag = jnp.where(rows < cols, packed, jnp.where(rows > cols, -flipped, 0.0))
+        flat_re = jnp.where(keep, raw_one, swapped(raw_two))
+        flat_im = jnp.where(keep, swapped(raw_one), raw_two)
+        turned = jnp.concatenate([raw_one, raw_two], 0).T
+        odd = jnp.where(keep, odd_one, odd_two)
+        held = ((rows >= cols).astype(jnp.int32) ^ odd) > 0
+        line = jnp.where(keep[:8], d_ref[one >> 1], swapped(d_ref[two >> 1]))
+        on = rows == cols
+        real = jnp.where(held, flat_re, turned[:64])
+        real = jnp.where(on & (odd > 0), jnp.concatenate([line] * 8, 0), real)
+        imag = jnp.where(on, 0.0, jnp.where(held, flat_im, -turned[64:]))
         extra = []
         for base in (0, 2):
             line_one = m_ref[one >> 2, pl.ds(base + ((one >> 1) & 1), 1), :]
@@ -281,7 +254,6 @@
             line_two = pltpu.roll(jnp.broadcast_to(line_two, (8, 128)), 64 * (1 - odd_two), 1)
             line = jnp.where(keep[:8], line_one, line_two)
             extra.append(jnp.broadcast_to(line[:1], (64, 128)))
-        on = rows == cols
         ar_ref[i] = jnp.where(on, energy - extra[0], 0.0) - real
         ai_ref[i] = jnp.where(on, broadening + extra[1], 0.0) - imag
         return carry
@@ -512,6 +484,7 @@
         scratch_shapes=[
             pltpu.VMEM((4 * segs, 64, 128), f32),
             pltpu.VMEM((2 * segs, 64, 128), f32),
+            pltpu.VMEM((2 * segs, 8, 128), f32),
             pltpu.VMEM((segs, 8, 128), f32),
             pltpu.SMEM((2 * segs + 4,), jnp.int32),
             pltpu.VMEM((half + 1, 64, 128), f32),
@@ -528,43 +501,91 @@
     )(*own, *other)
 
 
-def sum_kernel(chips, sources_ref, *refs):
-    own = refs[:chips]
-    other = refs[chips : 2 * chips]
-    screened_ref, out_ref, all_ref = refs[2 * chips :]
-    chip, core = lax.axis_index("energy") >> 1, lax.axis_index("energy") & 1
-    for k in range(chips):
-        place = jnp.bitwise_xor(chip, k) * cores
-        all_ref[place + core] = own[k][...]
-        all_ref[place + 1 - core] = other[k][...]
-    shifts = screened_ref.shape[0]
+def order_kernel(chips, sources_ref, screened_ref, *out_refs):
+    energy = lax.axis_index("energy")
+    for side, (plain_ref, other_ref) in enumerate((out_refs[:2], out_refs[2:])):
+        for k in range(chips):
+            wanted = ((energy >> 1) ^ k) * cores + ((energy & 1) ^ side)
+            place, found = jnp.int32(0), jnp.int32(0)
+            for j in range(screened_ref.shape[0]):
+                hit = (sources_ref[0, j] == wanted).astype(jnp.int32)
+                place, found = place + j * hit, found + hit
+            for slot in range(4):
+                weight = screened_ref[place, slot] * found.astype(f32)
+                plain_ref[k, slot] = weight
+                other_ref[k, slot] = swapped(weight)
+
+
+def order_weights(chips, sources, screened):
+    shape = jax.ShapeDtypeStruct((chips,) + screened.shape[1:], f32)
+
+    def kernel(*refs):
+        order_kernel(chips, *refs)
+
+    return pl.pallas_call(
+        kernel,
+        out_shape=[shape] * 4,
+        in_specs=[SMEM, VMEM],
+        out_specs=[VMEM] * 4,
+        compiler_params=pltpu.CompilerParams(vmem_limit_bytes=(4 + chips) * 2**20),
+        name="order_weights",
+    )(sources, screened)
+
+
+def sum_kernel(pieces, plain_ref, other_ref, *refs):
+    greens, rest = refs[:pieces], refs[pieces:]
     keep = low_lanes(jnp.zeros((64, 128), f32))
-    for slot in range(4):
+
+    def total(slot):
         direct = jnp.zeros((64, 128), f32)
         crossed = jnp.zeros((64, 128), f32)
-        for j in range(shifts):
-            green = all_ref[sources_ref[0, j], slot].astype(f32)
-            weight = screened_ref[j, slot]
-            direct = direct + green * weight
-            crossed = crossed + green * swapped(weight)
-        out_ref[slot] = jnp.where(keep, direct - swapped(direct), crossed + swapped(crossed))
-
-
-def sum_shifts(sources, own, other, screened):
-    chips = len(own)
-
+        for k in range(pieces):
+            green = greens[k][slot].astype(f32)
+            direct = direct + green * plain_ref[k, slot]
+            crossed = crossed + green * other_ref[k, slot]
+        return jnp.where(keep, direct - swapped(direct), crossed + swapped(crossed))
+
+    if len(rest) == 1:
+        for slot in range(4):
+            rest[0][slot] = total(slot)
+    else:
+        before_ref, out_ref, done_ref, sem = rest
+        copies = []
+        for slot in range(4):
+            done_ref[slot] = total(slot) + before_ref[slot]
+            copies.append(pltpu.make_async_copy(done_ref.at[slot], out_ref.at[slot], sem.at[slot]))
+            copies[-1].start()
+        for copy in copies:
+            copy.wait()
+
+
+def sum_near(greens, plain, other):
     def kernel(*refs):
-        sum_kernel(chips, *refs)
+        sum_kernel(len(greens), *refs)
 
     return pl.pallas_call(
         kernel,
-        out_shape=jax.ShapeDtypeStruct(screened.shape[1:], f32),
-        in_specs=[SMEM] + [VMEM] * (2 * chips + 1),
+        out_shape=jax.ShapeDtypeStruct(plain.shape[1:], f32),
+        in_specs=[VMEM] * (2 + len(greens)),
         out_specs=VMEM,
-        scratch_shapes=[pltpu.VMEM((cores * chips,) + screened.shape[1:], bf16)],
-        compiler_params=pltpu.CompilerParams(vmem_limit_bytes=(4 + 2 * chips) * 2**20),
-        name="sum_shifts",
-    )(sources, *own, *other, screened)
+        compiler_params=pltpu.CompilerParams(vmem_limit_bytes=(4 + len(greens)) * 2**20),
+        name="sum_near",
+    )(plain, other, *greens)
+
+
+def sum_far(greens, plain, other, before):
+    def kernel(*refs):
+        sum_kernel(len(greens), *refs)
+
+    return pl.pallas_call(
+        kernel,
+        out_shape=jax.ShapeDtypeStruct(plain.shape[1:], f32),
+        in_specs=[VMEM] * (3 + len(greens)),
+        out_specs=pl.BlockSpec(memory_space=pl.ANY),
+        scratch_shapes=[pltpu.VMEM(plain.shape[1:], f32), pltpu.SemaphoreType.DMA((4,))],
+        compiler_params=pltpu.CompilerParams(vmem_limit_bytes=(4 + len(greens)) * 2**20),
+        name="sum_far",
+    )(plain, other, *greens, before)
 
 
 def flipped_to(x, axis, mask):
@@ -579,20 +600,21 @@
     hams, links = h_blocks[0], couplings[0]
     one = jnp.where(first, hams[0], hams[2])
     two = jnp.where(first, hams[1], hams[3])
-    lower = jnp.arange(64)[:, None] >= jnp.arange(64)[None, :]
-    packed = jnp.concatenate(
-        [jnp.where(lower, one[:, :64], one[:, 64:]), jnp.where(lower, two[:, :64], two[:, 64:])], 1
-    )
-    piece = jnp.concatenate(
-        [
-            jnp.where(first, links[0], links[2]),
-            jnp.where(first, links[1], links[3]),
-            packed,
-            shift_real.reshape(2, 128),
-            shift_rate.reshape(2, 128),
-            jnp.broadcast_to(counts.astype(f32)[:, None], (4, 128)),
-        ],
-        0,
+    lower = jnp.arange(64)[:, None] >= jnp.arange(128)[None, :] % 64
+    group = jnp.arange(128)[None, :] % 64 // 8
+    line = sum(jnp.where(group == n, two[8 * n : 8 * n + 8], 0.0) for n in range(8))
+
+    def at_rows(x, start):
+        return jnp.pad(x, ((start, 208 - start - x.shape[0]), (0, 0)))
+
+    piece = (
+        at_rows(jnp.where(first, links[0], links[2]), 0)
+        + at_rows(jnp.where(first, links[1], links[3]), 64)
+        + at_rows(jnp.where(lower, one, two), 128)
+        + at_rows(line, 192)
+        + at_rows(shift_real.reshape(2, 128), 200)
+        + at_rows(shift_rate.reshape(2, 128), 202)
+        + at_rows(jnp.broadcast_to(counts.astype(f32)[:, None], (4, 128)), 204)
     )
     sent = [flipped_to(piece, "seg", k) for k in range(1, segs)]
     own = [settle(energies, piece)] + sent
@@ -600,7 +622,9 @@
     greens = wire(own, other)
     near = [greens] + [flipped_to(greens, "energy", cores * k) for k in range(1, chips)]
     far = [flipped_to(x, "energy", 1) for x in near]
-    return sum_shifts(sources, near, far, screened[:, 0])[None, None]
+    plain_near, other_near, plain_far, other_far = order_weights(chips, sources, screened[:, 0])
+    partial = sum_near(near, plain_near, other_near)
+    return sum_far(far, plain_far, other_far, partial)[None, None]
 
 
 def solution(mesh):

time: 37.1 us -> 36.4 us (0.981)
  starting transfers between devices: 9.72 us -> 8.98 us
  local copies, waits for them, and re-layouts: 0.74 us -> 0.09 us
  other arithmetic: 1.12 us -> 1.68 us
    add x0 -> x2, other arithmetic: none -> 0.8 us  [the longest x1 0.79 us: body(): at_rows(jnp.where(first, links[0], links[2]), 0)]
    ppermute x14, starting transfers between devices: 9.72 us -> 8.98 us  [flipped_to(): return lax.ppermute(x, axis, [(i, i ^ mask) for i in range(count)])]
    concatenate x1 -> x0, local copies, waits for them, and re-layouts: 0.73 us -> none  [body(): jnp.concatenate([jnp.where(first, links[0], links[2]), jnp.where(first, l...]
    pallas_call x1 -> x3, Pallas kernels: 1.85 us -> 1.9 us  [the longest x1 0.9 us: order_weights(): pl.pallas_call(kernel, out_shape=[shape] * 4, in_specs=[SMEM, VMEM], out_...]
  transfers between devices with their start and end apart: 14 -> 14, of which waited for: 9 -> 7; matrix products, arithmetic and copies ran while one was open for 0% -> 0% of each run, Pallas kernels for 0% -> 3%
where the time goes in v4:
time: 36.4 us; the launch traced here: 36.2 us
  Pallas kernels  12.5 us (34%)
  waiting for transfers between devices  11.4 us (31%)
  starting transfers between devices  8.98 us (25%)
  other arithmetic  1.68 us (5%)
  between operations  1.55 us (4%)
    ppermute x14, waiting for transfers between devices, flipped_to(): return lax.ppermute(x, axis, [(i, i ^ mask) for i in range(count)])  11.4 us
    pallas_call x1, Pallas kernels, wire(): pl.pallas_call(kernel, out_shape=jax.ShapeDtypeStruct((4, 64, 128), bf16)...  10.6 us
    ppermute x14, starting transfers between devices, flipped_to(): return lax.ppermute(x, axis, [(i, i ^ mask) for i in range(count)])  8.98 us
    pallas_call x1, Pallas kernels, order_weights(): pl.pallas_call(kernel, out_shape=[shape] * 4, in_specs=[SMEM, VMEM], out_...  0.9 us
    pallas_call x1, Pallas kernels, sum_far(): pl.pallas_call(kernel, out_shape=jax.ShapeDtypeStruct(plain.shape[1:], f3...  0.82 us
    select_n x1, other arithmetic, body(): jnp.where(first, links[0], links[2])  0.82 us
    add x1, other arithmetic, body(): at_rows(jnp.where(first, links[0], links[2]), 0)  0.79 us
  transfers between devices with their start and end apart: 14, of which 7 were waited for; matrix products, arithmetic and copies ran while one was open for 0% of the time, Pallas kernels for 3%

profile of v4, /device:TPU:0, one launch (start us, length us, event | category | flops | bytes accessed | tf_op | source)
XLA Modules:
  0.0 36.2 jit_solution(211084631794940124)
XLA Ops:
  0.0 0.0 copy-start.2
  0.0 0.0 copy-start
  0.8 0.8 %select_bitcast_fusion.1 = (f32[64,128]{1,0:T(8,128)S(1)}, f32[64,128]{1,0:T(8,128)S(1)}) fusion(f32[1,4,64,128]{3,2,1,0:T(8,128)} %param.10, pred[]{:T(512)S(6)} %eq.88), kind=kLoop, calls=%fused_computation.5 | loop fusion | flops 16384 | bytes 196609 | tf_op jit(solution)/shard_map/jit(_where)/select_n | solution.py:611
  1.6 0.0 copy-done.2
  1.7 0.1 pad.36
  1.8 0.8 %add_add_fusion.in_ref = f32[208,128]{1,0:T(8,128)S(1)} fusion(f32[2,128]{1,0:T(2,128)} %bitcast.74, f32[2,128]{1,0:T(2,128)} %bitcast.75, f32[8,128]{1,0:T(8,128)S(1)} %fusion.1, f32[64,128]{1,0:T(8,128)S(1)} %get-tuple-element.13, f32[64,128]{1,0:T(8,128)S(1)} %get-tuple-element.16, f32[64,128]{1,0:T(8,128)S(1)} %get-tuple-element.15, f32[208]{0:T(256)S(1)} %pad.36), kind=kLoop, calls=%fused_computation | loop fusion | flops 159744 | bytes 211776 | tf_op jit(solution)/shard_map/add | solution.py:611
  2.6 3.0 %collective-permute-start = (f32[208,128]{1,0:T(8,128)S(1)}, f32[208,128]{1,0:T(8,128)S(1)}, u32[]{:S(2)}, u32[]{:S(2)}) collective-permute-start(f32[208,128]{1,0:T(8,128)S(1)} %add_add_fusion.in_ref), channel_id=1, source_target_pairs={{0,1},{1,0},{2,3},{3,2},{4,5},{5,4},{6,7},{7,6},{8,9},{9,8},{10,11... | collective-permute-start | bytes 319496 | tf_op jit(solution)/shard_map/ppermute | solution.py:593
  5.6 1.5 %collective-permute-start.1 = (f32[208,128]{1,0:T(8,128)S(1)}, f32[208,128]{1,0:T(8,128)S(1)}, u32[]{:S(2)}, u32[]{:S(2)}) collective-permute-start(f32[208,128]{1,0:T(8,128)S(1)} %add_add_fusion.in_ref), channel_id=1, source_target_pairs={{0,2},{1,3},{2,0},{3,1},{4,6},{5,7},{6,4},{7,5},{8,10},{9,11},{10,... | collective-permute-start | bytes 319496 | tf_op jit(solution)/shard_map/ppermute | solution.py:593
  7.1 0.0 collective-permute-start.2
  7.1 0.0 collective-permute-start.3
  7.1 1.7 %collective-permute-done.refs_1_ = f32[208,128]{1,0:T(8,128)S(1)} collective-permute-done((f32[208,128]{1,0:T(8,128)S(1)}, f32[208,128]{1,0:T(8,128)S(1)}, u32[]{:S(2)}, u32[]{:S(2)}) %collective-permute-start) | collective-permute-done | bytes 106528 | tf_op jit(solution)/shard_map/ppermute | solution.py:593
  8.8 0.0 collective-permute-start.4
  8.8 2.6 %collective-permute-done.1.refs_2_ = f32[208,128]{1,0:T(8,128)S(1)} collective-permute-done((f32[208,128]{1,0:T(8,128)S(1)}, f32[208,128]{1,0:T(8,128)S(1)}, u32[]{:S(2)}, u32[]{:S(2)}) %collective-permute-start.1) | collective-permute-done | bytes 106528 | tf_op jit(solution)/shard_map/ppermute | solution.py:593
  11.4 0.0 collective-permute-start.5
  11.4 1.3 %collective-permute-done.2.refs_3_ = f32[208,128]{1,0:T(8,128)S(1)} collective-permute-done((f32[208,128]{1,0:T(8,128)S(1)}, f32[208,128]{1,0:T(8,128)S(1)}, u32[]{:S(2)}, u32[]{:S(2)}) %collective-permute-start.2) | collective-permute-done | bytes 106528 | tf_op jit(solution)/shard_map/ppermute | solution.py:593
  12.7 0.0 collective-permute-start.6
  13.4 0.0 collective-permute-done.3.refs_4_
  13.4 0.0 collective-permute-done.4.refs_5_
  13.4 0.0 collective-permute-done.5.refs_6_
  13.4 0.6 %collective-permute-done.6.refs_7_ = f32[208,128]{1,0:T(8,128)S(1)} collective-permute-done((f32[208,128]{1,0:T(8,128)S(1)}, f32[208,128]{1,0:T(8,128)S(1)}, u32[]{:S(2)}, u32[]{:S(2)}) %collective-permute-start.6) | collective-permute-done | bytes 106528 | tf_op jit(solution)/shard_map/ppermute | solution.py:593
  14.0 10.6 %wire.1.refs_2_ = bf16[4,64,128]{2,1,0:T(8,128)(2,1)S(1)} custom-call(f32[208,128]{1,0:T(8,128)S(1)} %settle.1.refs_0_, f32[208,128]{1,0:T(8,128)S(1)} %collective-permute-done.refs_1_, f32[208,128]{1,0:T(8,128)S(1)} %collective-permute-done.1.refs_2_, f32[208,128]{1,0:T(8,128)S(1)} %collective-permute-done.2.refs_3_, ...), custom_call_target="tpu_custom_call" | custom-call | tf_op jit(solution)/shard_map/wire/pallas_call | solution.py:479
  24.7 0.0 copy-start.1
  24.7 2.7 %collective-permute-start.10 = (bf16[4,64,128]{2,1,0:T(8,128)(2,1)S(1)}, bf16[4,64,128]{2,1,0:T(8,128)(2,1)S(1)}, u32[]{:S(2)}, u32[]{:S(2)}) collective-permute-start(bf16[4,64,128]{2,1,0:T(8,128)(2,1)S(1)} %wire.1.refs_2_), channel_id=1, source_target_pairs={{0,16},{4,20},{8,24},{12,28},{16,0},{20,4},{24,8},{28,12},{1,17},{... | collective-permute-start | bytes 196616 | tf_op jit(solution)/shard_map/ppermute | solution.py:593
  27.3 1.4 %collective-permute-start.12 = (bf16[4,64,128]{2,1,0:T(8,128)(2,1)S(1)}, bf16[4,64,128]{2,1,0:T(8,128)(2,1)S(1)}, u32[]{:S(2)}, u32[]{:S(2)}) collective-permute-start(bf16[4,64,128]{2,1,0:T(8,128)(2,1)S(1)} %wire.1.refs_2_), channel_id=1, source_target_pairs={{0,24},{4,28},{8,16},{12,20},{16,8},{20,12},{24,0},{28,4},{1,25},{... | collective-permute-start | bytes 196616 | tf_op jit(solution)/shard_map/ppermute | solution.py:593
  28.7 0.2 collective-permute-start.8
  28.9 0.0 collective-permute-start.7
  28.9 3.5 %collective-permute-done.10.refs_4_ = bf16[4,64,128]{2,1,0:T(8,128)(2,1)S(1)} collective-permute-done((bf16[4,64,128]{2,1,0:T(8,128)(2,1)S(1)}, bf16[4,64,128]{2,1,0:T(8,128)(2,1)S(1)}, u32[]{:S(2)}, u32[]{:S(2)}) %collective-permute-start.10) | collective-permute-done | bytes 65568 | tf_op jit(solution)/shard_map/ppermute | solution.py:593
  32.4 0.0 collective-permute-start.11
  32.5 1.3 %collective-permute-done.12.refs_5_ = bf16[4,64,128]{2,1,0:T(8,128)(2,1)S(1)} collective-permute-done((bf16[4,64,128]{2,1,0:T(8,128)(2,1)S(1)}, bf16[4,64,128]{2,1,0:T(8,128)(2,1)S(1)}, u32[]{:S(2)}, u32[]{:S(2)}) %collective-permute-start.12) | collective-permute-done | bytes 65568 | tf_op jit(solution)/shard_map/ppermute | solution.py:593
  33.7 0.0 collective-permute-start.13
  33.7 0.3 collective-permute-done.8.refs_3_
  34.1 0.2 collective-permute-start.9
  34.3 0.0 copy-done
  34.3 0.0 copy-done.1
  34.3 0.9 %order_weights.1 = (f32[4,4,64,128]{3,2,1,0:T(8,128)S(1)}, f32[4,4,64,128]{3,2,1,0:T(8,128)S(1)}, f32[4,4,64,128]{3,2,1,0:T(8,128)S(1)}, f32[4,4,64,128]{3,2,1,0:T(8,128)S(1)}) custom-call(s32[1,8]{1,0:T(1,128)S(1)} %copy-done.1, f32[8,4,64,128]{3,2,1,0:T(8,128)S(1)} %bitcast.73), custom_call_target="tpu_custom_call" | custom-call | tf_op jit(solution)/shard_map/order_weights/pallas_call | solution.py:525
  35.2 0.2 sum_near.1.refs_6_
  35.3 0.0 collective-permute-done.7.refs_2_
  35.4 0.0 collective-permute-done.11.refs_4_
  35.4 0.0 collective-permute-done.13.refs_5_
  35.4 0.0 collective-permute-done.9.refs_3_
  35.4 0.8 %sum_far.1 = f32[4,64,128]{2,1,0:T(8,128)} custom-call(f32[4,4,64,128]{3,2,1,0:T(8,128)S(1)} %get-tuple-element.9.refs_0_, f32[4,4,64,128]{3,2,1,0:T(8,128)S(1)} %get-tuple-element.10.refs_1_, bf16[4,64,128]{2,1,0:T(8,128)(2,1)S(1)} %collective-permute-done.7.refs_2_, bf16[4,64,128]{2,1,0:T(8,128)(2,1)S(1)} %collective-permute-done.9.refs_3_, ...), custom_call_target="tpu_custom_call" | custom-call | tf_op jit(solution)/shard_map/sum_far/pallas_call | solution.py:580
  (9 shorter events, 0.1 us)
Async XLA Ops:
  0.0 1.6 %copy-start.2 = (f32[1,4,64,128]{3,2,1,0:T(8,128)S(1)}, f32[1,4,64,128]{3,2,1,0:T(8,128)}, u32[]{:S(2)}) copy-start(f32[1,4,64,128]{3,2,1,0:T(8,128)} %param.9) | copy-start | bytes 393220
  0.0 34.3 %copy-start = (f32[8,1,4,64,128]{4,3,2,1,0:T(8,128)S(1)}, f32[8,1,4,64,128]{4,3,2,1,0:T(8,128)}, u32[]{:S(2)}) copy-start(f32[8,1,4,64,128]{4,3,2,1,0:T(8,128)} %param.13) | copy-start | bytes 3145732
  2.6 6.3 %collective-permute-start = (f32[208,128]{1,0:T(8,128)S(1)}, f32[208,128]{1,0:T(8,128)S(1)}, u32[]{:S(2)}, u32[]{:S(2)}) collective-permute-start(f32[208,128]{1,0:T(8,128)S(1)} %add_add_fusion.in_ref), channel_id=1, source_target_pairs={{0,1},{1,0},{2,3},{3,2},{4,5},{5,4},{6,7},{7,6},{8,9},{9,8},{10,11... | collective-permute-start | bytes 319496 | tf_op jit(solution)/shard_map/ppermute | solution.py:593
  5.6 5.8 %collective-permute-start.1 = (f32[208,128]{1,0:T(8,128)S(1)}, f32[208,128]{1,0:T(8,128)S(1)}, u32[]{:S(2)}, u32[]{:S(2)}) collective-permute-start(f32[208,128]{1,0:T(8,128)S(1)} %add_add_fusion.in_ref), channel_id=1, source_target_pairs={{0,2},{1,3},{2,0},{3,1},{4,6},{5,7},{6,4},{7,5},{8,10},{9,11},{10,... | collective-permute-start | bytes 319496 | tf_op jit(solution)/shard_map/ppermute | solution.py:593
  7.1 5.6 %collective-permute-start.2 = (f32[208,128]{1,0:T(8,128)S(1)}, f32[208,128]{1,0:T(8,128)S(1)}, u32[]{:S(2)}, u32[]{:S(2)}) collective-permute-start(f32[208,128]{1,0:T(8,128)S(1)} %add_add_fusion.in_ref), channel_id=1, source_target_pairs={{0,3},{1,2},{2,1},{3,0},{4,7},{5,6},{6,5},{7,4},{8,11},{9,10},{10,... | collective-permute-start | bytes 319496 | tf_op jit(solution)/shard_map/ppermute | solution.py:593
  7.1 6.3 %collective-permute-start.3 = (f32[208,128]{1,0:T(8,128)S(1)}, f32[208,128]{1,0:T(8,128)S(1)}, u32[]{:S(2)}, u32[]{:S(2)}) collective-permute-start(f32[208,128]{1,0:T(8,128)S(1)} %add_add_fusion.in_ref), channel_id=1, source_target_pairs={{0,4},{4,0},{8,12},{12,8},{16,20},{20,16},{24,28},{28,24},{1,5},{5... | collective-permute-start | bytes 319496 | tf_op jit(solution)/shard_map/ppermute | solution.py:593
  8.8 4.6 %collective-permute-start.4 = (f32[208,128]{1,0:T(8,128)S(1)}, f32[208,128]{1,0:T(8,128)S(1)}, u32[]{:S(2)}, u32[]{:S(2)}) collective-permute-start(f32[208,128]{1,0:T(8,128)S(1)} %collective-permute-done.refs_1_), channel_id=1, source_target_pairs={{0,4},{4,0},{8,12},{12,8},{16,20},{20,16},{24,28},{28,24},{1,5},{5... | collective-permute-start | bytes 319496 | tf_op jit(solution)/shard_map/ppermute | solution.py:593
  11.4 2.0 %collective-permute-start.5 = (f32[208,128]{1,0:T(8,128)S(1)}, f32[208,128]{1,0:T(8,128)S(1)}, u32[]{:S(2)}, u32[]{:S(2)}) collective-permute-start(f32[208,128]{1,0:T(8,128)S(1)} %collective-permute-done.1.refs_2_), channel_id=1, source_target_pairs={{0,4},{4,0},{8,12},{12,8},{16,20},{20,16},{24,28},{28,24},{1,5},{5... | collective-permute-start | bytes 319496 | tf_op jit(solution)/shard_map/ppermute | solution.py:593
  12.7 1.3 %collective-permute-start.6 = (f32[208,128]{1,0:T(8,128)S(1)}, f32[208,128]{1,0:T(8,128)S(1)}, u32[]{:S(2)}, u32[]{:S(2)}) collective-permute-start(f32[208,128]{1,0:T(8,128)S(1)} %collective-permute-done.2.refs_3_), channel_id=1, source_target_pairs={{0,4},{4,0},{8,12},{12,8},{16,20},{20,16},{24,28},{28,24},{1,5},{5... | collective-permute-start | bytes 319496 | tf_op jit(solution)/shard_map/ppermute | solution.py:593
  24.7 9.6 %copy-start.1 = (s32[1,8]{1,0:T(1,128)S(1)}, s32[1,8]{1,0:T(1,128)}, u32[]{:S(2)}) copy-start(s32[1,8]{1,0:T(1,128)} %refs_0_.1) | copy-start | bytes 100
  24.7 7.8 %collective-permute-start.10 = (bf16[4,64,128]{2,1,0:T(8,128)(2,1)S(1)}, bf16[4,64,128]{2,1,0:T(8,128)(2,1)S(1)}, u32[]{:S(2)}, u32[]{:S(2)}) collective-permute-start(bf16[4,64,128]{2,1,0:T(8,128)(2,1)S(1)} %wire.1.refs_2_), channel_id=1, source_target_pairs={{0,16},{4,20},{8,24},{12,28},{16,0},{20,4},{24,8},{28,12},{1,17},{... | collective-permute-start | bytes 196616 | tf_op jit(solution)/shard_map/ppermute | solution.py:593
  27.3 6.4 %collective-permute-start.12 = (bf16[4,64,128]{2,1,0:T(8,128)(2,1)S(1)}, bf16[4,64,128]{2,1,0:T(8,128)(2,1)S(1)}, u32[]{:S(2)}, u32[]{:S(2)}) collective-permute-start(bf16[4,64,128]{2,1,0:T(8,128)(2,1)S(1)} %wire.1.refs_2_), channel_id=1, source_target_pairs={{0,24},{4,28},{8,16},{12,20},{16,8},{20,12},{24,0},{28,4},{1,25},{... | collective-permute-start | bytes 196616 | tf_op jit(solution)/shard_map/ppermute | solution.py:593
  28.7 5.4 %collective-permute-start.8 = (bf16[4,64,128]{2,1,0:T(8,128)(2,1)S(1)}, bf16[4,64,128]{2,1,0:T(8,128)(2,1)S(1)}, u32[]{:S(2)}, u32[]{:S(2)}) collective-permute-start(bf16[4,64,128]{2,1,0:T(8,128)(2,1)S(1)} %wire.1.refs_2_), channel_id=1, source_target_pairs={{0,8},{4,12},{8,0},{12,4},{16,24},{20,28},{24,16},{28,20},{1,9},{5... | collective-permute-start | bytes 196616 | tf_op jit(solution)/shard_map/ppermute | solution.py:593
  28.9 6.5 %collective-permute-start.7 = (bf16[4,64,128]{2,1,0:T(8,128)(2,1)S(1)}, bf16[4,64,128]{2,1,0:T(8,128)(2,1)S(1)}, u32[]{:S(2)}, u32[]{:S(2)}) collective-permute-start(bf16[4,64,128]{2,1,0:T(8,128)(2,1)S(1)} %wire.1.refs_2_), channel_id=1, source_target_pairs={{0,4},{4,0},{8,12},{12,8},{16,20},{20,16},{24,28},{28,24},{1,5},{5... | collective-permute-start | bytes 196616 | tf_op jit(solution)/shard_map/ppermute | solution.py:593
  32.4 2.9 %collective-permute-start.11 = (bf16[4,64,128]{2,1,0:T(8,128)(2,1)S(1)}, bf16[4,64,128]{2,1,0:T(8,128)(2,1)S(1)}, u32[]{:S(2)}, u32[]{:S(2)}) collective-permute-start(bf16[4,64,128]{2,1,0:T(8,128)(2,1)S(1)} %collective-permute-done.10.refs_4_), channel_id=1, source_target_pairs={{0,4},{4,0},{8,12},{12,8},{16,20},{20,16},{24,28},{28,24},{1,5},{5... | collective-permute-start | bytes 196616 | tf_op jit(solution)/shard_map/ppermute | solution.py:593
  33.7 1.6 %collective-permute-start.13 = (bf16[4,64,128]{2,1,0:T(8,128)(2,1)S(1)}, bf16[4,64,128]{2,1,0:T(8,128)(2,1)S(1)}, u32[]{:S(2)}, u32[]{:S(2)}) collective-permute-start(bf16[4,64,128]{2,1,0:T(8,128)(2,1)S(1)} %collective-permute-done.12.refs_5_), channel_id=1, source_target_pairs={{0,4},{4,0},{8,12},{12,8},{16,20},{20,16},{24,28},{28,24},{1,5},{5... | collective-permute-start | bytes 196616 | tf_op jit(solution)/shard_map/ppermute | solution.py:593
  34.1 1.3 %collective-permute-start.9 = (bf16[4,64,128]{2,1,0:T(8,128)(2,1)S(1)}, bf16[4,64,128]{2,1,0:T(8,128)(2,1)S(1)}, u32[]{:S(2)}, u32[]{:S(2)}) collective-permute-start(bf16[4,64,128]{2,1,0:T(8,128)(2,1)S(1)} %collective-permute-done.8.refs_3_), channel_id=1, source_target_pairs={{0,4},{4,0},{8,12},{12,8},{16,20},{20,16},{24,28},{28,24},{1,5},{5... | collective-permute-start | bytes 196616 | tf_op jit(solution)/shard_map/ppermute | solution.py:593

commit v5 on v4

--- a/solution.py
+++ b/solution.py
@@ -198,8 +198,8 @@
 
 
 def wire_kernel(segs, *refs):
-    own = refs[:segs]
-    other = refs[segs : 2 * segs]
+    other = refs[:segs][::-1]
+    own = refs[segs : 2 * segs][::-1]
     out_ref = refs[2 * segs]
     (u_ref, h_ref, d_ref, m_ref, at_ref, ar_ref, ai_ref, yright_ref, yleft_ref, g_ref, s_ref, k_ref, t_ref) = (
         refs[2 * segs + 1 :]
@@ -498,7 +498,7 @@
         ],
         compiler_params=pltpu.CompilerParams(vmem_limit_bytes=(8 + 2 * segs) * 2**20),
         name="wire",
-    )(*own, *other)
+    )(*other[::-1], *own[::-1])
 
 
 def order_kernel(chips, sources_ref, screened_ref, *out_refs):

time: 36.4 us -> 36 us (0.989)
  waiting for transfers between devices: 11.4 us -> 10.4 us
  starting transfers between devices: 8.98 us -> 9.53 us
    ppermute x14, waiting for transfers between devices: 11.4 us -> 10.4 us  [flipped_to(): return lax.ppermute(x, axis, [(i, i ^ mask) for i in range(count)])]
    ppermute x14, starting transfers between devices: 8.98 us -> 9.53 us  [flipped_to(): return lax.ppermute(x, axis, [(i, i ^ mask) for i in range(count)])]
  transfers between devices with their start and end apart: 14 -> 14, of which waited for: 7 -> 8; matrix products, arithmetic and copies ran while one was open for 0% -> 0% of each run, Pallas kernels for 3% -> 3%
where the time goes in v5:
time: 36 us; the launch traced here: 35.8 us
  Pallas kernels  12.5 us (35%)
  waiting for transfers between devices  10.4 us (29%)
  starting transfers between devices  9.53 us (26%)
  other arithmetic  1.68 us (5%)
  between operations  1.54 us (4%)
    pallas_call x1, Pallas kernels, wire(): pl.pallas_call(kernel, out_shape=jax.ShapeDtypeStruct((4, 64, 128), bf16)...  10.6 us
    ppermute x14, waiting for transfers between devices, flipped_to(): return lax.ppermute(x, axis, [(i, i ^ mask) for i in range(count)])  10.4 us
    ppermute x14, starting transfers between devices, flipped_to(): return lax.ppermute(x, axis, [(i, i ^ mask) for i in range(count)])  9.53 us
    pallas_call x1, Pallas kernels, order_weights(): pl.pallas_call(kernel, out_shape=[shape] * 4, in_specs=[SMEM, VMEM], out_...  0.9 us
    pallas_call x1, Pallas kernels, sum_far(): pl.pallas_call(kernel, out_shape=jax.ShapeDtypeStruct(plain.shape[1:], f3...  0.82 us
    select_n x1, other arithmetic, body(): jnp.where(first, links[0], links[2])  0.82 us
    add x1, other arithmetic, body(): at_rows(jnp.where(first, links[0], links[2]), 0)  0.79 us
  transfers between devices with their start and end apart: 14, of which 8 were waited for; matrix products, arithmetic and copies ran while one was open for 0% of the time, Pallas kernels for 3%

profile of v5, /device:TPU:0, one launch (start us, length us, event | category | flops | bytes accessed | tf_op | source)
XLA Modules:
  0.0 35.8 jit_solution(4150899444347763123)
XLA Ops:
  0.0 0.0 copy-start.2
  0.0 0.0 copy-start
  0.8 0.8 %select_bitcast_fusion.1 = (f32[64,128]{1,0:T(8,128)S(1)}, f32[64,128]{1,0:T(8,128)S(1)}) fusion(f32[1,4,64,128]{3,2,1,0:T(8,128)} %param.10, pred[]{:T(512)S(6)} %eq.88), kind=kLoop, calls=%fused_computation.5 | loop fusion | flops 16384 | bytes 196609 | tf_op jit(solution)/shard_map/jit(_where)/select_n | solution.py:611
  1.6 0.0 copy-done.2
  1.7 0.1 pad.36
  1.8 0.8 %add_add_fusion.in_ref = f32[208,128]{1,0:T(8,128)S(1)} fusion(f32[2,128]{1,0:T(2,128)} %bitcast.74, f32[2,128]{1,0:T(2,128)} %bitcast.75, f32[8,128]{1,0:T(8,128)S(1)} %fusion.1, f32[64,128]{1,0:T(8,128)S(1)} %get-tuple-element.13, f32[64,128]{1,0:T(8,128)S(1)} %get-tuple-element.16, f32[64,128]{1,0:T(8,128)S(1)} %get-tuple-element.15, f32[208]{0:T(256)S(1)} %pad.36), kind=kLoop, calls=%fused_computation | loop fusion | flops 159744 | bytes 211776 | tf_op jit(solution)/shard_map/add | solution.py:611
  2.6 4.0 %collective-permute-start = (f32[208,128]{1,0:T(8,128)S(1)}, f32[208,128]{1,0:T(8,128)S(1)}, u32[]{:S(2)}, u32[]{:S(2)}) collective-permute-start(f32[208,128]{1,0:T(8,128)S(1)} %add_add_fusion.in_ref), channel_id=1, source_target_pairs={{0,3},{1,2},{2,1},{3,0},{4,7},{5,6},{6,5},{7,4},{8,11},{9,10},{10,... | collective-permute-start | bytes 319496 | tf_op jit(solution)/shard_map/ppermute | solution.py:593
  6.5 0.5 %collective-permute-start.2 = (f32[208,128]{1,0:T(8,128)S(1)}, f32[208,128]{1,0:T(8,128)S(1)}, u32[]{:S(2)}, u32[]{:S(2)}) collective-permute-start(f32[208,128]{1,0:T(8,128)S(1)} %add_add_fusion.in_ref), channel_id=1, source_target_pairs={{0,2},{1,3},{2,0},{3,1},{4,6},{5,7},{6,4},{7,5},{8,10},{9,11},{10,... | collective-permute-start | bytes 319496 | tf_op jit(solution)/shard_map/ppermute | solution.py:593
  7.0 0.1 collective-permute-start.4
  7.2 0.0 collective-permute-start.6
  7.2 2.7 %collective-permute-done.refs_4_ = f32[208,128]{1,0:T(8,128)S(1)} collective-permute-done((f32[208,128]{1,0:T(8,128)S(1)}, f32[208,128]{1,0:T(8,128)S(1)}, u32[]{:S(2)}, u32[]{:S(2)}) %collective-permute-start) | collective-permute-done | bytes 106528 | tf_op jit(solution)/shard_map/ppermute | solution.py:593
  9.9 0.0 collective-permute-start.1
  9.9 1.9 %collective-permute-done.2.refs_5_ = f32[208,128]{1,0:T(8,128)S(1)} collective-permute-done((f32[208,128]{1,0:T(8,128)S(1)}, f32[208,128]{1,0:T(8,128)S(1)}, u32[]{:S(2)}, u32[]{:S(2)}) %collective-permute-start.2) | collective-permute-done | bytes 106528 | tf_op jit(solution)/shard_map/ppermute | solution.py:593
  11.8 0.0 collective-permute-start.3
  11.8 0.2 collective-permute-done.4.refs_6_
  12.0 0.3 collective-permute-start.5
  13.0 0.0 collective-permute-done.6.refs_3_
  13.0 0.0 collective-permute-done.1.refs_0_
  13.0 0.1 collective-permute-done.3.refs_1_
  13.1 0.2 collective-permute-done.5.refs_2_
  13.3 10.6 %wire.1.refs_2_ = bf16[4,64,128]{2,1,0:T(8,128)(2,1)S(1)} custom-call(f32[208,128]{1,0:T(8,128)S(1)} %collective-permute-done.1.refs_0_, f32[208,128]{1,0:T(8,128)S(1)} %collective-permute-done.3.refs_1_, f32[208,128]{1,0:T(8,128)S(1)} %collective-permute-done.5.refs_2_, f32[208,128]{1,0:T(8,128)S(1)} %collective-permute-done.6.refs_3_, ...), custom_call_target="tpu_custom_call" | custom-call | tf_op jit(solution)/shard_map/wire/pallas_call | solution.py:479
  24.0 0.0 copy-start.1
  24.0 2.8 %collective-permute-start.10 = (bf16[4,64,128]{2,1,0:T(8,128)(2,1)S(1)}, bf16[4,64,128]{2,1,0:T(8,128)(2,1)S(1)}, u32[]{:S(2)}, u32[]{:S(2)}) collective-permute-start(bf16[4,64,128]{2,1,0:T(8,128)(2,1)S(1)} %wire.1.refs_2_), channel_id=1, source_target_pairs={{0,16},{4,20},{8,24},{12,28},{16,0},{20,4},{24,8},{28,12},{1,17},{... | collective-permute-start | bytes 196616 | tf_op jit(solution)/shard_map/ppermute | solution.py:593
  26.8 1.3 %collective-permute-start.12 = (bf16[4,64,128]{2,1,0:T(8,128)(2,1)S(1)}, bf16[4,64,128]{2,1,0:T(8,128)(2,1)S(1)}, u32[]{:S(2)}, u32[]{:S(2)}) collective-permute-start(bf16[4,64,128]{2,1,0:T(8,128)(2,1)S(1)} %wire.1.refs_2_), channel_id=1, source_target_pairs={{0,24},{4,28},{8,16},{12,20},{16,8},{20,12},{24,0},{28,4},{1,25},{... | collective-permute-start | bytes 196616 | tf_op jit(solution)/shard_map/ppermute | solution.py:593
  28.1 0.2 collective-permute-start.8
  28.3 0.0 collective-permute-start.7
  28.3 2.6 %collective-permute-done.10.refs_4_ = bf16[4,64,128]{2,1,0:T(8,128)(2,1)S(1)} collective-permute-done((bf16[4,64,128]{2,1,0:T(8,128)(2,1)S(1)}, bf16[4,64,128]{2,1,0:T(8,128)(2,1)S(1)}, u32[]{:S(2)}, u32[]{:S(2)}) %collective-permute-start.10) | collective-permute-done | bytes 65568 | tf_op jit(solution)/shard_map/ppermute | solution.py:593
  30.9 0.0 collective-permute-start.11
  30.9 2.4 %collective-permute-done.12.refs_5_ = bf16[4,64,128]{2,1,0:T(8,128)(2,1)S(1)} collective-permute-done((bf16[4,64,128]{2,1,0:T(8,128)(2,1)S(1)}, bf16[4,64,128]{2,1,0:T(8,128)(2,1)S(1)}, u32[]{:S(2)}, u32[]{:S(2)}) %collective-permute-start.12) | collective-permute-done | bytes 65568 | tf_op jit(solution)/shard_map/ppermute | solution.py:593
  33.3 0.0 collective-permute-start.13
  33.3 0.2 collective-permute-done.8.refs_3_
  33.6 0.3 collective-permute-start.9
  33.9 0.0 copy-done
  33.9 0.0 copy-done.1
  33.9 0.9 %order_weights.1 = (f32[4,4,64,128]{3,2,1,0:T(8,128)S(1)}, f32[4,4,64,128]{3,2,1,0:T(8,128)S(1)}, f32[4,4,64,128]{3,2,1,0:T(8,128)S(1)}, f32[4,4,64,128]{3,2,1,0:T(8,128)S(1)}) custom-call(s32[1,8]{1,0:T(1,128)S(1)} %copy-done.1, f32[8,4,64,128]{3,2,1,0:T(8,128)S(1)} %bitcast.73), custom_call_target="tpu_custom_call" | custom-call | tf_op jit(solution)/shard_map/order_weights/pallas_call | solution.py:525
  34.8 0.2 sum_near.1.refs_6_
  35.0 0.0 collective-permute-done.7.refs_2_
  35.0 0.0 collective-permute-done.11.refs_4_
  35.0 0.0 collective-permute-done.13.refs_5_
  35.0 0.0 collective-permute-done.9.refs_3_
  35.0 0.8 %sum_far.1 = f32[4,64,128]{2,1,0:T(8,128)} custom-call(f32[4,4,64,128]{3,2,1,0:T(8,128)S(1)} %get-tuple-element.9.refs_0_, f32[4,4,64,128]{3,2,1,0:T(8,128)S(1)} %get-tuple-element.10.refs_1_, bf16[4,64,128]{2,1,0:T(8,128)(2,1)S(1)} %collective-permute-done.7.refs_2_, bf16[4,64,128]{2,1,0:T(8,128)(2,1)S(1)} %collective-permute-done.9.refs_3_, ...), custom_call_target="tpu_custom_call" | custom-call | tf_op jit(solution)/shard_map/sum_far/pallas_call | solution.py:580
  (9 shorter events, 0.1 us)
Async XLA Ops:
  0.0 1.6 %copy-start.2 = (f32[1,4,64,128]{3,2,1,0:T(8,128)S(1)}, f32[1,4,64,128]{3,2,1,0:T(8,128)}, u32[]{:S(2)}) copy-start(f32[1,4,64,128]{3,2,1,0:T(8,128)} %param.9) | copy-start | bytes 393220
  0.0 33.9 %copy-start = (f32[8,1,4,64,128]{4,3,2,1,0:T(8,128)S(1)}, f32[8,1,4,64,128]{4,3,2,1,0:T(8,128)}, u32[]{:S(2)}) copy-start(f32[8,1,4,64,128]{4,3,2,1,0:T(8,128)} %param.13) | copy-start | bytes 3145732
  2.6 7.3 %collective-permute-start = (f32[208,128]{1,0:T(8,128)S(1)}, f32[208,128]{1,0:T(8,128)S(1)}, u32[]{:S(2)}, u32[]{:S(2)}) collective-permute-start(f32[208,128]{1,0:T(8,128)S(1)} %add_add_fusion.in_ref), channel_id=1, source_target_pairs={{0,3},{1,2},{2,1},{3,0},{4,7},{5,6},{6,5},{7,4},{8,11},{9,10},{10,... | collective-permute-start | bytes 319496 | tf_op jit(solution)/shard_map/ppermute | solution.py:593
  6.5 5.3 %collective-permute-start.2 = (f32[208,128]{1,0:T(8,128)S(1)}, f32[208,128]{1,0:T(8,128)S(1)}, u32[]{:S(2)}, u32[]{:S(2)}) collective-permute-start(f32[208,128]{1,0:T(8,128)S(1)} %add_add_fusion.in_ref), channel_id=1, source_target_pairs={{0,2},{1,3},{2,0},{3,1},{4,6},{5,7},{6,4},{7,5},{8,10},{9,11},{10,... | collective-permute-start | bytes 319496 | tf_op jit(solution)/shard_map/ppermute | solution.py:593
  7.0 5.0 %collective-permute-start.4 = (f32[208,128]{1,0:T(8,128)S(1)}, f32[208,128]{1,0:T(8,128)S(1)}, u32[]{:S(2)}, u32[]{:S(2)}) collective-permute-start(f32[208,128]{1,0:T(8,128)S(1)} %add_add_fusion.in_ref), channel_id=1, source_target_pairs={{0,1},{1,0},{2,3},{3,2},{4,5},{5,4},{6,7},{7,6},{8,9},{9,8},{10,11... | collective-permute-start | bytes 319496 | tf_op jit(solution)/shard_map/ppermute | solution.py:593
  7.2 5.8 %collective-permute-start.6 = (f32[208,128]{1,0:T(8,128)S(1)}, f32[208,128]{1,0:T(8,128)S(1)}, u32[]{:S(2)}, u32[]{:S(2)}) collective-permute-start(f32[208,128]{1,0:T(8,128)S(1)} %add_add_fusion.in_ref), channel_id=1, source_target_pairs={{0,4},{4,0},{8,12},{12,8},{16,20},{20,16},{24,28},{28,24},{1,5},{5... | collective-permute-start | bytes 319496 | tf_op jit(solution)/shard_map/ppermute | solution.py:593
  9.9 3.1 %collective-permute-start.1 = (f32[208,128]{1,0:T(8,128)S(1)}, f32[208,128]{1,0:T(8,128)S(1)}, u32[]{:S(2)}, u32[]{:S(2)}) collective-permute-start(f32[208,128]{1,0:T(8,128)S(1)} %collective-permute-done.refs_4_), channel_id=1, source_target_pairs={{0,4},{4,0},{8,12},{12,8},{16,20},{20,16},{24,28},{28,24},{1,5},{5... | collective-permute-start | bytes 319496 | tf_op jit(solution)/shard_map/ppermute | solution.py:593
  11.8 1.3 %collective-permute-start.3 = (f32[208,128]{1,0:T(8,128)S(1)}, f32[208,128]{1,0:T(8,128)S(1)}, u32[]{:S(2)}, u32[]{:S(2)}) collective-permute-start(f32[208,128]{1,0:T(8,128)S(1)} %collective-permute-done.2.refs_5_), channel_id=1, source_target_pairs={{0,4},{4,0},{8,12},{12,8},{16,20},{20,16},{24,28},{28,24},{1,5},{5... | collective-permute-start | bytes 319496 | tf_op jit(solution)/shard_map/ppermute | solution.py:593
  12.0 1.3 %collective-permute-start.5 = (f32[208,128]{1,0:T(8,128)S(1)}, f32[208,128]{1,0:T(8,128)S(1)}, u32[]{:S(2)}, u32[]{:S(2)}) collective-permute-start(f32[208,128]{1,0:T(8,128)S(1)} %collective-permute-done.4.refs_6_), channel_id=1, source_target_pairs={{0,4},{4,0},{8,12},{12,8},{16,20},{20,16},{24,28},{28,24},{1,5},{5... | collective-permute-start | bytes 319496 | tf_op jit(solution)/shard_map/ppermute | solution.py:593
  24.0 9.9 %copy-start.1 = (s32[1,8]{1,0:T(1,128)S(1)}, s32[1,8]{1,0:T(1,128)}, u32[]{:S(2)}) copy-start(s32[1,8]{1,0:T(1,128)} %refs_0_.1) | copy-start | bytes 100
  24.0 6.9 %collective-permute-start.10 = (bf16[4,64,128]{2,1,0:T(8,128)(2,1)S(1)}, bf16[4,64,128]{2,1,0:T(8,128)(2,1)S(1)}, u32[]{:S(2)}, u32[]{:S(2)}) collective-permute-start(bf16[4,64,128]{2,1,0:T(8,128)(2,1)S(1)} %wire.1.refs_2_), channel_id=1, source_target_pairs={{0,16},{4,20},{8,24},{12,28},{16,0},{20,4},{24,8},{28,12},{1,17},{... | collective-permute-start | bytes 196616 | tf_op jit(solution)/shard_map/ppermute | solution.py:593
  26.8 6.6 %collective-permute-start.12 = (bf16[4,64,128]{2,1,0:T(8,128)(2,1)S(1)}, bf16[4,64,128]{2,1,0:T(8,128)(2,1)S(1)}, u32[]{:S(2)}, u32[]{:S(2)}) collective-permute-start(bf16[4,64,128]{2,1,0:T(8,128)(2,1)S(1)} %wire.1.refs_2_), channel_id=1, source_target_pairs={{0,24},{4,28},{8,16},{12,20},{16,8},{20,12},{24,0},{28,4},{1,25},{... | collective-permute-start | bytes 196616 | tf_op jit(solution)/shard_map/ppermute | solution.py:593
  28.1 5.5 %collective-permute-start.8 = (bf16[4,64,128]{2,1,0:T(8,128)(2,1)S(1)}, bf16[4,64,128]{2,1,0:T(8,128)(2,1)S(1)}, u32[]{:S(2)}, u32[]{:S(2)}) collective-permute-start(bf16[4,64,128]{2,1,0:T(8,128)(2,1)S(1)} %wire.1.refs_2_), channel_id=1, source_target_pairs={{0,8},{4,12},{8,0},{12,4},{16,24},{20,28},{24,16},{28,20},{1,9},{5... | collective-permute-start | bytes 196616 | tf_op jit(solution)/shard_map/ppermute | solution.py:593
  28.3 6.6 %collective-permute-start.7 = (bf16[4,64,128]{2,1,0:T(8,128)(2,1)S(1)}, bf16[4,64,128]{2,1,0:T(8,128)(2,1)S(1)}, u32[]{:S(2)}, u32[]{:S(2)}) collective-permute-start(bf16[4,64,128]{2,1,0:T(8,128)(2,1)S(1)} %wire.1.refs_2_), channel_id=1, source_target_pairs={{0,4},{4,0},{8,12},{12,8},{16,20},{20,16},{24,28},{28,24},{1,5},{5... | collective-permute-start | bytes 196616 | tf_op jit(solution)/shard_map/ppermute | solution.py:593
  30.9 4.0 %collective-permute-start.11 = (bf16[4,64,128]{2,1,0:T(8,128)(2,1)S(1)}, bf16[4,64,128]{2,1,0:T(8,128)(2,1)S(1)}, u32[]{:S(2)}, u32[]{:S(2)}) collective-permute-start(bf16[4,64,128]{2,1,0:T(8,128)(2,1)S(1)} %collective-permute-done.10.refs_4_), channel_id=1, source_target_pairs={{0,4},{4,0},{8,12},{12,8},{16,20},{20,16},{24,28},{28,24},{1,5},{5... | collective-permute-start | bytes 196616 | tf_op jit(solution)/shard_map/ppermute | solution.py:593
  33.3 1.6 %collective-permute-start.13 = (bf16[4,64,128]{2,1,0:T(8,128)(2,1)S(1)}, bf16[4,64,128]{2,1,0:T(8,128)(2,1)S(1)}, u32[]{:S(2)}, u32[]{:S(2)}) collective-permute-start(bf16[4,64,128]{2,1,0:T(8,128)(2,1)S(1)} %collective-permute-done.12.refs_5_), channel_id=1, source_target_pairs={{0,4},{4,0},{8,12},{12,8},{16,20},{20,16},{24,28},{28,24},{1,5},{5... | collective-permute-start | bytes 196616 | tf_op jit(solution)/shard_map/ppermute | solution.py:593
  33.6 1.4 %collective-permute-start.9 = (bf16[4,64,128]{2,1,0:T(8,128)(2,1)S(1)}, bf16[4,64,128]{2,1,0:T(8,128)(2,1)S(1)}, u32[]{:S(2)}, u32[]{:S(2)}) collective-permute-start(bf16[4,64,128]{2,1,0:T(8,128)(2,1)S(1)} %collective-permute-done.8.refs_3_), channel_id=1, source_target_pairs={{0,4},{4,0},{8,12},{12,8},{16,20},{20,16},{24,28},{28,24},{1,5},{5... | collective-permute-start | bytes 196616 | tf_op jit(solution)/shard_map/ppermute | solution.py:593

commit v6 on v5

--- a/solution.py
+++ b/solution.py
@@ -180,24 +180,7 @@
     return pltpu.roll(x, 64, 1)
 
 
-def settle_kernel(energies_ref, in_ref, out_ref):
-    out_ref[0:200] = in_ref[0:200]
-    last = lax.broadcasted_iota(jnp.int32, (8, 128), 0) >= 6
-    out_ref[200:208] = jnp.where(last, energies_ref[0], in_ref[200:208])
-
-
-def settle(energies, piece):
-    return pl.pallas_call(
-        settle_kernel,
-        out_shape=jax.ShapeDtypeStruct(piece.shape, f32),
-        in_specs=[SMEM, VMEM],
-        out_specs=VMEM,
-        compiler_params=pltpu.CompilerParams(vmem_limit_bytes=4 * 2**20),
-        name="settle",
-    )(energies, piece)
-
-
-def wire_kernel(segs, *refs):
+def wire_kernel(segs, energy_ref, *refs):
     other = refs[:segs][::-1]
     own = refs[segs : 2 * segs][::-1]
     out_ref = refs[2 * segs]
@@ -216,7 +199,7 @@
             h_ref[2 * seg + c] = ref[128:192]
             d_ref[2 * seg + c] = ref[192:200]
         m_ref[seg] = own[k][200:208]
-    energy = own[0][206:207]
+    energy = energy_ref[0]
 
     start = jnp.int32(0)
     first, used = jnp.int32(0), jnp.int32(0)
@@ -469,7 +452,7 @@
         out_ref[k] = (jnp.where(keep, re, im) * live).astype(bf16)
 
 
-def wire(own, other):
+def wire(energies, own, other):
     segs = len(own)
     half = segs
 
@@ -479,7 +462,7 @@
     return pl.pallas_call(
         kernel,
         out_shape=jax.ShapeDtypeStruct((4, 64, 128), bf16),
-        in_specs=[VMEM] * (2 * segs),
+        in_specs=[SMEM] + [VMEM] * (2 * segs),
         out_specs=VMEM,
         scratch_shapes=[
             pltpu.VMEM((4 * segs, 64, 128), f32),
@@ -498,7 +481,7 @@
         ],
         compiler_params=pltpu.CompilerParams(vmem_limit_bytes=(8 + 2 * segs) * 2**20),
         name="wire",
-    )(*other[::-1], *own[::-1])
+    )(energies, *other[::-1], *own[::-1])
 
 
 def order_kernel(chips, sources_ref, screened_ref, *out_refs):
@@ -617,9 +600,9 @@
         + at_rows(jnp.broadcast_to(counts.astype(f32)[:, None], (4, 128)), 204)
     )
     sent = [flipped_to(piece, "seg", k) for k in range(1, segs)]
-    own = [settle(energies, piece)] + sent
+    own = [piece] + sent
     other = [flipped_to(x, "energy", 1) for x in [piece] + sent]
-    greens = wire(own, other)
+    greens = wire(energies, own, other)
     near = [greens] + [flipped_to(greens, "energy", cores * k) for k in range(1, chips)]
     far = [flipped_to(x, "energy", 1) for x in near]
     plain_near, other_near, plain_far, other_far = order_weights(chips, sources, screened[:, 0])

time: 36 us -> 36 us (level)
  no operation moved by 1% of the time
where the time goes in v6:
time: 36 us; the launch traced here: 35.8 us
  Pallas kernels  12.5 us (35%)
  waiting for transfers between devices  10.4 us (29%)
  starting transfers between devices  9.53 us (26%)
  other arithmetic  1.68 us (5%)
  between operations  1.53 us (4%)
    pallas_call x1, Pallas kernels, wire(): pl.pallas_call(kernel, out_shape=jax.ShapeDtypeStruct((4, 64, 128), bf16)...  10.6 us
    ppermute x14, waiting for transfers between devices, flipped_to(): return lax.ppermute(x, axis, [(i, i ^ mask) for i in range(count)])  10.4 us
    ppermute x14, starting transfers between devices, flipped_to(): return lax.ppermute(x, axis, [(i, i ^ mask) for i in range(count)])  9.53 us
    pallas_call x1, Pallas kernels, order_weights(): pl.pallas_call(kernel, out_shape=[shape] * 4, in_specs=[SMEM, VMEM], out_...  0.9 us
    pallas_call x1, Pallas kernels, sum_far(): pl.pallas_call(kernel, out_shape=jax.ShapeDtypeStruct(plain.shape[1:], f3...  0.82 us
    select_n x1, other arithmetic, body(): jnp.where(first, links[0], links[2])  0.82 us
    add x1, other arithmetic, body(): at_rows(jnp.where(first, links[0], links[2]), 0)  0.79 us
  transfers between devices with their start and end apart: 14, of which 8 were waited for; matrix products, arithmetic and copies ran while one was open for 0% of the time, Pallas kernels for 3%

profile of v6, /device:TPU:0, one launch (start us, length us, event | category | flops | bytes accessed | tf_op | source)
XLA Modules:
  0.0 35.8 jit_solution(9262530969365636040)
XLA Ops:
  0.0 0.0 copy-start.2
  0.0 0.0 copy-start
  0.8 0.8 %select_bitcast_fusion.1 = (f32[64,128]{1,0:T(8,128)S(1)}, f32[64,128]{1,0:T(8,128)S(1)}) fusion(f32[1,4,64,128]{3,2,1,0:T(8,128)} %param.10, pred[]{:T(512)S(6)} %eq.88), kind=kLoop, calls=%fused_computation.5 | loop fusion | flops 16384 | bytes 196609 | tf_op jit(solution)/shard_map/jit(_where)/select_n | solution.py:594
  1.6 0.0 copy-done.2
  1.7 0.1 pad.36
  1.8 0.8 %add_add_fusion.refs_8_ = f32[208,128]{1,0:T(8,128)S(1)} fusion(f32[2,128]{1,0:T(2,128)} %bitcast.74, f32[2,128]{1,0:T(2,128)} %bitcast.75, f32[8,128]{1,0:T(8,128)S(1)} %fusion.1, f32[64,128]{1,0:T(8,128)S(1)} %get-tuple-element.13, f32[64,128]{1,0:T(8,128)S(1)} %get-tuple-element.16, f32[64,128]{1,0:T(8,128)S(1)} %get-tuple-element.15, f32[208]{0:T(256)S(1)} %pad.36), kind=kLoop, calls=%fused_computation | loop fusion | flops 159744 | bytes 211776 | tf_op jit(solution)/shard_map/add | solution.py:594
  2.6 4.0 %collective-permute-start = (f32[208,128]{1,0:T(8,128)S(1)}, f32[208,128]{1,0:T(8,128)S(1)}, u32[]{:S(2)}, u32[]{:S(2)}) collective-permute-start(f32[208,128]{1,0:T(8,128)S(1)} %add_add_fusion.refs_8_), channel_id=1, source_target_pairs={{0,3},{1,2},{2,1},{3,0},{4,7},{5,6},{6,5},{7,4},{8,11},{9,10},{10,... | collective-permute-start | bytes 319496 | tf_op jit(solution)/shard_map/ppermute | solution.py:576
  6.5 0.5 %collective-permute-start.2 = (f32[208,128]{1,0:T(8,128)S(1)}, f32[208,128]{1,0:T(8,128)S(1)}, u32[]{:S(2)}, u32[]{:S(2)}) collective-permute-start(f32[208,128]{1,0:T(8,128)S(1)} %add_add_fusion.refs_8_), channel_id=1, source_target_pairs={{0,2},{1,3},{2,0},{3,1},{4,6},{5,7},{6,4},{7,5},{8,10},{9,11},{10,... | collective-permute-start | bytes 319496 | tf_op jit(solution)/shard_map/ppermute | solution.py:576
  7.0 0.1 collective-permute-start.4
  7.2 0.0 collective-permute-start.6
  7.2 2.7 %collective-permute-done.refs_5_ = f32[208,128]{1,0:T(8,128)S(1)} collective-permute-done((f32[208,128]{1,0:T(8,128)S(1)}, f32[208,128]{1,0:T(8,128)S(1)}, u32[]{:S(2)}, u32[]{:S(2)}) %collective-permute-start) | collective-permute-done | bytes 106528 | tf_op jit(solution)/shard_map/ppermute | solution.py:576
  9.9 0.0 collective-permute-start.1
  9.9 1.9 %collective-permute-done.2.refs_6_ = f32[208,128]{1,0:T(8,128)S(1)} collective-permute-done((f32[208,128]{1,0:T(8,128)S(1)}, f32[208,128]{1,0:T(8,128)S(1)}, u32[]{:S(2)}, u32[]{:S(2)}) %collective-permute-start.2) | collective-permute-done | bytes 106528 | tf_op jit(solution)/shard_map/ppermute | solution.py:576
  11.8 0.0 collective-permute-start.3
  11.8 0.2 collective-permute-done.4.refs_7_
  12.0 0.3 collective-permute-start.5
  12.9 0.0 collective-permute-done.6.refs_4_
  13.0 0.0 collective-permute-done.1.refs_1_
  13.0 0.1 collective-permute-done.3.refs_2_
  13.1 0.2 collective-permute-done.5.refs_3_
  13.3 10.6 %wire.1.refs_2_ = bf16[4,64,128]{2,1,0:T(8,128)(2,1)S(1)} custom-call(f32[1]{0:T(128)S(6)} %copy.9.refs_0_, f32[208,128]{1,0:T(8,128)S(1)} %collective-permute-done.1.refs_1_, f32[208,128]{1,0:T(8,128)S(1)} %collective-permute-done.3.refs_2_, f32[208,128]{1,0:T(8,128)S(1)} %collective-permute-done.5.refs_3_, f32[208,128]{1,0:T(8,128)S(1)} %collective-permute-done.6.refs_4_, ...), custom_call_target="tpu_custom_call" | custom-call | tf_op jit(solution)/shard_map/wire/pallas_call | solution.py:462
  24.0 0.0 copy-start.1
  24.0 2.8 %collective-permute-start.10 = (bf16[4,64,128]{2,1,0:T(8,128)(2,1)S(1)}, bf16[4,64,128]{2,1,0:T(8,128)(2,1)S(1)}, u32[]{:S(2)}, u32[]{:S(2)}) collective-permute-start(bf16[4,64,128]{2,1,0:T(8,128)(2,1)S(1)} %wire.1.refs_2_), channel_id=1, source_target_pairs={{0,16},{4,20},{8,24},{12,28},{16,0},{20,4},{24,8},{28,12},{1,17},{... | collective-permute-start | bytes 196616 | tf_op jit(solution)/shard_map/ppermute | solution.py:576
  26.8 1.3 %collective-permute-start.12 = (bf16[4,64,128]{2,1,0:T(8,128)(2,1)S(1)}, bf16[4,64,128]{2,1,0:T(8,128)(2,1)S(1)}, u32[]{:S(2)}, u32[]{:S(2)}) collective-permute-start(bf16[4,64,128]{2,1,0:T(8,128)(2,1)S(1)} %wire.1.refs_2_), channel_id=1, source_target_pairs={{0,24},{4,28},{8,16},{12,20},{16,8},{20,12},{24,0},{28,4},{1,25},{... | collective-permute-start | bytes 196616 | tf_op jit(solution)/shard_map/ppermute | solution.py:576
  28.1 0.2 collective-permute-start.8
  28.3 0.0 collective-permute-start.7
  28.3 2.6 %collective-permute-done.10.refs_4_ = bf16[4,64,128]{2,1,0:T(8,128)(2,1)S(1)} collective-permute-done((bf16[4,64,128]{2,1,0:T(8,128)(2,1)S(1)}, bf16[4,64,128]{2,1,0:T(8,128)(2,1)S(1)}, u32[]{:S(2)}, u32[]{:S(2)}) %collective-permute-start.10) | collective-permute-done | bytes 65568 | tf_op jit(solution)/shard_map/ppermute | solution.py:576
  30.9 0.0 collective-permute-start.11
  30.9 2.4 %collective-permute-done.12.refs_5_ = bf16[4,64,128]{2,1,0:T(8,128)(2,1)S(1)} collective-permute-done((bf16[4,64,128]{2,1,0:T(8,128)(2,1)S(1)}, bf16[4,64,128]{2,1,0:T(8,128)(2,1)S(1)}, u32[]{:S(2)}, u32[]{:S(2)}) %collective-permute-start.12) | collective-permute-done | bytes 65568 | tf_op jit(solution)/shard_map/ppermute | solution.py:576
  33.3 0.0 collective-permute-start.13
  33.3 0.2 collective-permute-done.8.refs_3_
  33.6 0.3 collective-permute-start.9
  33.9 0.0 copy-done
  33.9 0.0 copy-done.1
  33.9 0.9 %order_weights.1 = (f32[4,4,64,128]{3,2,1,0:T(8,128)S(1)}, f32[4,4,64,128]{3,2,1,0:T(8,128)S(1)}, f32[4,4,64,128]{3,2,1,0:T(8,128)S(1)}, f32[4,4,64,128]{3,2,1,0:T(8,128)S(1)}) custom-call(s32[1,8]{1,0:T(1,128)S(1)} %copy-done.1, f32[8,4,64,128]{3,2,1,0:T(8,128)S(1)} %bitcast.73), custom_call_target="tpu_custom_call" | custom-call | tf_op jit(solution)/shard_map/order_weights/pallas_call | solution.py:508
  34.8 0.2 sum_near.1.refs_6_
  35.0 0.0 collective-permute-done.7.refs_2_
  35.0 0.0 collective-permute-done.11.refs_4_
  35.0 0.0 collective-permute-done.13.refs_5_
  35.0 0.0 collective-permute-done.9.refs_3_
  35.0 0.8 %sum_far.1 = f32[4,64,128]{2,1,0:T(8,128)} custom-call(f32[4,4,64,128]{3,2,1,0:T(8,128)S(1)} %get-tuple-element.9.refs_0_, f32[4,4,64,128]{3,2,1,0:T(8,128)S(1)} %get-tuple-element.10.refs_1_, bf16[4,64,128]{2,1,0:T(8,128)(2,1)S(1)} %collective-permute-done.7.refs_2_, bf16[4,64,128]{2,1,0:T(8,128)(2,1)S(1)} %collective-permute-done.9.refs_3_, ...), custom_call_target="tpu_custom_call" | custom-call | tf_op jit(solution)/shard_map/sum_far/pallas_call | solution.py:563
  (8 shorter events, 0.1 us)
Async XLA Ops:
  0.0 1.6 %copy-start.2 = (f32[1,4,64,128]{3,2,1,0:T(8,128)S(1)}, f32[1,4,64,128]{3,2,1,0:T(8,128)}, u32[]{:S(2)}) copy-start(f32[1,4,64,128]{3,2,1,0:T(8,128)} %param.9) | copy-start | bytes 393220
  0.0 33.9 %copy-start = (f32[8,1,4,64,128]{4,3,2,1,0:T(8,128)S(1)}, f32[8,1,4,64,128]{4,3,2,1,0:T(8,128)}, u32[]{:S(2)}) copy-start(f32[8,1,4,64,128]{4,3,2,1,0:T(8,128)} %param.13) | copy-start | bytes 3145732
  2.6 7.3 %collective-permute-start = (f32[208,128]{1,0:T(8,128)S(1)}, f32[208,128]{1,0:T(8,128)S(1)}, u32[]{:S(2)}, u32[]{:S(2)}) collective-permute-start(f32[208,128]{1,0:T(8,128)S(1)} %add_add_fusion.refs_8_), channel_id=1, source_target_pairs={{0,3},{1,2},{2,1},{3,0},{4,7},{5,6},{6,5},{7,4},{8,11},{9,10},{10,... | collective-permute-start | bytes 319496 | tf_op jit(solution)/shard_map/ppermute | solution.py:576
  6.5 5.3 %collective-permute-start.2 = (f32[208,128]{1,0:T(8,128)S(1)}, f32[208,128]{1,0:T(8,128)S(1)}, u32[]{:S(2)}, u32[]{:S(2)}) collective-permute-start(f32[208,128]{1,0:T(8,128)S(1)} %add_add_fusion.refs_8_), channel_id=1, source_target_pairs={{0,2},{1,3},{2,0},{3,1},{4,6},{5,7},{6,4},{7,5},{8,10},{9,11},{10,... | collective-permute-start | bytes 319496 | tf_op jit(solution)/shard_map/ppermute | solution.py:576
  7.0 5.0 %collective-permute-start.4 = (f32[208,128]{1,0:T(8,128)S(1)}, f32[208,128]{1,0:T(8,128)S(1)}, u32[]{:S(2)}, u32[]{:S(2)}) collective-permute-start(f32[208,128]{1,0:T(8,128)S(1)} %add_add_fusion.refs_8_), channel_id=1, source_target_pairs={{0,1},{1,0},{2,3},{3,2},{4,5},{5,4},{6,7},{7,6},{8,9},{9,8},{10,11... | collective-permute-start | bytes 319496 | tf_op jit(solution)/shard_map/ppermute | solution.py:576
  7.2 5.8 %collective-permute-start.6 = (f32[208,128]{1,0:T(8,128)S(1)}, f32[208,128]{1,0:T(8,128)S(1)}, u32[]{:S(2)}, u32[]{:S(2)}) collective-permute-start(f32[208,128]{1,0:T(8,128)S(1)} %add_add_fusion.refs_8_), channel_id=1, source_target_pairs={{0,4},{4,0},{8,12},{12,8},{16,20},{20,16},{24,28},{28,24},{1,5},{5... | collective-permute-start | bytes 319496 | tf_op jit(solution)/shard_map/ppermute | solution.py:576
  9.9 3.1 %collective-permute-start.1 = (f32[208,128]{1,0:T(8,128)S(1)}, f32[208,128]{1,0:T(8,128)S(1)}, u32[]{:S(2)}, u32[]{:S(2)}) collective-permute-start(f32[208,128]{1,0:T(8,128)S(1)} %collective-permute-done.refs_5_), channel_id=1, source_target_pairs={{0,4},{4,0},{8,12},{12,8},{16,20},{20,16},{24,28},{28,24},{1,5},{5... | collective-permute-start | bytes 319496 | tf_op jit(solution)/shard_map/ppermute | solution.py:576
  11.8 1.3 %collective-permute-start.3 = (f32[208,128]{1,0:T(8,128)S(1)}, f32[208,128]{1,0:T(8,128)S(1)}, u32[]{:S(2)}, u32[]{:S(2)}) collective-permute-start(f32[208,128]{1,0:T(8,128)S(1)} %collective-permute-done.2.refs_6_), channel_id=1, source_target_pairs={{0,4},{4,0},{8,12},{12,8},{16,20},{20,16},{24,28},{28,24},{1,5},{5... | collective-permute-start | bytes 319496 | tf_op jit(solution)/shard_map/ppermute | solution.py:576
  12.0 1.3 %collective-permute-start.5 = (f32[208,128]{1,0:T(8,128)S(1)}, f32[208,128]{1,0:T(8,128)S(1)}, u32[]{:S(2)}, u32[]{:S(2)}) collective-permute-start(f32[208,128]{1,0:T(8,128)S(1)} %collective-permute-done.4.refs_7_), channel_id=1, source_target_pairs={{0,4},{4,0},{8,12},{12,8},{16,20},{20,16},{24,28},{28,24},{1,5},{5... | collective-permute-start | bytes 319496 | tf_op jit(solution)/shard_map/ppermute | solution.py:576
  24.0 9.9 %copy-start.1 = (s32[1,8]{1,0:T(1,128)S(1)}, s32[1,8]{1,0:T(1,128)}, u32[]{:S(2)}) copy-start(s32[1,8]{1,0:T(1,128)} %refs_0_.2) | copy-start | bytes 100
  24.0 7.0 %collective-permute-start.10 = (bf16[4,64,128]{2,1,0:T(8,128)(2,1)S(1)}, bf16[4,64,128]{2,1,0:T(8,128)(2,1)S(1)}, u32[]{:S(2)}, u32[]{:S(2)}) collective-permute-start(bf16[4,64,128]{2,1,0:T(8,128)(2,1)S(1)} %wire.1.refs_2_), channel_id=1, source_target_pairs={{0,16},{4,20},{8,24},{12,28},{16,0},{20,4},{24,8},{28,12},{1,17},{... | collective-permute-start | bytes 196616 | tf_op jit(solution)/shard_map/ppermute | solution.py:576
  26.8 6.6 %collective-permute-start.12 = (bf16[4,64,128]{2,1,0:T(8,128)(2,1)S(1)}, bf16[4,64,128]{2,1,0:T(8,128)(2,1)S(1)}, u32[]{:S(2)}, u32[]{:S(2)}) collective-permute-start(bf16[4,64,128]{2,1,0:T(8,128)(2,1)S(1)} %wire.1.refs_2_), channel_id=1, source_target_pairs={{0,24},{4,28},{8,16},{12,20},{16,8},{20,12},{24,0},{28,4},{1,25},{... | collective-permute-start | bytes 196616 | tf_op jit(solution)/shard_map/ppermute | solution.py:576
  28.1 5.5 %collective-permute-start.8 = (bf16[4,64,128]{2,1,0:T(8,128)(2,1)S(1)}, bf16[4,64,128]{2,1,0:T(8,128)(2,1)S(1)}, u32[]{:S(2)}, u32[]{:S(2)}) collective-permute-start(bf16[4,64,128]{2,1,0:T(8,128)(2,1)S(1)} %wire.1.refs_2_), channel_id=1, source_target_pairs={{0,8},{4,12},{8,0},{12,4},{16,24},{20,28},{24,16},{28,20},{1,9},{5... | collective-permute-start | bytes 196616 | tf_op jit(solution)/shard_map/ppermute | solution.py:576
  28.3 6.6 %collective-permute-start.7 = (bf16[4,64,128]{2,1,0:T(8,128)(2,1)S(1)}, bf16[4,64,128]{2,1,0:T(8,128)(2,1)S(1)}, u32[]{:S(2)}, u32[]{:S(2)}) collective-permute-start(bf16[4,64,128]{2,1,0:T(8,128)(2,1)S(1)} %wire.1.refs_2_), channel_id=1, source_target_pairs={{0,4},{4,0},{8,12},{12,8},{16,20},{20,16},{24,28},{28,24},{1,5},{5... | collective-permute-start | bytes 196616 | tf_op jit(solution)/shard_map/ppermute | solution.py:576
  30.9 4.0 %collective-permute-start.11 = (bf16[4,64,128]{2,1,0:T(8,128)(2,1)S(1)}, bf16[4,64,128]{2,1,0:T(8,128)(2,1)S(1)}, u32[]{:S(2)}, u32[]{:S(2)}) collective-permute-start(bf16[4,64,128]{2,1,0:T(8,128)(2,1)S(1)} %collective-permute-done.10.refs_4_), channel_id=1, source_target_pairs={{0,4},{4,0},{8,12},{12,8},{16,20},{20,16},{24,28},{28,24},{1,5},{5... | collective-permute-start | bytes 196616 | tf_op jit(solution)/shard_map/ppermute | solution.py:576
  33.3 1.6 %collective-permute-start.13 = (bf16[4,64,128]{2,1,0:T(8,128)(2,1)S(1)}, bf16[4,64,128]{2,1,0:T(8,128)(2,1)S(1)}, u32[]{:S(2)}, u32[]{:S(2)}) collective-permute-start(bf16[4,64,128]{2,1,0:T(8,128)(2,1)S(1)} %collective-permute-done.12.refs_5_), channel_id=1, source_target_pairs={{0,4},{4,0},{8,12},{12,8},{16,20},{20,16},{24,28},{28,24},{1,5},{5... | collective-permute-start | bytes 196616 | tf_op jit(solution)/shard_map/ppermute | solution.py:576
  33.6 1.4 %collective-permute-start.9 = (bf16[4,64,128]{2,1,0:T(8,128)(2,1)S(1)}, bf16[4,64,128]{2,1,0:T(8,128)(2,1)S(1)}, u32[]{:S(2)}, u32[]{:S(2)}) collective-permute-start(bf16[4,64,128]{2,1,0:T(8,128)(2,1)S(1)} %collective-permute-done.8.refs_3_), channel_id=1, source_target_pairs={{0,4},{4,0},{8,12},{12,8},{16,20},{20,16},{24,28},{28,24},{1,5},{5... | collective-permute-start | bytes 196616 | tf_op jit(solution)/shard_map/ppermute | solution.py:576
